TPU v7x, 32 devices: a whole 2x2x4 slice. The times are simulated.
32 devices in a mesh: batch: 4 (over y, x), blk: 8 (over z, core).
Axes of the slice: x: 2, y: 2, z: 4, core: 2. Of those that a mesh axis runs over, the one named last changes fastest.
Arguments:
- tokens: bfloat16 [4, 4096, 768], P('batch', 'blk'), may hold values from -6 to 6
- lengths: int32 [4, 3], P('batch'), may hold values from 128 to 3839, as said below
- norm_one: bfloat16 [768], P(('batch', 'blk')), may hold values from 0.5 to 1.5
- w_qkv: bfloat16 [768, 2304], P(('batch', 'blk')), may hold values from -0.109375 to 0.109375
- rel_table: float32 [32, 12], replicated, may hold values from -4 to 4
- w_out: bfloat16 [768, 768], P(('batch', 'blk')), may hold values from -6 to 6
- norm_two: bfloat16 [768], P(('batch', 'blk')), may hold values from 0.5 to 1.5
- w_gateup: bfloat16 [768, 4096], P(('batch', 'blk')), may hold values from -0.21875 to 0.21875
- w_down: bfloat16 [2048, 768], P(('batch', 'blk')), may hold values from -0.125 to 0.125
- cotangent: bfloat16 [4, 4096, 768], P('batch', 'blk'), may hold values from -6 to 6
- row_qkv: float32 [768], P(('batch', 'blk')), may hold values from 0.25 to 4
- col_qkv: float32 [2304], replicated, may hold values from 0.25 to 4
- row_out: float32 [768], P(('batch', 'blk')), may hold values from 0.25 to 4
- col_out: float32 [768], replicated, may hold values from 0.25 to 4
- row_gateup: float32 [768], P(('batch', 'blk')), may hold values from 0.25 to 4
- col_gateup: float32 [4096], replicated, may hold values from 0.25 to 4
- row_down: float32 [2048], P(('batch', 'blk')), may hold values from 0.25 to 4
- col_down: float32 [768], replicated, may hold values from 0.25 to 4
Outputs:
- output: bfloat16 [4, 4096, 768], P('batch', 'blk')
- d_tokens: bfloat16 [4, 4096, 768], P('batch', 'blk')
- d_norm_one: float32 [768], P(('batch', 'blk'))
- d_qkv: float32 [768, 2304], P(('batch', 'blk'))
- d_table: float32 [32, 12], replicated
- d_out: float32 [768, 768], P(('batch', 'blk'))
- d_norm_two: float32 [768], P(('batch', 'blk'))
- d_gateup: float32 [768, 4096], P(('batch', 'blk'))
- d_down: float32 [2048, 768], P(('batch', 'blk'))
- new_row_qkv: float32 [768], P(('batch', 'blk'))
- new_col_qkv: float32 [2304], replicated
- new_row_out: float32 [768], P(('batch', 'blk'))
- new_col_out: float32 [768], replicated
- new_row_gateup: float32 [768], P(('batch', 'blk'))
- new_col_gateup: float32 [4096], replicated
- new_row_down: float32 [2048], P(('batch', 'blk'))
- new_col_down: float32 [768], replicated
Inputs may be any that keep to these rules, and one draw needn't show every extreme that they name: `lengths`: each row holds 3 documents one after the other from position 0, then 1 to 128 padding positions at the end. The first document is shorter than 512; the third is 128 to 256 long, so the second document begins on the first device of blk and ends on the last.
All inputs are finite; a program needn't handle non-finite values.
Results may differ from a plain program's by a relative error of at most 0.022.
Values may be sent and summed in bfloat16 or wider, within the bound.
No kernel may reach another device: no remote copies, remote signals or barrier semaphores. Data moves between devices by JAX's collectives and lax.ppermute only.
A program may use at most 192 MiB of HBM per device.

v0:
```python
import functools
import math

import jax
import jax.numpy as jnp
from jax import lax
from jax.experimental import pallas as pl
from jax.experimental.pallas import tpu as pltpu
from jax.sharding import Mesh
from jax.sharding import PartitionSpec as P

THRESHOLDS = (12, 16, 23, 32, 46, 64, 91)
EPSILON = 1e-06
DECAY_RATE = 0.5
GELU_SCALE = 0.7978845608028654
MASKED = -1e9
LEEWAY = 20.0
ALL = ("batch", "group", "split")
LANES = 128
TILE = 256
GROUP = 4
VMEM = 56 * 2**20
F32 = jnp.float32
BF16 = jnp.bfloat16


def bucket_of(offset):
    distance = jnp.abs(offset)
    steps_up = 8 + sum(((distance >= limit).astype(jnp.int32) for limit in THRESHOLDS))
    within = jnp.where(distance < 8, distance, steps_up)
    return within + 16 * (offset > 0).astype(jnp.int32)


def after(value, *others):
    return lax.optimization_barrier((value, *others))[0]


def rms_scale(values, gain):
    return values * lax.rsqrt(jnp.mean(values * values, axis=-1, keepdims=True) + EPSILON) * gain


def rms_back(values, gain, grad):
    scale = lax.rsqrt(jnp.mean(values * values, axis=-1, keepdims=True) + EPSILON)
    scaled = grad * gain
    return scale * scaled - values * scale**3 * jnp.mean(scaled * values, axis=-1, keepdims=True)


def dot_nn(left, right):
    return jnp.dot(left, right, preferred_element_type=F32)


def dot_nt(left, right):
    return lax.dot_general(left, right, (((1,), (1,)), ((), ())), preferred_element_type=F32)


def dot_tt(left, right):
    return lax.dot_general(left, right, (((0,), (1,)), ((), ())), preferred_element_type=F32)


class Layout:
    def __init__(self, tokens, groups, splits, ints):
        self.tokens, self.groups, self.splits = tokens, groups, splits
        self.blocks = groups * splits
        self.seq = tokens * self.blocks
        self.near = tokens + 2 * LANES
        self.subs = tokens // LANES
        self.split = ints[0]
        self.ends = (ints[1], ints[2], ints[3])
        slot = pl.program_id(0)
        self.block = self.block_of(slot, 0)
        self.first = pl.multiple_of(self.block * tokens, LANES)
        self.lefts = jnp.maximum(0, self.block * (tokens // TILE) - 1)
        self.loops = (self.seq // TILE - 2 - tokens // TILE) // GROUP
        self.edge = jnp.logical_or(self.block == 0, self.block == self.blocks - 1)

    def block_of(self, slot, other):
        return slot * self.splits + lax.rem(self.split + other, self.splits)

    def keys_of(self, tile):
        before = 2 * LANES + TILE * tile
        after = self.first + self.near + TILE * (tile - self.lefts)
        return pl.ds(pl.multiple_of(jnp.where(tile < self.lefts, before, after), LANES), TILE)

    def rows_of(self, tile):
        return pl.ds(pl.multiple_of(self.near + TILE * tile, LANES), TILE)

    def segment(self, positions):
        return sum((positions >= end).astype(jnp.int32) for end in self.ends)


def iota(shape, dim):
    return lax.broadcasted_iota(jnp.int32, shape, dim)


def fold(values):
    return values.reshape(values.shape[0] // 8, 8, values.shape[1])


def forward_kernel(tokens, groups, splits, ints, table, query, *refs):
    kvs, (probs, context, stats, k_aug, v_t, scores, biases, best) = refs[:splits], refs[splits:]
    lay = Layout(tokens, groups, splits, ints)
    half = query.shape[1] // 2
    buckets = table.shape[1]

    @pl.when(pl.program_id(0) == 0)
    def prepare():
        lane = iota((tokens, LANES), 1)
        for slot in range(groups):
            for other in range(splits):
                start = lay.block_of(slot, other) * tokens
                rows = pl.ds(pl.multiple_of(LANES + start, LANES), tokens)
                kv = kvs[other][slot * tokens : (slot + 1) * tokens, :].astype(F32)
                seg = lay.segment(start + iota((tokens, LANES), 0))
                k_aug[rows, :] = jnp.where(lane < half, kv, (lane - half == seg).astype(F32)).astype(BF16)
                turned = jnp.transpose(kv)
                ones = (iota((16, tokens), 0) == 0).astype(F32)
                v_t[:, rows] = jnp.concatenate([turned[half:], ones], axis=0).astype(BF16)
        outside = (iota((LANES, LANES), 1) == half + 3).astype(BF16)
        for start in (0, lay.seq + LANES):
            k_aug[start : start + LANES, :] = outside
            v_t[:, start : start + LANES] = jnp.zeros((half + 16, LANES), BF16)
        for place in range(3):
            bucket = bucket_of(
                LANES * (place - 1) + iota((LANES, LANES), 0) - iota((LANES, LANES), 1)
            )
            bias = jnp.zeros((LANES, LANES), F32)
            for label in range(buckets):
                bias = jnp.where(bucket == label, table[0, label], bias)
            biases[place] = bias

    far_left, far_right = table[0, buckets // 2 - 1], table[0, buckets - 1]
    positions = lay.block * tokens + iota((1, tokens), 1)
    seg_q = lay.segment(positions)
    row = iota((2 * half, tokens), 0)
    apart = jnp.logical_or(row - half != seg_q, row == half + 3)
    q_aug = jnp.where(
        row < half, jnp.transpose(query[...].astype(F32)), jnp.where(apart, MASKED, 0.0)
    ).astype(BF16)

    near = dot_nn(k_aug[pl.ds(lay.first, lay.near), :], q_aug)
    eye = iota((LANES, LANES), 0) == iota((LANES, LANES), 1)
    for sub_q in range(lay.subs):
        lanes = slice(LANES * sub_q, LANES * (sub_q + 1))
        top = None
        for sub_k in range(lay.subs + 2):
            rows = slice(LANES * sub_k, LANES * (sub_k + 1))
            place = sub_k - sub_q
            piece = near[rows, lanes] + (
                far_left if place < 0 else far_right if place > 2 else biases[place]
            )
            if place == 1:
                alone = jnp.logical_and(eye, positions[:, lanes] >= lay.ends[2])
                piece = jnp.where(alone, 0.0, piece)
            scores[rows, lanes] = piece
            high = jnp.max(fold(piece), axis=0)
            top = high if top is None else jnp.maximum(top, high)
        best[:, lanes] = top

    def sweep(peak):
        weights = jnp.exp(scores[...] - peak).astype(BF16)
        probs[: lay.near, :] = weights
        stats[...] = dot_nn(v_t[:, pl.ds(lay.first, lay.near)], weights)
        left_peak, right_peak = peak - far_left, peak - far_right

        def tiles(index, count):
            places = [lay.keys_of(index + step) for step in range(count)]
            piece = dot_nn(jnp.concatenate([k_aug[keys, :] for keys in places], axis=0), q_aug)
            parts, top = [], best[...]
            for step in range(count):
                score = piece[TILE * step : TILE * (step + 1)]
                is_left = index + step < lay.lefts
                top = jnp.maximum(
                    top,
                    jnp.max(fold(score), axis=0) + jnp.where(is_left, far_left, far_right),
                )
                part = jnp.exp(score - jnp.where(is_left, left_peak, right_peak)).astype(BF16)
                probs[lay.rows_of(index + step), :] = part
                parts.append(part)
            best[...] = top
            values = jnp.concatenate([v_t[:, keys] for keys in places], axis=1)
            stats[...] += dot_nn(values, jnp.concatenate(parts, axis=0))

        if lay.loops <= 3:
            for index in range(lay.loops):
                tiles(index * GROUP, GROUP)
        else:

            def group(index, carry):
                tiles(index * GROUP, GROUP)
                return carry

            lax.fori_loop(0, lay.loops, group, 0)

        @pl.when(lay.edge)
        def _():
            tiles(lay.loops * GROUP, 1)

    peak = jnp.max(best[...], axis=0, keepdims=True)
    sweep(peak)
    true_peak = jnp.max(best[...], axis=0, keepdims=True)

    @pl.when(jnp.max(true_peak - peak) > LEEWAY)
    def _():
        sweep(true_peak)

    inverse = 1.0 / stats[half : half + 1, :]
    result = stats[:half, :] * inverse
    context[...] = result.astype(BF16)
    stats[:half, :] = result
    stats[half : half + 1, :] = inverse


def backward_kernel(tokens, groups, splits, ints, query, d_context, stats, probs, *refs):
    kvs, d_kvs = refs[:splits], refs[splits : 2 * splits]
    d_table, v_aug, k_t, d_kv, bands, sides, d_q = refs[2 * splits :]
    lay = Layout(tokens, groups, splits, ints)
    half = query.shape[1] // 2
    buckets = d_table.shape[0]

    @pl.when(pl.program_id(0) == 0)
    def prepare():
        lane = iota((tokens, LANES), 1)
        for slot in range(groups):
            for other in range(splits):
                start = lay.block_of(slot, other) * tokens
                rows = pl.ds(pl.multiple_of(LANES + start, LANES), tokens)
                kv = kvs[other][slot * tokens : (slot + 1) * tokens, :].astype(F32)
                v_aug[rows, :] = jnp.where(lane >= half, kv, (lane < 3).astype(F32)).astype(BF16)
                ones = (iota((16, tokens), 0) == 0).astype(F32)
                k_t[:, rows] = jnp.concatenate([jnp.transpose(kv)[:half], ones], axis=0).astype(BF16)
        for start in (0, lay.seq + LANES):
            v_aug[start : start + LANES, :] = jnp.zeros((LANES, LANES), BF16)
            k_t[:, start : start + LANES] = jnp.zeros((half + 16, LANES), BF16)
        d_kv[...] = jnp.zeros_like(d_kv)
        bands[...] = jnp.zeros_like(bands)
        sides[...] = jnp.zeros_like(sides)

    inverse = stats[half : half + 1, :]
    upstream = d_context[...].astype(F32)
    delta = jnp.sum(upstream * stats[:half, :], axis=0, keepdims=True) * inverse
    scaled = upstream * inverse
    high = delta.astype(BF16).astype(F32)
    middle = (delta - high).astype(BF16).astype(F32)
    low = delta - high - middle
    row = iota((half, tokens), 0)
    shift = jnp.where(row == 0, high, jnp.where(row == 1, middle, jnp.where(row == 2, low, 0.0)))
    up_aug = jnp.concatenate([-shift, scaled], axis=0).astype(BF16)
    up_rows = jnp.transpose(jnp.concatenate([jnp.zeros_like(scaled), scaled], axis=0)).astype(BF16)
    both = jnp.concatenate([query[...], up_rows], axis=0)

    def grads(keys, rows):
        part = jnp.concatenate([probs[where, :] for where in rows], axis=0)
        values = jnp.concatenate([v_aug[where, :] for where in keys], axis=0)
        d_scores = part.astype(F32) * dot_nn(values, up_aug)
        rounded = d_scores.astype(BF16)
        added = dot_nn(jnp.concatenate([rounded, part], axis=1), both)
        size = part.shape[0] // len(keys)
        for index, where in enumerate(keys):
            d_kv[where, :] += added[size * index : size * (index + 1)]
        return d_scores, rounded

    near, rounded = grads([pl.ds(lay.first, lay.near)], [pl.ds(0, lay.near)])
    total = dot_nn(k_t[:, pl.ds(lay.first, lay.near)], rounded)
    for sub_q in range(lay.subs):
        lanes = slice(LANES * sub_q, LANES * (sub_q + 1))
        for sub_k in range(lay.subs + 2):
            piece = near[LANES * sub_k : LANES * (sub_k + 1), lanes]
            place = sub_k - sub_q
            if 0 <= place <= 2:
                bands[place] += piece
            else:
                sides[int(place > 2), :, lanes] += jnp.sum(fold(piece), axis=0)
    d_q[...] = total
    near_sum = total[half : half + 8, :]

    def far(index, count):
        places = [lay.keys_of(index + step) for step in range(count)]
        rounded = grads(places, [lay.rows_of(index + step) for step in range(count)])[1]
        keys = jnp.concatenate([k_t[:, where] for where in places], axis=1)
        lefts = jnp.clip(lay.lefts - index, 0, count) * TILE
        row = iota(keys.shape, 0)
        side = jnp.logical_and(row == half + 8, iota(keys.shape, 1) < lefts)
        keys = jnp.where(side, 1.0, keys.astype(F32)).astype(BF16)
        d_q[...] += dot_nn(keys, rounded)

    if lay.loops <= 3:
        for index in range(lay.loops):
            far(index * GROUP, GROUP)
    else:

        def group(index, carry):
            far(index * GROUP, GROUP)
            return carry

        lax.fori_loop(0, lay.loops, group, 0)

    @pl.when(lay.edge)
    def _():
        far(lay.loops * GROUP, 1)

    left_sum = d_q[half + 8 : half + 16, :]
    sides[0] += left_sum
    sides[1] += d_q[half : half + 8, :] - near_sum - left_sum
    d_kvs[0][pl.program_id(0), :half, :] = d_q[:half, :].astype(BF16)

    @pl.when(pl.program_id(0) == groups - 1)
    def finish():
        for slot in range(groups):
            for other in range(splits):
                start = lay.block_of(slot, other) * tokens
                rows = pl.ds(pl.multiple_of(LANES + start, LANES), tokens)
                turned = jnp.transpose(d_kv[rows, :]).astype(BF16)
                if other:
                    d_kvs[other][slot] = turned
                else:
                    d_kvs[0][slot, half:, :] = turned
        labels = [
            bucket_of(LANES * (place - 1) + iota((LANES, LANES), 0) - iota((LANES, LANES), 1))
            for place in range(3)
        ]
        for label in range(buckets):
            found = jnp.zeros((8, LANES), F32)
            for place in range(3):
                kept = jnp.where(labels[place] == label, bands[place], 0.0)
                found += jnp.sum(fold(kept), axis=0)
            if label in (buckets // 2 - 1, buckets - 1):
                side = sides[int(label == buckets - 1)]
                for sub in range(lay.subs):
                    found += side[:, LANES * sub : LANES * (sub + 1)]
            d_table[label : label + 1, :] = jnp.sum(found, axis=0, keepdims=True)


def chosen(shape, source):
    return (source(iota((shape[0], 1), 0)) == iota(shape, 1)).astype(F32).astype(BF16)


def project_block(values, weights, gains, order, normed_t, query, kv):
    normed = rms_scale(values.astype(F32), gains[0:1, :]).astype(BF16)
    normed_t[...] = dot_nt(order[...], normed).astype(BF16)
    both = dot_nn(normed, weights[...])
    narrow = kv.shape[1]
    kv[...] = both[:, :narrow].astype(BF16)
    size = LANES // 2
    blank = jnp.zeros((both.shape[0], size), F32)
    parts = []
    for start in range(narrow, narrow + narrow // 2, size):
        parts += [both[:, start : start + size], blank]
    query[...] = jnp.concatenate(parts, axis=1).astype(BF16)


def project_kernel(dims, ints, weights, own, *refs):
    rows_apart, groups, splits = dims
    others, (normed_t, query, kv, gains, order, values) = refs[:-6], refs[-6:]
    slot, split, group, batch = pl.program_id(0), ints[0], ints[4], ints[5]
    width, narrow = own.shape[1], kv.shape[1]
    unit = width // (rows_apart * groups * splits)

    @pl.when(slot == 0)
    def _():
        def source(index):
            within = lax.rem(index, unit)
            index = index // unit
            g = lax.rem(group + lax.rem(index, groups), groups)
            index = index // groups
            b = lax.rem(batch + lax.rem(index, rows_apart), rows_apart)
            r = lax.rem(split + index // rows_apart, splits)
            return ((b * groups + g) * splits + r) * unit + within

        order[...] = chosen((width, width), source)
        turned = jnp.transpose(weights[:, weights.shape[1] - LANES :].astype(F32))
        gains[...] = turned[LANES // 2 : LANES // 2 + 8]

    @pl.when(slot == group)
    def _():
        values[...] = own[...]

    for by in range(1, groups - 1):

        @pl.when(slot == group - by)
        def _():
            values[...] = others[by - 1][...]

        @pl.when(slot == group + by)
        def _():
            values[...] = others[groups + by - 3][...]

    @pl.when(jnp.abs(slot - group) < groups - 1)
    def _():
        project_block(values[...], weights, gains, order, normed_t, query, kv)


def project(dims, ints, weights, own, others):
    tokens, width = own.shape
    groups = dims[1]
    narrow = 2 * width // groups
    whole = pl.BlockSpec((tokens, width), lambda slot, ints: (0, 0))
    by_row = pl.BlockSpec((tokens, narrow), lambda slot, ints: (slot, 0))
    return pl.pallas_call(
        functools.partial(project_kernel, dims),
        grid_spec=pltpu.PrefetchScalarGridSpec(
            num_scalar_prefetch=1,
            grid=(groups,),
            in_specs=[pl.BlockSpec((width, weights.shape[1] // groups), lambda slot, ints: (0, ints[4]))]
            + [whole] * (1 + len(others)),
            out_specs=[
                pl.BlockSpec((width, tokens), lambda slot, ints: (0, slot)),
                by_row,
                by_row,
                pl.BlockSpec((8, width), lambda slot, ints: (0, 0)),
                pl.BlockSpec((width, width), lambda slot, ints: (0, 0)),
            ],
            scratch_shapes=[pltpu.VMEM((tokens, width), BF16)],
        ),
        out_shape=[
            jax.ShapeDtypeStruct((width, groups * tokens), BF16),
            jax.ShapeDtypeStruct((groups * tokens, narrow), BF16),
            jax.ShapeDtypeStruct((groups * tokens, narrow), BF16),
            jax.ShapeDtypeStruct((8, width), F32),
            jax.ShapeDtypeStruct((width, width), BF16),
        ],
        compiler_params=pltpu.CompilerParams(vmem_limit_bytes=VMEM),
        cost_estimate=pl.CostEstimate(
            flops=4 * groups * tokens * width * width,
            bytes_accessed=8 * groups * tokens * width,
            transcendentals=0,
        ),
        name="project",
    )(ints, weights, own, *others)


def project_last_kernel(groups, ints, weights, own, before, behind, order, gains, *refs):
    normed_t, query, kv, values = refs[3:]
    group = ints[4]
    values[...] = own[...]

    @pl.when(group == 0)
    def _():
        values[...] = behind[...]

    @pl.when(group == groups - 1)
    def _():
        values[...] = before[...]

    project_block(values[...], weights, gains, order, normed_t, query, kv)


def project_last(dims, ints, weights, own, before, behind, order, gains, normed_t, query, kv):
    tokens, width = own.shape
    narrow = kv.shape[1]
    whole = lambda array: pl.BlockSpec(array.shape, lambda step, ints: (0, 0))
    by_row = pl.BlockSpec((tokens, narrow), lambda step, ints: (ints[6], 0))
    return pl.pallas_call(
        functools.partial(project_last_kernel, dims[1]),
        grid_spec=pltpu.PrefetchScalarGridSpec(
            num_scalar_prefetch=1,
            grid=(1,),
            in_specs=[
                pl.BlockSpec((width, weights.shape[1] // dims[1]), lambda step, ints: (0, ints[4]))
            ]
            + [whole(array) for array in (own, before, behind, order, gains)]
            + [pl.BlockSpec(memory_space=pl.ANY)] * 3,
            out_specs=[
                pl.BlockSpec((width, tokens), lambda step, ints: (0, ints[6])),
                by_row,
                by_row,
            ],
            scratch_shapes=[pltpu.VMEM((tokens, width), BF16)],
        ),
        out_shape=[jax.ShapeDtypeStruct(x.shape, x.dtype) for x in (normed_t, query, kv)],
        input_output_aliases={7: 0, 8: 1, 9: 2},
        compiler_params=pltpu.CompilerParams(vmem_limit_bytes=VMEM),
        cost_estimate=pl.CostEstimate(
            flops=4 * tokens * width * width, bytes_accessed=8 * tokens * width, transcendentals=0
        ),
        name="project_last",
    )(ints, weights, own, before, behind, order, gains, normed_t, query, kv)


def split_order(split, splits, unit):
    def source_of(count):
        part = count // splits

        def source(index):
            r = lax.rem(split + index // part, splits)
            index = lax.rem(index, part)
            return (index // unit * splits + r) * unit + lax.rem(index, unit)

        return source

    return source_of


def packed_rows(values, tall, low):
    piece = math.gcd(tall, low)
    across, down = low // piece, tall // piece
    wide = values.shape[1] // across
    rows = []
    for start in range(0, values.shape[0], tall):
        for part in range(across):
            columns = slice(wide * part, wide * (part + 1))
            rows.append(
                jnp.concatenate(
                    [
                        values[start + piece * i : start + piece * (i + 1), columns]
                        for i in range(down)
                    ],
                    axis=1,
                )
            )
    return jnp.concatenate(rows, axis=0)


def unpacked_rows(values, tall, low, columns):
    piece = math.gcd(tall, low)
    across, down = low // piece, tall // piece
    wide = columns // across
    rows = []
    for start in range(0, values.shape[0], low):
        for index in range(down):
            lanes = slice(wide * index, wide * (index + 1))
            rows.append(
                jnp.concatenate(
                    [
                        values[start + piece * part : start + piece * (part + 1), lanes]
                        for part in range(across)
                    ],
                    axis=1,
                )
            )
    return jnp.concatenate(rows, axis=0)


def block_kernel(
    dims, heads, ints, tokens, w_out, gains, w_gate, w_up, w_packed, upstream, *refs
):
    rows_apart, groups, splits = dims
    contexts, refs = refs[:heads], refs[heads:]
    result, d_mixed, d_first, d_rest = refs[:4]
    grads_wide, grads_down = refs[4 : 4 + splits], refs[4 + splits : 4 + 2 * splits]
    (context_t, mixed, normed, normed_t, d_normed, total, order, order_hidden) = refs[4 + 2 * splits :]
    step, chunks = pl.program_id(0), pl.num_programs(0) - 1
    width, chunk = w_gate.shape
    devices = rows_apart * groups * splits
    hidden_unit = chunk * chunks // devices
    gain = gains[1:2, :]

    @pl.when(step == 0)
    def first():
        order[...] = chosen(
            (width, width), split_order(ints[0], splits, width // devices)(width)
        )
        order_hidden[...] = chosen((chunk, chunk), split_order(ints[0], splits, hidden_unit)(chunk))
        each = width // groups // heads
        for g in range(groups):
            for head in range(heads):
                start = (g * heads + head) * each
                context_t[start : start + each, :] = contexts[head][g]
        context = jnp.transpose(context_t[...].astype(F32)).astype(BF16)
        values = tokens[...].astype(F32) + dot_nn(context, w_out[...])
        mixed[...] = values
        total[...] = values
        normed[...] = rms_scale(values, gain).astype(BF16)
        normed_t[...] = dot_nt(order[...], normed[...]).astype(BF16)
        d_normed[...] = jnp.zeros_like(d_normed)

    def stored(outs, rows, values):
        part = values.shape[0] // splits
        for other in range(splits):
            outs[other][:, rows] = values[part * other : part * (other + 1)].astype(BF16)

    @pl.when(step < chunks)
    def work():
        w_down = unpacked_rows(
            w_packed[...].astype(F32), hidden_unit, width // devices, width
        ).astype(BF16)
        gate = dot_nn(normed[...], w_gate[...])
        upward = dot_nn(normed[...], w_up[...])
        d_hidden = dot_nt(upstream[...], w_down)
        square = gate * gate
        turn = jnp.tanh(GELU_SCALE * (gate + 0.044715 * gate * square))
        half = 0.5 * (1.0 + turn)
        active = gate * half
        slope = half + 0.5 * gate * (1.0 - turn * turn) * (GELU_SCALE * (1.0 + 0.134145 * square))
        hidden = (active * upward).astype(BF16)
        d_gate = (d_hidden * upward * slope).astype(BF16)
        d_up = (d_hidden * active).astype(BF16)
        total[...] += dot_nn(hidden, w_down)
        d_normed[...] += dot_nt(d_gate, w_gate[...]) + dot_nt(d_up, w_up[...])
        hidden_t = dot_nt(order_hidden[...], hidden).astype(BF16)

        down = dot_nn(hidden_t, upstream[...])
        part = chunk // splits
        for other in range(splits):
            grads_down[other][...] = packed_rows(
                down[part * other : part * (other + 1)], hidden_unit, width // devices
            ).astype(BF16)
        stored(grads_wide, slice(0, chunk), dot_nn(normed_t[...], d_gate))
        stored(grads_wide, slice(chunk, 2 * chunk), dot_nn(normed_t[...], d_up))

    @pl.when(step == chunks)
    def finish():
        result[...] = total[...].astype(BF16)
        back = upstream[...].astype(F32) + rms_back(mixed[...], gain, d_normed[...])
        d_mixed[...] = back
        branch = back.astype(BF16)
        d_context = dot_nt(w_out[...], branch).astype(BF16)
        each = d_first.shape[1]
        size = width // groups
        for g in range(groups):
            d_first[g] = d_context[size * g : size * g + each]
            d_rest[g] = d_context[size * g + each : size * (g + 1)]
        ordered = dot_nn(order[...], context_t[...]).astype(BF16)
        stored(grads_wide, slice(0, width), dot_nn(ordered, branch))
        for out in grads_wide:
            out[:, width:] = jnp.zeros((out.shape[0], out.shape[1] - width), BF16)


def feed_forward(dims, ints, tokens, contexts, gains, late, upstream):
    groups, splits = dims[1:]
    rows, width = tokens.shape
    hidden = (late.shape[1] - width) // 3
    chunk = 2 * TILE
    steps = hidden // chunk
    each = contexts[0].shape[1]
    full = lambda *shape: pl.BlockSpec(shape, lambda step: (0,) * len(shape))
    return pl.pallas_call(
        functools.partial(block_kernel, dims, len(contexts)),
        grid=(steps + 1,),
        in_specs=[
            smem(),
            full(rows, width),
            pl.BlockSpec((width, width), lambda step: (0, 3 * hidden // width)),
            full(8, width),
            pl.BlockSpec((width, chunk), lambda step: (0, steps + jnp.minimum(step, steps - 1))),
            pl.BlockSpec(
                (width, chunk), lambda step: (0, 2 * steps + jnp.minimum(step, steps - 1))
            ),
            pl.BlockSpec((width // steps, hidden), lambda step: (jnp.minimum(step, steps - 1), 0)),
            full(rows, width),
        ]
        + [full(*context.shape) for context in contexts],
        out_specs=[
            full(rows, width),
            full(rows, width),
            full(groups, each, rows),
            full(groups, width // groups - each, rows),
        ]
        + [pl.BlockSpec((width // splits, 2 * chunk), lambda step: (0, step))] * splits
        + [
            pl.BlockSpec(
                (width // splits // steps, hidden), lambda step: (jnp.minimum(step, steps - 1), 0)
            )
        ]
        * splits,
        out_shape=[
            jax.ShapeDtypeStruct((rows, width), BF16),
            jax.ShapeDtypeStruct((rows, width), F32),
            jax.ShapeDtypeStruct((groups, each, rows), BF16),
            jax.ShapeDtypeStruct((groups, width // groups - each, rows), BF16),
        ]
        + [jax.ShapeDtypeStruct((width // splits, 2 * hidden + 2 * chunk), BF16)] * splits
        + [jax.ShapeDtypeStruct((width // splits, hidden), BF16)] * splits,
        scratch_shapes=[
            pltpu.VMEM((width, rows), BF16),
            pltpu.VMEM((rows, width), F32),
            pltpu.VMEM((rows, width), BF16),
            pltpu.VMEM((width, rows), BF16),
            pltpu.VMEM((rows, width), F32),
            pltpu.VMEM((rows, width), F32),
            pltpu.VMEM((width, width), BF16),
            pltpu.VMEM((chunk, chunk), BF16),
        ],
        compiler_params=pltpu.CompilerParams(vmem_limit_bytes=VMEM),
        cost_estimate=pl.CostEstimate(
            flops=18 * rows * width * hidden + 6 * rows * width * width,
            bytes_accessed=12 * width * hidden,
            transcendentals=rows * hidden,
        ),
        name="feed_forward",
    )(ints, tokens, late, gains, late, late, late, upstream, *contexts)


def weight_kernel(splits, normed_t, *refs):
    d_heads, outs, total = refs[: -splits - 1], refs[-splits - 1 : -1], refs[-1]
    step = pl.program_id(0)
    added = dot_nt(normed_t[...], jnp.concatenate([d_head[...] for d_head in d_heads], axis=0))

    @pl.when(step == 0)
    def _():
        total[...] = added

    @pl.when(step > 0)
    def _():
        total[...] += added

    @pl.when(step == pl.num_programs(0) - 1)
    def _():
        part = total.shape[0] // splits
        for other in range(splits):
            outs[other][...] = total[part * other : part * (other + 1), :].astype(BF16)


def weight_grads(splits, normed_t, d_heads):
    groups, rows, tokens = d_heads[0].shape
    width = normed_t.shape[0]
    out = (width // splits, rows * len(d_heads))
    return pl.pallas_call(
        functools.partial(weight_kernel, splits),
        grid=(groups,),
        in_specs=[pl.BlockSpec((width, tokens), lambda step: (0, step))]
        + [by_slot(rows, tokens)] * len(d_heads),
        out_specs=[pl.BlockSpec(out, lambda step: (0, 0))] * splits,
        out_shape=[jax.ShapeDtypeStruct(out, BF16)] * splits,
        scratch_shapes=[pltpu.VMEM((width, out[1]), F32)],
        compiler_params=pltpu.CompilerParams(vmem_limit_bytes=VMEM),
        cost_estimate=pl.CostEstimate(
            flops=2 * width * out[1] * groups * tokens,
            bytes_accessed=2 * width * groups * tokens,
            transcendentals=0,
        ),
        name="weight_grads",
    )(normed_t, *d_heads)


def added_kernel(count, *refs):
    held, outs = refs[:count], refs[count:]
    total = held[0][...].astype(F32)
    for piece in held[1:]:
        total += piece[...].astype(F32)
    part = total.shape[0] // len(outs)
    for index, out in enumerate(outs):
        out[...] = total[part * index : part * (index + 1)].astype(out.dtype)


def added(pieces, parts):
    rows, columns = pieces[0].shape
    return pl.pallas_call(
        functools.partial(added_kernel, len(pieces)),
        out_shape=[jax.ShapeDtypeStruct((rows // parts, columns), BF16)] * parts,
        compiler_params=pltpu.CompilerParams(vmem_limit_bytes=VMEM),
        cost_estimate=pl.CostEstimate(flops=0, bytes_accessed=2**20, transcendentals=0),
        name="added",
    )(*pieces)


def joined_kernel(count, *refs):
    wide, down, out = refs[:count], refs[count : 2 * count], refs[-1]
    columns = wide[0].shape[1]
    for pieces, lanes in ((wide, slice(0, columns)), (down, slice(columns, out.shape[1]))):
        total = pieces[0][...].astype(F32)
        for piece in pieces[1:]:
            total += piece[...].astype(F32)
        out[:, lanes] = total.astype(BF16)


def joined(wide, down):
    rows, columns = wide[0].shape[0], wide[0].shape[1] + down[0].shape[1]
    block = lambda size: pl.BlockSpec((rows // 4, size), lambda step: (step, 0))
    return pl.pallas_call(
        functools.partial(joined_kernel, len(wide)),
        grid=(4,),
        in_specs=[block(piece.shape[1]) for piece in (*wide, *down)],
        out_specs=block(columns),
        out_shape=jax.ShapeDtypeStruct((rows, columns), BF16),
        compiler_params=pltpu.CompilerParams(vmem_limit_bytes=VMEM),
        cost_estimate=pl.CostEstimate(flops=0, bytes_accessed=2**20, transcendentals=0),
        name="joined",
    )(*wide, *down)


def unpacked(pieces, heads, size):
    return jnp.concatenate(
        [
            piece[:, (3 * head + part) * size : (3 * head + part + 1) * size]
            for part in range(3)
            for piece in pieces
            for head in range(heads)
        ],
        axis=1,
    )


def count_kernel(groups, heads, size, count, down, ints, *refs):
    held, tables, grads = refs[:count], refs[count : count + heads], refs[count + heads]
    outs, counts = refs[count + heads + 1 : -1], refs[-1]
    total = held[0][...].astype(F32)
    for piece in held[1:]:
        total += piece[...].astype(F32)
    part = total.shape[0] // groups
    blank = jnp.zeros((part, counts.shape[1] - total.shape[1]), F32)
    for index, out in enumerate(outs):
        rows = total[part * index : part * (index + 1)]
        out[...] = jnp.concatenate([rows, blank], axis=1)
    squares = jnp.sum(total * total, axis=0, keepdims=True)
    table = jnp.concatenate(
        [jnp.sum(jnp.transpose(table[...]), axis=0, keepdims=True) for table in tables], axis=1
    )
    mine = [(ints[4] == g).astype(F32) for g in range(groups)]
    values = grads[...].astype(F32)
    values = values * values
    wide = values.shape[1] - down[0]
    piece = math.gcd(*down[1:3])
    across = down[2] // piece
    each = down[0] * piece // down[1]
    packed = []
    for part in range(across):
        rows = jnp.sum(values[piece * part : piece * (part + 1), wide:], axis=0, keepdims=True)
        packed.append(sum(rows[:, start : start + each] for start in range(0, down[0], each)))
    row = jnp.concatenate(
        [table * own for own in mine]
        + [unpacked([squares * own for own in mine], heads, size)]
        + [jnp.sum(values[:, : wide - down[3]], axis=0, keepdims=True)]
        + packed,
        axis=1,
    )
    counts[...] = jnp.zeros_like(counts)
    each = counts.shape[1]
    for start in range(0, row.shape[1], each):
        held_row = row[:, start : start + each]
        counts[start // each : start // each + 1, : held_row.shape[1]] = held_row


def counted(groups, heads, size, ints, pieces, tables, grads, down):
    rows, columns = pieces[0].shape
    buckets = tables[0].shape[0]
    length = groups * (heads * buckets + columns) + grads.shape[1] - down[0] - down[3]
    length += down[0] * down[2] // down[1]
    across = -(-columns // LANES) * LANES
    counts = -(-length // (8 * across)) * 8
    vmem = pl.BlockSpec(memory_space=pltpu.VMEM)
    return pl.pallas_call(
        functools.partial(count_kernel, groups, heads, size, len(pieces), down),
        in_specs=[smem()] + [vmem] * (len(pieces) + len(tables) + 1),
        out_shape=[jax.ShapeDtypeStruct((rows // groups, across), F32)] * groups
        + [jax.ShapeDtypeStruct((counts, across), F32)],
        compiler_params=pltpu.CompilerParams(vmem_limit_bytes=VMEM),
        cost_estimate=pl.CostEstimate(flops=0, bytes_accessed=2**20, transcendentals=0),
        name="counted",
    )(ints, *pieces, *tables, grads)


def input_kernel(heads, weights, own, gains, d_mixed, *refs):
    d_heads, (out, total) = refs[:heads], refs[heads:]
    step = pl.program_id(0)
    size = d_heads[0].shape[0] // 3
    blank = jnp.zeros((size, own.shape[0]), BF16)
    pieces = [d_head[size:, :] for d_head in d_heads]
    pieces += [d_head[:size, :] for d_head in d_heads] + [blank]
    added = dot_nn(weights[...], jnp.concatenate(pieces, axis=0))

    @pl.when(step == 0)
    def _():
        total[...] = added

    @pl.when(step > 0)
    def _():
        total[...] += added

    @pl.when(step == pl.num_programs(0) - 1)
    def _():
        back = rms_back(own[...].astype(F32), gains[0:1, :], jnp.transpose(total[...]))
        out[...] = (d_mixed[...] + back).astype(BF16)


def input_grads(groups, weights, own, gains, d_mixed, d_heads):
    tokens, width = own.shape
    full = lambda *shape: pl.BlockSpec(shape, lambda step: (0,) * len(shape))
    return pl.pallas_call(
        functools.partial(input_kernel, len(d_heads)),
        grid=(groups,),
        in_specs=[
            pl.BlockSpec((width, weights.shape[1] // groups), lambda step: (0, step)),
            full(tokens, width),
            full(8, width),
            full(tokens, width),
        ]
        + [by_slot(*d_heads[0].shape[1:])] * len(d_heads),
        out_specs=full(tokens, width),
        out_shape=jax.ShapeDtypeStruct((tokens, width), BF16),
        scratch_shapes=[pltpu.VMEM((width, tokens), F32)],
        compiler_params=pltpu.CompilerParams(vmem_limit_bytes=VMEM),
        name="input_grads",
    )(weights, own, gains, d_mixed, *d_heads)


def by_slot(rows, tokens):
    return pl.BlockSpec((None, rows, tokens), lambda slot: (slot, 0, 0))


def smem():
    return pl.BlockSpec(memory_space=pltpu.SMEM)


def attend(head, tokens, groups, splits, ints, table, query, kvs):
    seq, rows = tokens * groups * splits, tokens * groups
    half = LANES // 2
    whole = pl.BlockSpec((rows, LANES), lambda slot: (0, head))
    return pl.pallas_call(
        functools.partial(forward_kernel, tokens, groups, splits),
        grid=(groups,),
        in_specs=[smem(), smem(), pl.BlockSpec((tokens, LANES), lambda slot: (slot, head))]
        + [whole] * splits,
        out_specs=[
            pl.BlockSpec((seq, tokens), lambda slot: (slot, 0)),
            by_slot(half, tokens),
            by_slot(half + 16, tokens),
        ],
        out_shape=[
            jax.ShapeDtypeStruct((groups * seq, tokens), BF16),
            jax.ShapeDtypeStruct((groups, half, tokens), BF16),
            jax.ShapeDtypeStruct((groups, half + 16, tokens), F32),
        ],
        scratch_shapes=[
            pltpu.VMEM((seq + 2 * LANES, LANES), BF16),
            pltpu.VMEM((half + 16, seq + 2 * LANES), BF16),
            pltpu.VMEM((tokens + 2 * LANES, tokens), F32),
            pltpu.VMEM((3, LANES, LANES), F32),
            pltpu.VMEM((8, tokens), F32),
        ],
        compiler_params=pltpu.CompilerParams(vmem_limit_bytes=VMEM),
        cost_estimate=pl.CostEstimate(
            flops=16 * seq * rows * half, bytes_accessed=2 * seq * rows, transcendentals=seq * rows
        ),
        name="attend",
    )(ints, table, query, *kvs)


def attend_back(
    head, tokens, groups, splits, ints, buckets, query, d_context, place, stats, probs, kvs
):
    seq, rows = tokens * groups * splits, tokens * groups
    half = LANES // 2
    whole = pl.BlockSpec((rows, LANES), lambda slot: (0, head))
    kept = pl.BlockSpec((groups, LANES, tokens), lambda slot: (0, 0, 0))
    return pl.pallas_call(
        functools.partial(backward_kernel, tokens, groups, splits),
        grid=(groups,),
        in_specs=[
            smem(),
            pl.BlockSpec((tokens, LANES), lambda slot: (slot, head)),
            pl.BlockSpec((None, None, half, tokens), lambda slot: (slot, place, 0, 0)),
            by_slot(half + 16, tokens),
            pl.BlockSpec((seq, tokens), lambda slot: (slot, 0)),
        ]
        + [whole] * splits,
        out_specs=[pl.BlockSpec((groups, half + LANES, tokens), lambda slot: (0, 0, 0))]
        + [kept] * (splits - 1)
        + [pl.BlockSpec((buckets, LANES), lambda slot: (0, 0))],
        out_shape=[jax.ShapeDtypeStruct((groups, half + LANES, tokens), BF16)]
        + [jax.ShapeDtypeStruct((groups, LANES, tokens), BF16)] * (splits - 1)
        + [jax.ShapeDtypeStruct((buckets, LANES), F32)],
        scratch_shapes=[
            pltpu.VMEM((seq + 2 * LANES, LANES), BF16),
            pltpu.VMEM((half + 16, seq + 2 * LANES), BF16),
            pltpu.VMEM((seq + 2 * LANES, LANES), F32),
            pltpu.VMEM((3, LANES, LANES), F32),
            pltpu.VMEM((2, 8, tokens), F32),
            pltpu.VMEM((half + 16, tokens), F32),
        ],
        compiler_params=pltpu.CompilerParams(vmem_limit_bytes=VMEM),
        cost_estimate=pl.CostEstimate(
            flops=32 * seq * rows * half, bytes_accessed=2 * seq * rows, transcendentals=0
        ),
        name="attend_back",
    )(ints, query, d_context, stats, probs, *kvs)


def factored(grad_shard, column_total, row_old, column_old, row_total):
    columns = grad_shard.shape[1]
    mean_square = jnp.sum(column_total) / (row_total * columns) + EPSILON
    row_new = (
        DECAY_RATE * row_old
        + (1.0 - DECAY_RATE) * (jnp.sum(grad_shard * grad_shard, axis=1) / columns) / mean_square
    )
    column_new = (
        DECAY_RATE * column_old + (1.0 - DECAY_RATE) * (column_total / row_total) / mean_square
    )
    return (row_new, column_new)


def shards(
    tokens,
    lengths,
    norm_one,
    w_qkv,
    rel_table,
    w_out,
    norm_two,
    w_gateup,
    w_down,
    cotangent,
    row_qkv,
    col_qkv,
    row_out,
    col_out,
    row_gateup,
    col_gateup,
    row_down,
    col_down,
):
    own = tokens[0]
    tok_rows, width = own.shape
    heads = rel_table.shape[1]
    buckets = rel_table.shape[0]
    rows_apart, groups, splits = (lax.axis_size(name) for name in ALL)
    group_heads = heads // groups
    head_size = width // heads
    group, split = lax.axis_index("group"), lax.axis_index("split")
    group_width = width // groups

    def ahead(array, axis, by):
        size = lax.axis_size(axis)
        return lax.ppermute(array, axis, [((i + by) % size, i) for i in range(size)])

    def swap_groups(array):
        return lax.all_to_all(array, "group", 0, 0)

    def swap_rows(array):
        return lax.all_to_all(array, "batch", 0, 0)

    def line(array, by):
        pairs = [(i, i + by) for i in range(groups) if 0 <= i + by < groups]
        return lax.ppermute(array, "group", pairs)

    before, behind = [own], [own]
    for _ in range(groups - 1):
        before.append(line(before[-1], 1))
        behind.append(line(behind[-1], -1))

    unit = w_qkv.shape[0]
    by_part = w_qkv.reshape(unit, 3, groups, group_heads, head_size)
    gains = jnp.pad(jnp.stack([norm_one, norm_two], axis=1), ((0, 0), (0, head_size - 2)))
    packed = jnp.concatenate(
        [
            jnp.concatenate([by_part[:, 1], by_part[:, 2]], axis=-1).reshape(unit, groups, -1),
            by_part[:, 0].reshape(unit, groups, -1),
            jnp.broadcast_to(gains[:, None], (unit, groups, head_size)),
        ],
        axis=2,
    )
    early = lax.all_gather(packed.reshape(unit, -1), ALL, axis=0, tiled=True)
    together = math.gcd(unit, w_down.shape[0])
    packed_down = w_down.reshape(w_down.shape[0] // together, together, unit // together, -1)
    packed_down = jnp.transpose(packed_down, (2, 1, 0, 3)).reshape(unit, -1)
    late = lax.all_gather(
        after(jnp.concatenate([packed_down, w_gateup, w_out], axis=1), before[1], behind[1]),
        ALL,
        axis=0,
        tiled=True,
    )

    dims = (rows_apart, groups, splits)
    far = jnp.where(group == 0, groups - 1, jnp.where(group == groups - 1, 0, group))
    ends = jnp.cumsum(lengths[0])
    ints = jnp.concatenate(
        [
            split.astype(jnp.int32)[None],
            ends.astype(jnp.int32),
            jnp.stack([group, lax.axis_index("batch"), far]).astype(jnp.int32),
        ]
    )
    *blocks, gains, order = project(dims, ints, early, own, before[1:-1] + behind[1:-1])
    normed_t, query, kv = project_last(
        dims, ints, early, own, before[-1], behind[-1], order, gains, *blocks
    )
    kvs = [kv] + [ahead(kv, "split", other) for other in range(1, splits)]

    table_own = lax.dynamic_slice_in_dim(rel_table.T, group * group_heads, group_heads, 0)

    contexts, moved, stats, probs = [], [], [], []
    for head in range(group_heads):
        prob, context, stat = attend(
            head,
            tok_rows,
            groups,
            splits,
            after(ints, *contexts[-1:]),
            table_own[head : head + 1],
            query,
            kvs,
        )
        contexts.append(context)
        moved.append(swap_groups(after(context, *moved[-1:])))
        stats.append(stat)
        probs.append(prob)

    outs = feed_forward(
        dims, ints, own, moved, gains, late, cotangent[0]
    )
    result, d_mixed, d_first, d_rest = outs[:4]
    grads_wide, grads_down = outs[4 : 4 + splits], outs[4 + splits :]

    def by_split(grads):
        return [grads[0]] + [ahead(grads[by], "split", splits - by) for by in range(1, splits)]

    d_first = swap_groups(d_first)
    d_rest = swap_groups(d_rest)
    d_contexts = [d_first[:, None], d_rest.reshape(groups, group_heads - 1, head_size, tok_rows)]
    wide, down = by_split(grads_wide), by_split(grads_down)
    wide[-1] = after(wide[-1], d_first)
    held = joined(wide, down)
    held = held.reshape(rows_apart, groups, -1, held.shape[-1])
    row_sum = after(lax.psum_scatter(held, "batch", scatter_dimension=0))
    grads_own = lax.psum_scatter(row_sum, "group", scatter_dimension=0)

    d_heads, d_received, d_tables = [], [], []
    ready = [(held,), ()] + [(row_sum,)] * (group_heads - 2)
    for head in range(group_heads):
        outs = attend_back(
            head,
            tok_rows,
            groups,
            splits,
            ints,
            buckets,
            query,
            after(d_contexts[int(head > 0)], *ready[head], *d_heads[-1:]),
            head - int(head > 0),
            stats[head],
            probs[head],
            kvs,
        )
        beside = d_received[-1] if head else d_contexts[1]
        if head < group_heads - 1:
            outs = lax.optimization_barrier((*outs, beside))[:-1]
        d_head = outs[0].astype(F32)
        for other in range(1, splits):
            d_kv = ahead(outs[other], "split", splits - other).astype(F32)
            d_head = d_head + jnp.pad(d_kv, ((0, 0), (head_size, 0), (0, 0)))
        d_head = d_head.astype(BF16)
        if head == group_heads - 1:
            d_head = after(d_head, beside)
        d_heads.append(d_head)
        d_received.append(swap_groups(d_head))
        d_tables.append(outs[-1])

    down_shape = (w_down.shape[0] * width // unit, w_down.shape[0], unit)
    down_start = grads_own.shape[1] - down_shape[0]
    down_shape += (down_start - w_gateup.shape[1] - width,)
    grads = weight_grads(splits, normed_t, d_heads)
    held = added(
        [grads[0]] + [ahead(grads[by], "split", splits - by) for by in range(1, splits)], rows_apart
    )
    held = [held[0]] + [ahead(held[by], "batch", rows_apart - by) for by in range(1, rows_apart)]
    held[0] = after(held[0], d_received[-1])
    *columns, counts = counted(
        groups, group_heads, head_size, ints, held, d_tables, grads_own, down_shape
    )
    d_received[-1] = after(d_received[-1], counts)
    d_inputs = input_grads(groups, early, own, gains, d_mixed, d_received)
    counts = sum([ahead(counts, "batch", by) for by in range(1, rows_apart)], counts)
    counts = after(counts, d_inputs)
    counts_rows = counts.shape[0]
    travelled = [jnp.concatenate([counts, columns[0]], axis=0)] + [
        ahead(jnp.concatenate([counts, columns[by]], axis=0), "group", groups - by)
        for by in range(1, groups)
    ]
    columns = [both[counts_rows:] for both in travelled]
    counts = sum([both[:counts_rows] for both in travelled[1:]], travelled[0][:counts_rows])
    counts = sum([ahead(counts, "split", by) for by in range(1, splits)], counts)
    pieces = []
    for index in range(groups):
        piece = columns[0]
        for by in range(1, groups):
            piece = jnp.where((group + groups - by) % groups == index, columns[by], piece)
        pieces.append(piece)
    shard_qkv = unpacked(pieces, group_heads, head_size)
    steps = w_down.shape[0] * rows_apart * groups * splits // (2 * TILE)

    def in_order(array):
        array = array.reshape(*array.shape[:-1], steps, 2, -1)
        return jnp.swapaxes(array, -3, -2).reshape(*array.shape[:-3], -1)

    shard_rest = grads_own.astype(F32)
    shard_gateup = in_order(shard_rest[:, : w_gateup.shape[1]])
    shard_out = shard_rest[:, w_gateup.shape[1] :][:, :width]
    shard_down = shard_rest[:, down_start:].reshape(
        unit // together, together, w_down.shape[0] // together, -1
    )
    shard_down = jnp.transpose(shard_down, (2, 1, 0, 3)).reshape(-1, width)
    summed = counts.reshape(-1)
    sizes = (heads * buckets, 3 * width, w_gateup.shape[1], width, width)
    table_total, column_qkv, column_gateup, column_out, column_down, _ = jnp.split(
        summed, [sum(sizes[: i + 1]) for i in range(len(sizes))]
    )
    table_total = table_total.reshape(heads, buckets)
    column_gateup = in_order(column_gateup)
    shard_gain_one = jnp.sum(w_qkv.astype(F32) * shard_qkv, axis=1) / norm_one.astype(F32)
    shard_gain_two = jnp.sum(w_gateup.astype(F32) * shard_gateup, axis=1) / norm_two.astype(F32)
    new_row_qkv, new_col_qkv = factored(shard_qkv, column_qkv, row_qkv, col_qkv, width)
    new_row_out, new_col_out = factored(shard_out, column_out, row_out, col_out, width)
    new_row_gateup, new_col_gateup = factored(
        shard_gateup, column_gateup, row_gateup, col_gateup, width
    )
    new_row_down, new_col_down = factored(
        shard_down, column_down, row_down, col_down, w_down.shape[0] * rows_apart * groups * splits
    )
    return (
        result[None],
        d_inputs[None],
        shard_gain_one,
        shard_qkv,
        table_total.T,
        shard_out,
        shard_gain_two,
        shard_gateup,
        shard_down,
        new_row_qkv,
        new_col_qkv,
        new_row_out,
        new_col_out,
        new_row_gateup,
        new_col_gateup,
        new_row_down,
        new_col_down,
    )


def solution(mesh):
    row_blocks = P("batch", ("group", "split"), None)
    split_rows = P(ALL, None)
    split_row = P(ALL)

    def run(*arrays):
        rows, ring = mesh.devices.shape
        groups = math.gcd(ring, arrays[4].shape[1])
        fine = Mesh(mesh.devices.reshape(rows, groups, ring // groups), ALL)
        return jax.shard_map(
            shards,
            mesh=fine,
            in_specs=(
                row_blocks,
                P("batch", None),
                split_row,
                split_rows,
                P(),
                split_rows,
                split_row,
                split_rows,
                split_rows,
                row_blocks,
            )
            + (split_row, P()) * 4,
            out_specs=(
                row_blocks,
                row_blocks,
                split_row,
                split_rows,
                P(),
                split_rows,
                split_row,
                split_rows,
                split_rows,
            )
            + (split_row, P()) * 4,
            check_vma=False,
        )(*arrays)

    return run
```

profile of v0, /device:TPU:0, one launch (start us, length us, event | category | flops | bytes accessed | tf_op | source)
XLA Modules:
  0.0 404.3 jit_solution(4176211778946597204)
XLA Ops:
  7.3 1.2 reshape.120
  9.2 0.7 copy.73
  10.0 5.0 %collective-permute-start = (bf16[512,768]{1,0:T(8,128)(2,1)S(1)}, bf16[512,768]{1,0:T(8,128)(2,1)S(1)}, u32[]{:S(2)}, u32[]{:S(2)}) collective-permute-start(bf16[512,768]{1,0:T(8,128)(2,1)S(1)} %bitcast.53), channel_id=1, source_target_pairs={{0,2},{2,4},{4,6},{1,3},{3,5},{5,7},{8,10},{10,12},{12,14},{9,11},... | collective-permute-start | bytes 2359304 | tf_op jit(solution)/shard_map/ppermute | solution.py:1023
  15.0 1.3 collective-permute-start.1
  16.3 0.7 pad_maximum_fusion
  17.1 17.3 %collective-permute-done.refs_0_ = bf16[512,768]{1,0:T(8,128)(2,1)S(1)} collective-permute-done((bf16[512,768]{1,0:T(8,128)(2,1)S(1)}, bf16[512,768]{1,0:T(8,128)(2,1)S(1)}, u32[]{:S(2)}, u32[]{:S(2)}) %collective-permute-start) | collective-permute-done | bytes 786464 | tf_op jit(solution)/shard_map/ppermute | solution.py:1023
  34.3 4.2 %collective-permute-done.1.refs_2_ = bf16[512,768]{1,0:T(8,128)(2,1)S(1)} collective-permute-done((bf16[512,768]{1,0:T(8,128)(2,1)S(1)}, bf16[512,768]{1,0:T(8,128)(2,1)S(1)}, u32[]{:S(2)}, u32[]{:S(2)}) %collective-permute-start.1) | collective-permute-done | bytes 786464 | tf_op jit(solution)/shard_map/ppermute | solution.py:1023
  38.5 4.4 %collective-permute-start.2 = (bf16[512,768]{1,0:T(8,128)(2,1)S(1)}, bf16[512,768]{1,0:T(8,128)(2,1)}, u32[]{:S(2)}, u32[]{:S(2)}) collective-permute-start(bf16[512,768]{1,0:T(8,128)(2,1)S(1)} %collective-permute-done.refs_0_), channel_id=1, source_target_pairs={{0,2},{2,4},{4,6},{1,3},{3,5},{5,7},{8,10},{10,12},{12,14},{9,11},... | collective-permute-start | bytes 2359304 | tf_op jit(solution)/shard_map/ppermute | solution.py:1023
  42.9 1.3 collective-permute-start.3
  44.2 22.3 %collective-permute-done.2.refs_1_ = bf16[512,768]{1,0:T(8,128)(2,1)} collective-permute-done((bf16[512,768]{1,0:T(8,128)(2,1)S(1)}, bf16[512,768]{1,0:T(8,128)(2,1)}, u32[]{:S(2)}, u32[]{:S(2)}) %collective-permute-start.2) | collective-permute-done | bytes 786464 | tf_op jit(solution)/shard_map/ppermute | solution.py:1023
  66.5 5.1 %collective-permute-start.4 = (bf16[512,768]{1,0:T(8,128)(2,1)}, bf16[512,768]{1,0:T(8,128)(2,1)S(1)}, u32[]{:S(2)}, u32[]{:S(2)}) collective-permute-start(bf16[512,768]{1,0:T(8,128)(2,1)} %collective-permute-done.2.refs_1_), channel_id=1, source_target_pairs={{0,2},{2,4},{4,6},{1,3},{3,5},{5,7},{8,10},{10,12},{12,14},{9,11},... | collective-permute-start | bytes 2359304 | tf_op jit(solution)/shard_map/ppermute | solution.py:1023
  71.6 2.4 collective-permute-done.3.refs_3_
  73.9 1.3 collective-permute-start.5
  76.0 3.1 all-gather.5.cloned.1.call-done.weights
  79.1 12.1 %project.1 = (bf16[768,2048]{1,0:T(8,128)(2,1)}, bf16[2048,384]{1,0:T(8,128)(2,1)}, bf16[2048,384]{1,0:T(8,128)(2,1)}, f32[8,768]{1,0:T(8,128)}, bf16[768,768]{1,0:T(8,128)(2,1)}) custom-call(s32[7]{0:T(128)} %concatenate.24.ints, bf16[768,2560]{1,0:T(8,128)(2,1)} %all-gather.5.cloned.1.call-done.weights, bf16[512,768]{1,0:T(8,128)(2,1)} %bitcast.49, ...), custom_call_target="tpu_custom_call" | custom-call | flops 4831838208 | bytes 12582912 | tf_op jit(solution)/shard_map/project/pallas_call | solution.py:398
  91.2 2.3 collective-permute-done.5.behind
  93.5 0.9 copy-done.11
  94.4 5.8 %project_last.1 = (bf16[768,2048]{1,0:T(8,128)(2,1)}, bf16[2048,384]{1,0:T(8,128)(2,1)}, bf16[2048,384]{1,0:T(8,128)(2,1)}) custom-call(s32[7]{0:T(128)} %concatenate.24.ints, bf16[768,2560]{1,0:T(8,128)(2,1)} %all-gather.5.cloned.1.call-done.weights, bf16[512,768]{1,0:T(8,128)(2,1)} %bitcast.50, ...), custom_call_target="tpu_custom_call", output_to_operand_aliasing={{0}: (7, {}), {1}: (8, {}), {2}: (9, {})} | custom-call | flops 1207959552 | bytes 3145728 | tf_op jit(solution)/shard_map/project_last/pallas_call | solution.py:452
  100.7 3.1 collective-permute-done.6.refs_1_
  103.8 1.2 copy-done.35
  105.0 16.0 %attend.3 = (bf16[16384,512]{1,0:T(8,128)(2,1)}, bf16[4,64,512]{2,1,0:T(8,128)(2,1)}, f32[4,80,512]{2,1,0:T(8,128)}) custom-call(s32[7]{0:T(128)} %concatenate.24.ints, f32[1,32]{1,0:T(1,128)} %get-tuple-element.200.table, bf16[2048,384]{1,0:T(8,128)(2,1)} %get-tuple-element.87.query, bf16[2048,384]{1,0:T(8,128)(2,1)} %get-tuple-element.88.refs_0_, ...), custom_call_target="tpu_custom_call" | custom-call | flops 8589934592 | bytes 16777216 | tf_op jit(solution)/shard_map/attend/pallas_call | solution.py:898
  121.0 3.6 all-to-all-start
  124.6 16.0 %attend.4 = (bf16[16384,512]{1,0:T(8,128)(2,1)}, bf16[4,64,512]{2,1,0:T(8,128)(2,1)}, f32[4,80,512]{2,1,0:T(8,128)}) custom-call(s32[7]{0:T(128)} %concatenate.24.ints, f32[1,32]{1,0:T(1,128)} %get-tuple-element.199.table, bf16[2048,384]{1,0:T(8,128)(2,1)} %get-tuple-element.87.query, bf16[2048,384]{1,0:T(8,128)(2,1)} %get-tuple-element.88.refs_0_, ...), custom_call_target="tpu_custom_call" | custom-call | flops 8589934592 | bytes 16777216 | tf_op jit(solution)/shard_map/attend/pallas_call | solution.py:898
  140.7 5.1 %all-to-all-start.1 = ((bf16[4,64,512]{2,1,0:T(8,128)(2,1)}), bf16[4,64,512]{2,1,0:T(8,128)(2,1)S(1)}, u32[]{:S(2)}, u32[]{:S(2)}) async-start(bf16[4,64,512]{2,1,0:T(8,128)(2,1)} %get-tuple-element.92), calls=%async_computation.1 | async-start | bytes 524288 | tf_op jit(solution)/shard_map/all_to_all | solution.py:1016
  145.7 16.0 %attend.5 = (bf16[16384,512]{1,0:T(8,128)(2,1)}, bf16[4,64,512]{2,1,0:T(8,128)(2,1)}, f32[4,80,512]{2,1,0:T(8,128)}) custom-call(s32[7]{0:T(128)} %concatenate.24.ints, f32[1,32]{1,0:T(1,128)} %get-tuple-element.198.table, bf16[2048,384]{1,0:T(8,128)(2,1)} %get-tuple-element.87.query, bf16[2048,384]{1,0:T(8,128)(2,1)} %get-tuple-element.88.refs_0_, ...), custom_call_target="tpu_custom_call" | custom-call | flops 8589934592 | bytes 16777216 | tf_op jit(solution)/shard_map/attend/pallas_call | solution.py:898
  162.1 15.4 %all_to_all.40.refs_2_ = bf16[4,64,512]{2,1,0:T(8,128)(2,1)} all-to-all(bf16[4,64,512]{2,1,0:T(8,128)(2,1)} %get-tuple-element.95), channel_id=1, replica_groups=mesh['batch'=4,'group'=4,'split'=2] {'group'}, dimensions={0} | all-to-all | bytes 524288 | tf_op jit(solution)/shard_map/all_to_all | solution.py:1016
  177.5 0.7 all-gather.3.cloned.1.call-done.w_out.w_gate.w_up.w_packed
  178.2 28.6 %feed_forward.1 = (bf16[512,768]{1,0:T(8,128)(2,1)}, f32[512,768]{1,0:T(8,128)}, bf16[4,64,512]{2,1,0:T(8,128)(2,1)}, bf16[4,128,512]{2,1,0:T(8,128)(2,1)}, bf16...) custom-call(s32[7]{0:T(128)} %concatenate.24.ints, ...), custom_call_target="tpu_custom_call" | custom-call | flops 16307453952 | bytes 18874368 | tf_op jit(solution)/shard_map/feed_forward/pallas_call | solution.py:626
  207.4 13.7 %all_to_all.41 = bf16[4,64,512]{2,1,0:T(8,128)(2,1)} all-to-all(bf16[4,64,512]{2,1,0:T(8,128)(2,1)} %get-tuple-element.98), channel_id=1, replica_groups=mesh['batch'=4,'group'=4,'split'=2] {'group'}, dimensions={0} | all-to-all | bytes 524288 | tf_op jit(solution)/shard_map/all_to_all | solution.py:1016
  221.1 1.9 copy-done.2
  223.5 7.0 %joined.1 = bf16[384,7168]{1,0:T(8,128)(2,1)} custom-call(bf16[384,5120]{1,0:T(8,128)(2,1)} %get-tuple-element.99.refs_0_, bf16[384,5120]{1,0:T(8,128)(2,1)} %copy-done.2, bf16[384,2048]{1,0:T(8,128)(2,1)} %get-tuple-element.102.refs_2_, bf16[384,2048]{1,0:T(8,128)(2,1)} %copy-done.8), custom_call_target="tpu_custom_call" | custom-call | bytes 1048576 | tf_op jit(solution)/shard_map/joined/pallas_call | solution.py:759
  230.6 3.7 all-to-all-start.4
  234.2 22.2 %attend_back.3 = (bf16[4,192,512]{2,1,0:T(8,128)(2,1)}, bf16[4,128,512]{2,1,0:T(8,128)(2,1)}, f32[32,128]{1,0:T(8,128)}) custom-call(s32[7]{0:T(128)} %concatenate.24.ints, bf16[2048,384]{1,0:T(8,128)(2,1)} %get-tuple-element.87.query, bf16[4,1,64,512]{3,2,1,0:T(8,128)(2,1)} %bitcast.64, f32[4,80,512]{2,1,0:T(8,128)} %get-tuple-element.105.stats, ...), custom_call_target="tpu_custom_call" | custom-call | flops 17179869184 | bytes 16777216 | tf_op jit(solution)/shard_map/attend_back/pallas_call | solution.py:935
  256.6 2.1 collective-permute-done.9
  258.7 2.2 add_convert_fusion.2.refs_0_
  260.9 5.2 %all-to-all-start.5 = ((bf16[4,192,512]{2,1,0:T(8,128)(2,1)}), bf16[4,192,512]{2,1,0:T(8,128)(2,1)S(1)}, u32[]{:S(2)}, u32[]{:S(2)}) async-start(bf16[4,192,512]{2,1,0:T(8,128)(2,1)} %add_convert_fusion.2.refs_0_), calls=%async_computation.5 | async-start | bytes 1572864 | tf_op jit(solution)/shard_map/all_to_all | solution.py:1016
  266.0 21.5 %attend_back.4 = (bf16[4,192,512]{2,1,0:T(8,128)(2,1)}, bf16[4,128,512]{2,1,0:T(8,128)(2,1)}, f32[32,128]{1,0:T(8,128)}) custom-call(s32[7]{0:T(128)} %concatenate.24.ints, bf16[2048,384]{1,0:T(8,128)(2,1)} %get-tuple-element.87.query, bf16[4,2,64,512]{3,2,1,0:T(8,128)(2,1)} %bitcast.60, f32[4,80,512]{2,1,0:T(8,128)} %get-tuple-element.114.stats, ...), custom_call_target="tpu_custom_call" | custom-call | flops 17179869184 | bytes 16777216 | tf_op jit(solution)/shard_map/attend_back/pallas_call | solution.py:935
  287.6 2.1 collective-permute-done.10
  289.7 2.2 add_convert_fusion.1.refs_1_
  291.9 5.1 %all-to-all-start.6 = ((bf16[4,192,512]{2,1,0:T(8,128)(2,1)}), bf16[4,192,512]{2,1,0:T(8,128)(2,1)S(1)}, u32[]{:S(2)}, u32[]{:S(2)}) async-start(bf16[4,192,512]{2,1,0:T(8,128)(2,1)} %add_convert_fusion.1.refs_1_), calls=%async_computation.6 | async-start | bytes 1572864 | tf_op jit(solution)/shard_map/all_to_all | solution.py:1016
  297.5 21.6 %attend_back.5 = (bf16[4,192,512]{2,1,0:T(8,128)(2,1)}, bf16[4,128,512]{2,1,0:T(8,128)(2,1)}, f32[32,128]{1,0:T(8,128)}) custom-call(s32[7]{0:T(128)} %concatenate.24.ints, bf16[2048,384]{1,0:T(8,128)(2,1)} %get-tuple-element.87.query, bf16[4,2,64,512]{3,2,1,0:T(8,128)(2,1)} %bitcast.61, f32[4,80,512]{2,1,0:T(8,128)} %get-tuple-element.122.stats, ...), custom_call_target="tpu_custom_call" | custom-call | flops 17179869184 | bytes 16777216 | tf_op jit(solution)/shard_map/attend_back/pallas_call | solution.py:935
  319.1 2.1 collective-permute-done.11
  321.2 2.2 add_convert_fusion.refs_2_
  323.4 6.8 %all-to-all-done.6.refs_1_ = bf16[4,192,512]{2,1,0:T(8,128)(2,1)S(1)} async-done(((bf16[4,192,512]{2,1,0:T(8,128)(2,1)}), bf16[4,192,512]{2,1,0:T(8,128)(2,1)S(1)}, u32[]{:S(2)}, u32[]{:S(2)}) %all-to-all-start.6) | async-done | bytes 786464 | tf_op jit(solution)/shard_map/all_to_all | solution.py:1016
  330.3 4.5 %all-to-all-start.7 = ((bf16[4,192,512]{2,1,0:T(8,128)(2,1)}), bf16[4,192,512]{2,1,0:T(8,128)(2,1)S(1)}, u32[]{:S(2)}, u32[]{:S(2)}) async-start(bf16[4,192,512]{2,1,0:T(8,128)(2,1)} %add_convert_fusion.refs_2_), calls=%async_computation.7 | async-start | bytes 1572864 | tf_op jit(solution)/shard_map/all_to_all | solution.py:1016
  334.7 6.7 %weight_grads.1 = (bf16[384,576]{1,0:T(8,128)(2,1)}, bf16[384,576]{1,0:T(8,128)(2,1)}) custom-call(bf16[768,2048]{1,0:T(8,128)(2,1)} %get-tuple-element.127.normed_t, bf16[4,192,512]{2,1,0:T(8,128)(2,1)} %add_convert_fusion.2.refs_0_, bf16[4,192,512]{2,1,0:T(8,128)(2,1)} %add_convert_fusion.1.refs_1_, bf16[4,192,512]{2,1,0:T(8,128)(2,1)} %add_convert_fusion.refs_2_), custom_call_target="tpu_custom_call" | custom-call | flops 1811939328 | bytes 3145728 | tf_op jit(solution)/shard_map/weight_grads/pallas_call | solution.py:707
  341.5 2.1 collective-permute-done.12.refs_1_
  343.6 0.8 copy-done.14
  344.3 2.0 added.1
  346.3 1.5 collective-permute-start.13
  347.8 1.5 collective-permute-start.14
  349.3 1.5 collective-permute-start.15
  350.7 5.6 %all-to-all-done.7.refs_2_ = bf16[4,192,512]{2,1,0:T(8,128)(2,1)S(1)} async-done(((bf16[4,192,512]{2,1,0:T(8,128)(2,1)}), bf16[4,192,512]{2,1,0:T(8,128)(2,1)S(1)}, u32[]{:S(2)}, u32[]{:S(2)}) %all-to-all-start.7) | async-done | bytes 786464 | tf_op jit(solution)/shard_map/all_to_all | solution.py:1016
  357.2 2.2 counted.1
  359.4 2.4 collective-permute-start.16
  362.8 1.0 bitcast_convert_fusion
  363.9 0.7 multiply_reduce_fusion.5
  366.4 0.7 copy.67
  367.1 8.5 %input_grads.1 = bf16[512,768]{1,0:T(8,128)(2,1)} custom-call(bf16[768,2560]{1,0:T(8,128)(2,1)} %all-gather.5.cloned.1.call-done.weights, bf16[512,768]{1,0:T(8,128)(2,1)} %bitcast.52, f32[8,768]{1,0:T(8,128)} %get-tuple-element.82.gains, f32[512,768]{1,0:T(8,128)} %get-tuple-element.97.d_mixed, bf16[4,192,512]{2,1,0:T(8,128)(2,1)} %copy-done.4, ...), custom_call_target="tpu_custom_call" | custom-call | tf_op jit(solution)/shard_map/input_grads/pallas_call | solution.py:868
  375.7 2.8 collective-permute-start.19
  378.6 1.1 collective-permute-start.21
  379.8 2.1 collective-permute-done.19
  381.9 5.5 %collective-permute-done.20 = f32[40,640]{1,0:T(8,128)S(1)} collective-permute-done((f32[40,640]{1,0:T(8,128)S(1)}, f32[40,640]{1,0:T(8,128)S(1)}, u32[]{:S(2)}, u32[]{:S(2)}) %collective-permute-start.20) | collective-permute-done | bytes 102432 | tf_op jit(solution)/shard_map/ppermute | solution.py:1013
  394.6 0.6 multiply_add_fusion
  (170 shorter events, 14.9 us)
Async XLA Ops:
  7.2 93.0 %copy-start = (f32[32,12]{0,1:T(8,128)S(1)}, f32[32,12]{0,1:T(8,128)}, u32[]{:S(2)}) copy-start(f32[32,12]{0,1:T(8,128)} %param.22) | copy-start | bytes 4612
  7.2 2.8 copy-start.3
  7.2 9.0 %copy-start.22 = (bf16[64,768]{1,0:T(8,128)(2,1)S(1)}, bf16[64,768]{1,0:T(8,128)(2,1)}, u32[]{:S(2)}) copy-start(bf16[64,768]{1,0:T(8,128)(2,1)} %param.26) | copy-start | bytes 294916
  7.2 9.1 %copy-start.27 = (bf16[24,768]{1,0:T(8,128)(2,1)S(1)}, bf16[24,768]{1,0:T(8,128)(2,1)}, u32[]{:S(2)}) copy-start(bf16[24,768]{1,0:T(8,128)(2,1)} %param.23) | copy-start | bytes 110596
  7.3 9.1 %copy-start.12 = (bf16[24,4096]{1,0:T(8,128)(2,1)S(1)}, bf16[24,4096]{1,0:T(8,128)(2,1)}, u32[]{:S(2)}) copy-start(bf16[24,4096]{1,0:T(8,128)(2,1)} %param.25) | copy-start | bytes 589828
  7.3 71.9 %all-gather.5.cloned.1.call-start = ((), (), s32[]{:S(2)}) async-start(), calls=%async_computation.11 | async-start | bytes 4055040 | tf_op jit(solution)/shard_map/all_gather | solution.py:1041
  8.5 66.7 %copy-start.38 = (s32[1,3]{1,0:T(1,128)S(1)}, s32[1,3]{1,0:T(1,128)}, u32[]{:S(2)}) copy-start(s32[1,3]{1,0:T(1,128)} %param.19) | copy-start | bytes 40
  9.9 168.3 %all-gather.3.cloned.1.call-start = ((), (), s32[]{:S(2)}) async-start(), calls=%async_computation.10 | async-start | bytes 10948608 | tf_op jit(solution)/shard_map/all_gather | solution.py:1045
  10.0 24.4 %collective-permute-start = (bf16[512,768]{1,0:T(8,128)(2,1)S(1)}, bf16[512,768]{1,0:T(8,128)(2,1)S(1)}, u32[]{:S(2)}, u32[]{:S(2)}) collective-permute-start(bf16[512,768]{1,0:T(8,128)(2,1)S(1)} %bitcast.53), channel_id=1, source_target_pairs={{0,2},{2,4},{4,6},{1,3},{3,5},{5,7},{8,10},{10,12},{12,14},{9,11},... | collective-permute-start | bytes 2359304 | tf_op jit(solution)/shard_map/ppermute | solution.py:1023
  15.0 23.5 %collective-permute-start.1 = (bf16[512,768]{1,0:T(8,128)(2,1)S(1)}, bf16[512,768]{1,0:T(8,128)(2,1)S(1)}, u32[]{:S(2)}, u32[]{:S(2)}) collective-permute-start(bf16[512,768]{1,0:T(8,128)(2,1)S(1)} %bitcast.54), channel_id=1, source_target_pairs={{2,0},{4,2},{6,4},{3,1},{5,3},{7,5},{10,8},{12,10},{14,12},{11,9},... | collective-permute-start | bytes 2359304 | tf_op jit(solution)/shard_map/ppermute | solution.py:1023
  34.3 44.8 %copy-start.36 = (bf16[512,768]{1,0:T(8,128)(2,1)}, bf16[512,768]{1,0:T(8,128)(2,1)S(1)}, u32[]{:S(2)}) copy-start(bf16[512,768]{1,0:T(8,128)(2,1)S(1)} %collective-permute-done.refs_0_) | copy-start | bytes 2359300
  38.5 40.6 %copy-start.37 = (bf16[512,768]{1,0:T(8,128)(2,1)}, bf16[512,768]{1,0:T(8,128)(2,1)S(1)}, u32[]{:S(2)}) copy-start(bf16[512,768]{1,0:T(8,128)(2,1)S(1)} %collective-permute-done.1.refs_2_) | copy-start | bytes 2359300
  38.5 27.9 %collective-permute-start.2 = (bf16[512,768]{1,0:T(8,128)(2,1)S(1)}, bf16[512,768]{1,0:T(8,128)(2,1)}, u32[]{:S(2)}, u32[]{:S(2)}) collective-permute-start(bf16[512,768]{1,0:T(8,128)(2,1)S(1)} %collective-permute-done.refs_0_), channel_id=1, source_target_pairs={{0,2},{2,4},{4,6},{1,3},{3,5},{5,7},{8,10},{10,12},{12,14},{9,11},... | collective-permute-start | bytes 2359304 | tf_op jit(solution)/shard_map/ppermute | solution.py:1023
  42.9 31.0 %collective-permute-start.3 = (bf16[512,768]{1,0:T(8,128)(2,1)S(1)}, bf16[512,768]{1,0:T(8,128)(2,1)}, u32[]{:S(2)}, u32[]{:S(2)}) collective-permute-start(bf16[512,768]{1,0:T(8,128)(2,1)S(1)} %collective-permute-done.1.refs_2_), channel_id=1, source_target_pairs={{2,0},{4,2},{6,4},{3,1},{5,3},{7,5},{10,8},{12,10},{14,12},{11,9},... | collective-permute-start | bytes 2359304 | tf_op jit(solution)/shard_map/ppermute | solution.py:1023
  66.5 24.8 %collective-permute-start.4 = (bf16[512,768]{1,0:T(8,128)(2,1)}, bf16[512,768]{1,0:T(8,128)(2,1)S(1)}, u32[]{:S(2)}, u32[]{:S(2)}) collective-permute-start(bf16[512,768]{1,0:T(8,128)(2,1)} %collective-permute-done.2.refs_1_), channel_id=1, source_target_pairs={{0,2},{2,4},{4,6},{1,3},{3,5},{5,7},{8,10},{10,12},{12,14},{9,11},... | collective-permute-start | bytes 2359304 | tf_op jit(solution)/shard_map/ppermute | solution.py:1023
  73.9 19.6 %collective-permute-start.5 = (bf16[512,768]{1,0:T(8,128)(2,1)}, bf16[512,768]{1,0:T(8,128)(2,1)S(1)}, u32[]{:S(2)}, u32[]{:S(2)}) collective-permute-start(bf16[512,768]{1,0:T(8,128)(2,1)} %collective-permute-done.3.refs_3_), channel_id=1, source_target_pairs={{2,0},{4,2},{6,4},{3,1},{5,3},{7,5},{10,8},{12,10},{14,12},{11,9},... | collective-permute-start | bytes 2359304 | tf_op jit(solution)/shard_map/ppermute | solution.py:1023
  100.2 3.6 collective-permute-start.6
  121.0 19.7 %all-to-all-start = ((bf16[4,64,512]{2,1,0:T(8,128)(2,1)}), bf16[4,64,512]{2,1,0:T(8,128)(2,1)S(1)}, u32[]{:S(2)}, u32[]{:S(2)}) async-start(bf16[4,64,512]{2,1,0:T(8,128)(2,1)} %get-tuple-element.89), calls=%async_computation | async-start | bytes 524288 | tf_op jit(solution)/shard_map/all_to_all | solution.py:1016
  140.7 21.0 %copy-start.16 = (bf16[4,64,512]{2,1,0:T(8,128)(2,1)}, bf16[4,64,512]{2,1,0:T(8,128)(2,1)S(1)}, u32[]{:S(2)}) copy-start(bf16[4,64,512]{2,1,0:T(8,128)(2,1)S(1)} %all-to-all-done.refs_0_) | copy-start | bytes 786436
  140.7 21.5 %all-to-all-start.1 = ((bf16[4,64,512]{2,1,0:T(8,128)(2,1)}), bf16[4,64,512]{2,1,0:T(8,128)(2,1)S(1)}, u32[]{:S(2)}, u32[]{:S(2)}) async-start(bf16[4,64,512]{2,1,0:T(8,128)(2,1)} %get-tuple-element.92), calls=%async_computation.1 | async-start | bytes 524288 | tf_op jit(solution)/shard_map/all_to_all | solution.py:1016
  145.7 151.5 %reduce-scatter.7.cloned.1.call-start = ((), (), s32[]{:S(2)}) async-start(), calls=%async_computation.13 | async-start | bytes 6881280
  162.1 16.1 %copy-start.17 = (bf16[4,64,512]{2,1,0:T(8,128)(2,1)}, bf16[4,64,512]{2,1,0:T(8,128)(2,1)S(1)}, u32[]{:S(2)}) copy-start(bf16[4,64,512]{2,1,0:T(8,128)(2,1)S(1)} %all-to-all-done.1.refs_1_) | copy-start | bytes 786436
  206.8 14.3 %collective-permute-start.7 = (bf16[384,5120]{1,0:T(8,128)(2,1)}, bf16[384,5120]{1,0:T(8,128)(2,1)S(1)}, u32[]{:S(2)}, u32[]{:S(2)}) collective-permute-start(bf16[384,5120]{1,0:T(8,128)(2,1)} %get-tuple-element.100), channel_id=1, source_target_pairs={{1,0},{0,1},{3,2},{2,3},{5,4},{4,5},{7,6},{6,7},{9,8},{8,9},{11,10... | collective-permute-start | bytes 11796488 | tf_op jit(solution)/shard_map/ppermute | solution.py:1013
  207.2 13.9 %collective-permute-start.8 = (bf16[384,2048]{1,0:T(8,128)(2,1)}, bf16[384,2048]{1,0:T(8,128)(2,1)S(1)}, u32[]{:S(2)}, u32[]{:S(2)}) collective-permute-start(bf16[384,2048]{1,0:T(8,128)(2,1)} %get-tuple-element.103), channel_id=1, source_target_pairs={{1,0},{0,1},{3,2},{2,3},{5,4},{4,5},{7,6},{6,7},{9,8},{8,9},{11,10... | collective-permute-start | bytes 4718600 | tf_op jit(solution)/shard_map/ppermute | solution.py:1013
  230.6 25.9 %all-to-all-start.4 = ((bf16[4,128,512]{2,1,0:T(8,128)(2,1)}), bf16[4,128,512]{2,1,0:T(8,128)(2,1)S(1)}, u32[]{:S(2)}, u32[]{:S(2)}) async-start(bf16[4,128,512]{2,1,0:T(8,128)(2,1)} %get-tuple-element.110), calls=%async_computation.4 | async-start | bytes 1048576 | tf_op jit(solution)/shard_map/all_to_all | solution.py:1016
  256.5 4.4 %copy-start.13 = (bf16[4,128,512]{2,1,0:T(8,128)(2,1)}, bf16[4,128,512]{2,1,0:T(8,128)(2,1)S(1)}, u32[]{:S(2)}) copy-start(bf16[4,128,512]{2,1,0:T(8,128)(2,1)S(1)} %all-to-all-done.4) | copy-start | bytes 1572868
  256.5 2.2 collective-permute-start.9
  260.9 26.7 %all-to-all-start.5 = ((bf16[4,192,512]{2,1,0:T(8,128)(2,1)}), bf16[4,192,512]{2,1,0:T(8,128)(2,1)S(1)}, u32[]{:S(2)}, u32[]{:S(2)}) async-start(bf16[4,192,512]{2,1,0:T(8,128)(2,1)} %add_convert_fusion.2.refs_0_), calls=%async_computation.5 | async-start | bytes 1572864 | tf_op jit(solution)/shard_map/all_to_all | solution.py:1016
  287.5 4.4 %copy-start.4 = (bf16[4,192,512]{2,1,0:T(8,128)(2,1)}, bf16[4,192,512]{2,1,0:T(8,128)(2,1)S(1)}, u32[]{:S(2)}) copy-start(bf16[4,192,512]{2,1,0:T(8,128)(2,1)S(1)} %all-to-all-done.5.refs_0_) | copy-start | bytes 2359300
  287.5 2.2 collective-permute-start.10
  291.9 38.4 %all-to-all-start.6 = ((bf16[4,192,512]{2,1,0:T(8,128)(2,1)}), bf16[4,192,512]{2,1,0:T(8,128)(2,1)S(1)}, u32[]{:S(2)}, u32[]{:S(2)}) async-start(bf16[4,192,512]{2,1,0:T(8,128)(2,1)} %add_convert_fusion.1.refs_1_), calls=%async_computation.6 | async-start | bytes 1572864 | tf_op jit(solution)/shard_map/all_to_all | solution.py:1016
  297.0 59.5 %reduce-scatter.5.cloned.1.call-start = ((), (), s32[]{:S(2)}) async-start(), calls=%async_computation.12 | async-start | bytes 1720320 | tf_op jit(solution)/shard_map/reduce_scatter | solution.py:1104
  319.1 2.1 collective-permute-start.11
  330.3 11.2 %copy-start.5 = (bf16[4,192,512]{2,1,0:T(8,128)(2,1)}, bf16[4,192,512]{2,1,0:T(8,128)(2,1)S(1)}, u32[]{:S(2)}) copy-start(bf16[4,192,512]{2,1,0:T(8,128)(2,1)S(1)} %all-to-all-done.6.refs_1_) | copy-start | bytes 2359300
  330.3 26.1 %all-to-all-start.7 = ((bf16[4,192,512]{2,1,0:T(8,128)(2,1)}), bf16[4,192,512]{2,1,0:T(8,128)(2,1)S(1)}, u32[]{:S(2)}, u32[]{:S(2)}) async-start(bf16[4,192,512]{2,1,0:T(8,128)(2,1)} %add_convert_fusion.refs_2_), calls=%async_computation.7 | async-start | bytes 1572864 | tf_op jit(solution)/shard_map/all_to_all | solution.py:1016
  341.5 2.1 collective-permute-start.12
  346.3 10.0 %collective-permute-start.13 = (bf16[96,576]{1,0:T(8,128)(2,1)}, bf16[96,576]{1,0:T(8,128)(2,1)S(1)}, u32[]{:S(2)}, u32[]{:S(2)}) collective-permute-start(bf16[96,576]{1,0:T(8,128)(2,1)} %get-tuple-element.132), channel_id=1, source_target_pairs={{24,0},{0,8},{8,16},{16,24},{25,1},{1,9},{9,17},{17,25},{26,2},{2,... | collective-permute-start | bytes 331784 | tf_op jit(solution)/shard_map/ppermute | solution.py:1013
  347.8 8.6 %collective-permute-start.14 = (bf16[96,576]{1,0:T(8,128)(2,1)}, bf16[96,576]{1,0:T(8,128)(2,1)S(1)}, u32[]{:S(2)}, u32[]{:S(2)}) collective-permute-start(bf16[96,576]{1,0:T(8,128)(2,1)} %get-tuple-element.133), channel_id=1, source_target_pairs={{16,0},{24,8},{0,16},{8,24},{17,1},{25,9},{1,17},{9,25},{18,2},{26... | collective-permute-start | bytes 331784 | tf_op jit(solution)/shard_map/ppermute | solution.py:1013
  349.3 7.1 %collective-permute-start.15 = (bf16[96,576]{1,0:T(8,128)(2,1)}, bf16[96,576]{1,0:T(8,128)(2,1)S(1)}, u32[]{:S(2)}, u32[]{:S(2)}) collective-permute-start(bf16[96,576]{1,0:T(8,128)(2,1)} %get-tuple-element.134), channel_id=1, source_target_pairs={{8,0},{16,8},{24,16},{0,24},{9,1},{17,9},{25,17},{1,25},{10,2},{18... | collective-permute-start | bytes 331784 | tf_op jit(solution)/shard_map/ppermute | solution.py:1013
  356.4 8.6 %copy-start.6 = (bf16[4,192,512]{2,1,0:T(8,128)(2,1)}, bf16[4,192,512]{2,1,0:T(8,128)(2,1)S(1)}, u32[]{:S(2)}) copy-start(bf16[4,192,512]{2,1,0:T(8,128)(2,1)S(1)} %all-to-all-done.7.refs_2_) | copy-start | bytes 2359300
  359.4 16.2 %collective-permute-start.16 = (f32[16,640]{1,0:T(8,128)}, f32[16,640]{1,0:T(8,128)S(1)}, u32[]{:S(2)}, u32[]{:S(2)}) collective-permute-start(f32[16,640]{1,0:T(8,128)} %get-tuple-element.138), channel_id=1, source_target_pairs={{8,0},{16,8},{24,16},{0,24},{9,1},{17,9},{25,17},{1,25},{10,2},{18... | collective-permute-start | bytes 122888 | tf_op jit(solution)/shard_map/ppermute | solution.py:1013
  361.7 13.9 %collective-permute-start.17 = (f32[16,640]{1,0:T(8,128)}, f32[16,640]{1,0:T(8,128)S(1)}, u32[]{:S(2)}, u32[]{:S(2)}) collective-permute-start(f32[16,640]{1,0:T(8,128)} %get-tuple-element.138), channel_id=1, source_target_pairs={{16,0},{24,8},{0,16},{8,24},{17,1},{25,9},{1,17},{9,25},{18,2},{26... | collective-permute-start | bytes 122888 | tf_op jit(solution)/shard_map/ppermute | solution.py:1013
  362.3 13.3 %collective-permute-start.18 = (f32[16,640]{1,0:T(8,128)}, f32[16,640]{1,0:T(8,128)S(1)}, u32[]{:S(2)}, u32[]{:S(2)}) collective-permute-start(f32[16,640]{1,0:T(8,128)} %get-tuple-element.138), channel_id=1, source_target_pairs={{24,0},{0,8},{8,16},{16,24},{25,1},{1,9},{9,17},{17,25},{26,2},{2,... | collective-permute-start | bytes 122888 | tf_op jit(solution)/shard_map/ppermute | solution.py:1013
  365.4 10.2 %copy-start.7 = (f32[24,4096]{1,0:T(8,128)}, f32[24,4096]{1,0:T(8,128)S(1)}, u32[]{:S(2)}) copy-start(f32[24,4096]{1,0:T(8,128)S(1)} %reshape.126) | copy-start | bytes 1179652
  367.1 8.5 %copy-start.26 = (f32[16,640]{1,0:T(8,128)S(1)}, f32[16,640]{1,0:T(8,128)}, u32[]{:S(2)}) copy-start(f32[16,640]{1,0:T(8,128)} %get-tuple-element.138) | copy-start | bytes 122884
  367.1 8.5 %copy-start.23 = (f32[24,640]{1,0:T(8,128)S(1)}, f32[24,640]{1,0:T(8,128)}, u32[]{:S(2)}) copy-start(f32[24,640]{1,0:T(8,128)} %get-tuple-element.143) | copy-start | bytes 184324
  367.1 8.6 %copy-start.24 = (f32[24,640]{1,0:T(8,128)S(1)}, f32[24,640]{1,0:T(8,128)}, u32[]{:S(2)}) copy-start(f32[24,640]{1,0:T(8,128)} %get-tuple-element.142) | copy-start | bytes 184324
  367.1 8.6 %copy-start.25 = (f32[24,640]{1,0:T(8,128)S(1)}, f32[24,640]{1,0:T(8,128)}, u32[]{:S(2)}) copy-start(f32[24,640]{1,0:T(8,128)} %get-tuple-element.141) | copy-start | bytes 184324
  367.1 20.4 %copy-start.18 = (f32[24,640]{1,0:T(8,128)S(1)}, f32[24,640]{1,0:T(8,128)}, u32[]{:S(2)}) copy-start(f32[24,640]{1,0:T(8,128)} %get-tuple-element.144) | copy-start | bytes 184324
  375.7 12.5 %copy-start.15 = (bf16[24,2304]{1,0:T(8,128)(2,1)S(1)}, bf16[24,2304]{1,0:T(8,128)(2,1)}, u32[]{:S(2)}) copy-start(bf16[24,2304]{1,0:T(8,128)(2,1)} %param.21) | copy-start | bytes 331780
  375.7 6.2 %collective-permute-start.19 = (f32[40,640]{1,0:T(8,128)S(1)}, f32[40,640]{1,0:T(8,128)S(1)}, u32[]{:S(2)}, u32[]{:S(2)}) collective-permute-start(f32[40,640]{1,0:T(8,128)S(1)} %get-tuple-element.195), channel_id=1, source_target_pairs={{2,0},{4,2},{6,4},{0,6},{3,1},{5,3},{7,5},{1,7},{10,8},{12,10},{14... | collective-permute-start | bytes 307208 | tf_op jit(solution)/shard_map/ppermute | solution.py:1013
  378.6 8.9 %collective-permute-start.20 = (f32[40,640]{1,0:T(8,128)S(1)}, f32[40,640]{1,0:T(8,128)S(1)}, u32[]{:S(2)}, u32[]{:S(2)}) collective-permute-start(f32[40,640]{1,0:T(8,128)S(1)} %get-tuple-element.196), channel_id=1, source_target_pairs={{4,0},{6,2},{0,4},{2,6},{5,1},{7,3},{1,5},{3,7},{12,8},{14,10},{8,... | collective-permute-start | bytes 307208 | tf_op jit(solution)/shard_map/ppermute | solution.py:1013
  378.6 8.9 %collective-permute-start.21 = (f32[40,640]{1,0:T(8,128)S(1)}, f32[40,640]{1,0:T(8,128)S(1)}, u32[]{:S(2)}, u32[]{:S(2)}) collective-permute-start(f32[40,640]{1,0:T(8,128)S(1)} %get-tuple-element.197), channel_id=1, source_target_pairs={{6,0},{0,2},{2,4},{4,6},{7,1},{1,3},{3,5},{5,7},{14,8},{8,10},{10,... | collective-permute-start | bytes 307208 | tf_op jit(solution)/shard_map/ppermute | solution.py:1013
  387.5 1.4 collective-permute-start.22
  387.5 6.6 %copy-start.41 = (f32[64]{0:T(128)S(1)}, f32[64]{0:T(128)}, u32[]{:S(2)}) copy-start(f32[64]{0:T(128)} %param.34) | copy-start | bytes 772
  387.6 7.1 %copy-start.28 = (f32[4096]{0:T(1024)S(1)}, f32[4096]{0:T(1024)}, u32[]{:S(2)}) copy-start(f32[4096]{0:T(1024)} %param.33) | copy-start | bytes 49156
  387.6 10.0 %copy-start.1 = (f32[32,12]{0,1:T(8,128)S(1)}, f32[32,12]{0,1:T(8,128)}, u32[]{:S(2)}) copy-start(f32[32,12]{0,1:T(8,128)} %param.22) | copy-start | bytes 4612
  387.6 7.6 %copy-start.29 = (f32[2304]{0:T(1024)S(1)}, f32[2304]{0:T(1024)}, u32[]{:S(2)}) copy-start(f32[2304]{0:T(1024)} %param.29) | copy-start | bytes 27652
  387.6 8.2 %copy-start.32 = (f32[24]{0:T(128)S(1)}, f32[24]{0:T(128)}, u32[]{:S(2)}) copy-start(f32[24]{0:T(128)} %param.28) | copy-start | bytes 292
  387.6 8.8 %copy-start.30 = (f32[768]{0:T(1024)S(1)}, f32[768]{0:T(1024)}, u32[]{:S(2)}) copy-start(f32[768]{0:T(1024)} %param.35) | copy-start | bytes 9220
  387.7 8.7 %copy-start.31 = (f32[768]{0:T(1024)S(1)}, f32[768]{0:T(1024)}, u32[]{:S(2)}) copy-start(f32[768]{0:T(1024)} %param.31) | copy-start | bytes 9220
  387.7 9.3 %copy-start.33 = (f32[24]{0:T(128)S(1)}, f32[24]{0:T(128)}, u32[]{:S(2)}) copy-start(f32[24]{0:T(128)} %param.32) | copy-start | bytes 292
  387.7 9.3 %copy-start.34 = (f32[24]{0:T(128)S(1)}, f32[24]{0:T(128)}, u32[]{:S(2)}) copy-start(f32[24]{0:T(128)} %param.30) | copy-start | bytes 292
  388.1 9.4 %copy-start.9 = (f32[24,2304]{1,0:T(8,128)}, f32[24,2304]{1,0:T(8,128)S(1)}, u32[]{:S(2)}) copy-start(f32[24,2304]{1,0:T(8,128)S(1)} %concatenate.31) | copy-start | bytes 663556
  (11 other events, 15.3 us)
Sparse Core Ops, SparseCore 0:
  11.7 67.3 all-gather.4
  82.7 95.4 all-gather.2
  230.7 62.5 reduce-scatter.6
  299.8 45.8 reduce-scatter.4
where the time goes:
time: 410 us; the launch traced here: 404 us
  Pallas kernels  186 us (45%)
  waiting for transfers between devices  84.6 us (21%)
  starting transfers between devices  58.3 us (14%)
  blocking collectives  29.1 us (7%)
  between operations  17.4 us (4%)
  other arithmetic  16.6 us (4%)
  local copies, waits for them, and re-layouts  12.3 us (3%)
    pallas_call x3, Pallas kernels, attend_back(): pl.pallas_call(functools.partial(backward_kernel, tokens, groups, splits)...  65.3 us
    ppermute x6, waiting for transfers between devices, line(): return lax.ppermute(array, 'group', pairs)  48.3 us
    pallas_call x3, Pallas kernels, attend(): pl.pallas_call(functools.partial(forward_kernel, tokens, groups, splits),...  48 us
    all_to_all x2, blocking collectives, swap_groups(): return lax.all_to_all(array, 'group', 0, 0)  29.1 us
    pallas_call x1, Pallas kernels, feed_forward(): pl.pallas_call(functools.partial(block_kernel, dims, len(contexts)), grid...  28.6 us
    all_to_all x6, starting transfers between devices, swap_groups(): return lax.all_to_all(array, 'group', 0, 0)  27 us
    ppermute x17, waiting for transfers between devices, ahead(): lax.ppermute(array, axis, [((i + by) % size, i) for i in range(size)])  19.1 us
    ppermute x6, starting transfers between devices, line(): return lax.ppermute(array, 'group', pairs)  18.3 us
  transfers between devices with their start and end apart: 33, of which 17 were waited for; matrix products, arithmetic and copies ran while one was open for 3% of the time, Pallas kernels for 37%

commit v1 on v0

--- a/solution.py
+++ b/solution.py
@@ -476,18 +476,16 @@
     )(ints, weights, own, before, behind, order, gains, normed_t, query, kv)
 
 
-def split_order(split, splits, unit):
-    def source_of(count):
-        part = count // splits
-
-        def source(index):
-            r = lax.rem(split + index // part, splits)
-            index = lax.rem(index, part)
-            return (index // unit * splits + r) * unit + lax.rem(index, unit)
-
-        return source
-
-    return source_of
+def scatter_order(groups, splits, unit):
+    def source(index):
+        within = lax.rem(index, unit)
+        index = index // unit
+        g = lax.rem(index, groups)
+        index = index // groups
+        r = lax.rem(index, splits)
+        return ((index // splits * groups + g) * splits + r) * unit + within
+
+    return source
 
 
 def packed_rows(values, tall, low):
@@ -535,9 +533,9 @@
 ):
     rows_apart, groups, splits = dims
     contexts, refs = refs[:heads], refs[heads:]
-    result, d_mixed, d_first, d_rest = refs[:4]
-    grads_wide, grads_down = refs[4 : 4 + splits], refs[4 + splits : 4 + 2 * splits]
-    (context_t, mixed, normed, normed_t, d_normed, total, order, order_hidden) = refs[4 + 2 * splits :]
+    result, d_mixed, d_first, d_rest, grads = refs[:5]
+    (context_t, mixed, normed, normed_t, d_normed, total, order, order_hidden) = refs[5:13]
+    wide, down, sems = refs[13:]
     step, chunks = pl.program_id(0), pl.num_programs(0) - 1
     width, chunk = w_gate.shape
     devices = rows_apart * groups * splits
@@ -546,10 +544,8 @@
 
     @pl.when(step == 0)
     def first():
-        order[...] = chosen(
-            (width, width), split_order(ints[0], splits, width // devices)(width)
-        )
-        order_hidden[...] = chosen((chunk, chunk), split_order(ints[0], splits, hidden_unit)(chunk))
+        order[...] = chosen((width, width), scatter_order(groups, splits, width // devices))
+        order_hidden[...] = chosen((chunk, chunk), scatter_order(groups, splits, hidden_unit))
         each = width // groups // heads
         for g in range(groups):
             for head in range(heads):
@@ -563,10 +559,22 @@
         normed_t[...] = dot_nt(order[...], normed[...]).astype(BF16)
         d_normed[...] = jnp.zeros_like(d_normed)
 
-    def stored(outs, rows, values):
-        part = values.shape[0] // splits
-        for other in range(splits):
-            outs[other][:, rows] = values[part * other : part * (other + 1)].astype(BF16)
+    place = lax.rem(step, 2)
+    tall = down.shape[1]
+
+    def wide_copy(slot, index):
+        columns = pl.ds(pl.multiple_of(index * 2 * chunk, 2 * chunk), 2 * chunk)
+        return pltpu.make_async_copy(wide.at[slot], grads.at[:, columns], sems.at[0, slot])
+
+    def down_copy(slot, index):
+        rows = pl.ds(pl.multiple_of(index * tall, tall), tall)
+        columns = pl.ds(grads.shape[1] - down.shape[2], down.shape[2])
+        return pltpu.make_async_copy(down.at[slot], grads.at[rows, columns], sems.at[1, slot])
+
+    @pl.when(step >= 2)
+    def _():
+        wide_copy(place, step - 2).wait()
+        down_copy(place, step - 2).wait()
 
     @pl.when(step < chunks)
     def work():
@@ -588,14 +596,12 @@
         d_normed[...] += dot_nt(d_gate, w_gate[...]) + dot_nt(d_up, w_up[...])
         hidden_t = dot_nt(order_hidden[...], hidden).astype(BF16)
 
-        down = dot_nn(hidden_t, upstream[...])
-        part = chunk // splits
-        for other in range(splits):
-            grads_down[other][...] = packed_rows(
-                down[part * other : part * (other + 1)], hidden_unit, width // devices
-            ).astype(BF16)
-        stored(grads_wide, slice(0, chunk), dot_nn(normed_t[...], d_gate))
-        stored(grads_wide, slice(chunk, 2 * chunk), dot_nn(normed_t[...], d_up))
+        d_down = dot_nn(hidden_t, upstream[...])
+        down[place] = packed_rows(d_down, hidden_unit, width // devices).astype(BF16)
+        wide[place, :, :chunk] = dot_nn(normed_t[...], d_gate).astype(BF16)
+        wide[place, :, chunk:] = dot_nn(normed_t[...], d_up).astype(BF16)
+        wide_copy(place, step).start()
+        down_copy(place, step).start()
 
     @pl.when(step == chunks)
     def finish():
@@ -610,9 +616,12 @@
             d_first[g] = d_context[size * g : size * g + each]
             d_rest[g] = d_context[size * g + each : size * (g + 1)]
         ordered = dot_nn(order[...], context_t[...]).astype(BF16)
-        stored(grads_wide, slice(0, width), dot_nn(ordered, branch))
-        for out in grads_wide:
-            out[:, width:] = jnp.zeros((out.shape[0], out.shape[1] - width), BF16)
+        wide[place, :, :width] = dot_nn(ordered, branch).astype(BF16)
+        wide[place, :, width:] = jnp.zeros((width, 2 * chunk - width), BF16)
+        wide_copy(place, step).start()
+        wide_copy(1 - place, step - 1).wait()
+        down_copy(1 - place, step - 1).wait()
+        wide_copy(place, step).wait()
 
 
 def feed_forward(dims, ints, tokens, contexts, gains, late, upstream):
@@ -645,21 +654,14 @@
             full(groups, each, rows),
             full(groups, width // groups - each, rows),
         ]
-        + [pl.BlockSpec((width // splits, 2 * chunk), lambda step: (0, step))] * splits
-        + [
-            pl.BlockSpec(
-                (width // splits // steps, hidden), lambda step: (jnp.minimum(step, steps - 1), 0)
-            )
-        ]
-        * splits,
+        + [pl.BlockSpec(memory_space=pl.ANY)],
         out_shape=[
             jax.ShapeDtypeStruct((rows, width), BF16),
             jax.ShapeDtypeStruct((rows, width), F32),
             jax.ShapeDtypeStruct((groups, each, rows), BF16),
             jax.ShapeDtypeStruct((groups, width // groups - each, rows), BF16),
         ]
-        + [jax.ShapeDtypeStruct((width // splits, 2 * hidden + 2 * chunk), BF16)] * splits
-        + [jax.ShapeDtypeStruct((width // splits, hidden), BF16)] * splits,
+        + [jax.ShapeDtypeStruct((width, 3 * hidden + 2 * chunk), BF16)],
         scratch_shapes=[
             pltpu.VMEM((width, rows), BF16),
             pltpu.VMEM((rows, width), F32),
@@ -669,6 +671,9 @@
             pltpu.VMEM((rows, width), F32),
             pltpu.VMEM((width, width), BF16),
             pltpu.VMEM((chunk, chunk), BF16),
+            pltpu.VMEM((2, width, 2 * chunk), BF16),
+            pltpu.VMEM((2, width // steps, hidden), BF16),
+            pltpu.SemaphoreType.DMA((2, 2)),
         ],
         compiler_params=pltpu.CompilerParams(vmem_limit_bytes=VMEM),
         cost_estimate=pl.CostEstimate(
@@ -741,31 +746,6 @@
         cost_estimate=pl.CostEstimate(flops=0, bytes_accessed=2**20, transcendentals=0),
         name="added",
     )(*pieces)
-
-
-def joined_kernel(count, *refs):
-    wide, down, out = refs[:count], refs[count : 2 * count], refs[-1]
-    columns = wide[0].shape[1]
-    for pieces, lanes in ((wide, slice(0, columns)), (down, slice(columns, out.shape[1]))):
-        total = pieces[0][...].astype(F32)
-        for piece in pieces[1:]:
-            total += piece[...].astype(F32)
-        out[:, lanes] = total.astype(BF16)
-
-
-def joined(wide, down):
-    rows, columns = wide[0].shape[0], wide[0].shape[1] + down[0].shape[1]
-    block = lambda size: pl.BlockSpec((rows // 4, size), lambda step: (step, 0))
-    return pl.pallas_call(
-        functools.partial(joined_kernel, len(wide)),
-        grid=(4,),
-        in_specs=[block(piece.shape[1]) for piece in (*wide, *down)],
-        out_specs=block(columns),
-        out_shape=jax.ShapeDtypeStruct((rows, columns), BF16),
-        compiler_params=pltpu.CompilerParams(vmem_limit_bytes=VMEM),
-        cost_estimate=pl.CostEstimate(flops=0, bytes_accessed=2**20, transcendentals=0),
-        name="joined",
-    )(*wide, *down)
 
 
 def unpacked(pieces, heads, size):
@@ -1087,24 +1067,17 @@
     outs = feed_forward(
         dims, ints, own, moved, gains, late, cotangent[0]
     )
-    result, d_mixed, d_first, d_rest = outs[:4]
-    grads_wide, grads_down = outs[4 : 4 + splits], outs[4 + splits :]
-
-    def by_split(grads):
-        return [grads[0]] + [ahead(grads[by], "split", splits - by) for by in range(1, splits)]
+    result, d_mixed, d_first, d_rest, held = outs
 
     d_first = swap_groups(d_first)
     d_rest = swap_groups(d_rest)
     d_contexts = [d_first[:, None], d_rest.reshape(groups, group_heads - 1, head_size, tok_rows)]
-    wide, down = by_split(grads_wide), by_split(grads_down)
-    wide[-1] = after(wide[-1], d_first)
-    held = joined(wide, down)
-    held = held.reshape(rows_apart, groups, -1, held.shape[-1])
-    row_sum = after(lax.psum_scatter(held, "batch", scatter_dimension=0))
-    grads_own = lax.psum_scatter(row_sum, "group", scatter_dimension=0)
+    row_sum = lax.psum_scatter(held, ("batch", "split"), scatter_dimension=0, tiled=True)
+    row_sum = after(row_sum)
+    grads_own = lax.psum_scatter(row_sum, "group", scatter_dimension=0, tiled=True)
 
     d_heads, d_received, d_tables = [], [], []
-    ready = [(held,), ()] + [(row_sum,)] * (group_heads - 2)
+    ready = [(), ()] + [(row_sum,)] * (group_heads - 2)
     for head in range(group_heads):
         outs = attend_back(
             head,

time: 410 us -> 399 us (0.973)
  Pallas kernels: 186 us -> 179 us
    pallas_call x1 -> x0, Pallas kernels: 7.03 us -> none  [joined(): pl.pallas_call(functools.partial(joined_kernel, len(wide)), grid=(4,), in...]
    all_to_all x6, waiting for transfers between devices: 12.9 us -> 8.13 us  [swap_groups(): return lax.all_to_all(array, 'group', 0, 0)]
    ppermute x17 -> x15, starting transfers between devices: 12.7 us -> 12.2 us  [ahead(): lax.ppermute(array, axis, [((i + by) % size, i) for i in range(size)])]
    ppermute x17 -> x15, waiting for transfers between devices: 19.1 us -> 19.1 us  [ahead(): lax.ppermute(array, axis, [((i + by) % size, i) for i in range(size)])]
  transfers between devices with their start and end apart: 33 -> 31, of which waited for: 17 -> 18; matrix products, arithmetic and copies ran while one was open for 3% -> 4% of each run, Pallas kernels for 37% -> 38%
where the time goes in v1:
time: 399 us; the launch traced here: 394 us
  Pallas kernels  179 us (45%)
  waiting for transfers between devices  83.1 us (21%)
  starting transfers between devices  59.1 us (15%)
  blocking collectives  28 us (7%)
  between operations  17.4 us (4%)
  other arithmetic  15.5 us (4%)
  local copies, waits for them, and re-layouts  11.6 us (3%)
    pallas_call x3, Pallas kernels, attend_back(): pl.pallas_call(functools.partial(backward_kernel, tokens, groups, splits)...  64.6 us
    ppermute x6, waiting for transfers between devices, line(): return lax.ppermute(array, 'group', pairs)  48.3 us
    pallas_call x3, Pallas kernels, attend(): pl.pallas_call(functools.partial(forward_kernel, tokens, groups, splits),...  48 us
    pallas_call x1, Pallas kernels, feed_forward(): pl.pallas_call(functools.partial(block_kernel, dims, len(contexts)), grid...  29.1 us
    all_to_all x6, starting transfers between devices, swap_groups(): return lax.all_to_all(array, 'group', 0, 0)  28.4 us
    all_to_all x2, blocking collectives, swap_groups(): return lax.all_to_all(array, 'group', 0, 0)  28 us
    ppermute x15, waiting for transfers between devices, ahead(): lax.ppermute(array, axis, [((i + by) % size, i) for i in range(size)])  19.1 us
    ppermute x6, starting transfers between devices, line(): return lax.ppermute(array, 'group', pairs)  18.3 us
  transfers between devices with their start and end apart: 31, of which 18 were waited for; matrix products, arithmetic and copies ran while one was open for 4% of the time, Pallas kernels for 38%

profile of v1, /device:TPU:0, one launch (start us, length us, event | category | flops | bytes accessed | tf_op | source)
XLA Modules:
  0.0 393.6 jit_solution(13919064299432013464)
XLA Ops:
  7.3 1.2 reshape.117
  9.2 0.7 copy.64
  10.0 5.0 %collective-permute-start = (bf16[512,768]{1,0:T(8,128)(2,1)S(1)}, bf16[512,768]{1,0:T(8,128)(2,1)S(1)}, u32[]{:S(2)}, u32[]{:S(2)}) collective-permute-start(bf16[512,768]{1,0:T(8,128)(2,1)S(1)} %bitcast.47), channel_id=1, source_target_pairs={{0,2},{2,4},{4,6},{1,3},{3,5},{5,7},{8,10},{10,12},{12,14},{9,11},... | collective-permute-start | bytes 2359304 | tf_op jit(solution)/shard_map/ppermute | solution.py:1003
  15.0 1.3 collective-permute-start.1
  16.3 0.7 pad_maximum_fusion
  17.1 17.3 %collective-permute-done.refs_0_ = bf16[512,768]{1,0:T(8,128)(2,1)S(1)} collective-permute-done((bf16[512,768]{1,0:T(8,128)(2,1)S(1)}, bf16[512,768]{1,0:T(8,128)(2,1)S(1)}, u32[]{:S(2)}, u32[]{:S(2)}) %collective-permute-start) | collective-permute-done | bytes 786464 | tf_op jit(solution)/shard_map/ppermute | solution.py:1003
  34.3 4.2 %collective-permute-done.1.refs_2_ = bf16[512,768]{1,0:T(8,128)(2,1)S(1)} collective-permute-done((bf16[512,768]{1,0:T(8,128)(2,1)S(1)}, bf16[512,768]{1,0:T(8,128)(2,1)S(1)}, u32[]{:S(2)}, u32[]{:S(2)}) %collective-permute-start.1) | collective-permute-done | bytes 786464 | tf_op jit(solution)/shard_map/ppermute | solution.py:1003
  38.5 4.3 %collective-permute-start.2 = (bf16[512,768]{1,0:T(8,128)(2,1)S(1)}, bf16[512,768]{1,0:T(8,128)(2,1)}, u32[]{:S(2)}, u32[]{:S(2)}) collective-permute-start(bf16[512,768]{1,0:T(8,128)(2,1)S(1)} %collective-permute-done.refs_0_), channel_id=1, source_target_pairs={{0,2},{2,4},{4,6},{1,3},{3,5},{5,7},{8,10},{10,12},{12,14},{9,11},... | collective-permute-start | bytes 2359304 | tf_op jit(solution)/shard_map/ppermute | solution.py:1003
  42.9 1.3 collective-permute-start.3
  44.2 22.3 %collective-permute-done.2.refs_1_ = bf16[512,768]{1,0:T(8,128)(2,1)} collective-permute-done((bf16[512,768]{1,0:T(8,128)(2,1)S(1)}, bf16[512,768]{1,0:T(8,128)(2,1)}, u32[]{:S(2)}, u32[]{:S(2)}) %collective-permute-start.2) | collective-permute-done | bytes 786464 | tf_op jit(solution)/shard_map/ppermute | solution.py:1003
  66.5 5.1 %collective-permute-start.4 = (bf16[512,768]{1,0:T(8,128)(2,1)}, bf16[512,768]{1,0:T(8,128)(2,1)S(1)}, u32[]{:S(2)}, u32[]{:S(2)}) collective-permute-start(bf16[512,768]{1,0:T(8,128)(2,1)} %collective-permute-done.2.refs_1_), channel_id=1, source_target_pairs={{0,2},{2,4},{4,6},{1,3},{3,5},{5,7},{8,10},{10,12},{12,14},{9,11},... | collective-permute-start | bytes 2359304 | tf_op jit(solution)/shard_map/ppermute | solution.py:1003
  71.6 2.3 collective-permute-done.3.refs_3_
  73.9 1.3 collective-permute-start.5
  76.0 3.2 all-gather.5.cloned.1.call-done.weights
  79.1 12.1 %project.1 = (bf16[768,2048]{1,0:T(8,128)(2,1)}, bf16[2048,384]{1,0:T(8,128)(2,1)}, bf16[2048,384]{1,0:T(8,128)(2,1)}, f32[8,768]{1,0:T(8,128)}, bf16[768,768]{1,0:T(8,128)(2,1)}) custom-call(s32[7]{0:T(128)} %concatenate.24.ints, bf16[768,2560]{1,0:T(8,128)(2,1)} %all-gather.5.cloned.1.call-done.weights, bf16[512,768]{1,0:T(8,128)(2,1)} %bitcast.43, ...), custom_call_target="tpu_custom_call" | custom-call | flops 4831838208 | bytes 12582912 | tf_op jit(solution)/shard_map/project/pallas_call | solution.py:398
  91.3 2.2 collective-permute-done.5.behind
  93.5 0.9 copy-done.10
  94.4 5.8 %project_last.1 = (bf16[768,2048]{1,0:T(8,128)(2,1)}, bf16[2048,384]{1,0:T(8,128)(2,1)}, bf16[2048,384]{1,0:T(8,128)(2,1)}) custom-call(s32[7]{0:T(128)} %concatenate.24.ints, bf16[768,2560]{1,0:T(8,128)(2,1)} %all-gather.5.cloned.1.call-done.weights, bf16[512,768]{1,0:T(8,128)(2,1)} %bitcast.44, ...), custom_call_target="tpu_custom_call", output_to_operand_aliasing={{0}: (7, {}), {1}: (8, {}), {2}: (9, {})} | custom-call | flops 1207959552 | bytes 3145728 | tf_op jit(solution)/shard_map/project_last/pallas_call | solution.py:452
  100.7 3.1 collective-permute-done.6.refs_1_
  103.8 1.2 copy-done.35
  104.9 16.0 %attend.3 = (bf16[16384,512]{1,0:T(8,128)(2,1)}, bf16[4,64,512]{2,1,0:T(8,128)(2,1)}, f32[4,80,512]{2,1,0:T(8,128)}) custom-call(s32[7]{0:T(128)} %concatenate.24.ints, f32[1,32]{1,0:T(1,128)} %get-tuple-element.190.table, bf16[2048,384]{1,0:T(8,128)(2,1)} %get-tuple-element.82.query, bf16[2048,384]{1,0:T(8,128)(2,1)} %get-tuple-element.83.refs_0_, ...), custom_call_target="tpu_custom_call" | custom-call | flops 8589934592 | bytes 16777216 | tf_op jit(solution)/shard_map/attend/pallas_call | solution.py:878
  120.9 3.6 all-to-all-start
  124.6 16.0 %attend.4 = (bf16[16384,512]{1,0:T(8,128)(2,1)}, bf16[4,64,512]{2,1,0:T(8,128)(2,1)}, f32[4,80,512]{2,1,0:T(8,128)}) custom-call(s32[7]{0:T(128)} %concatenate.24.ints, f32[1,32]{1,0:T(1,128)} %get-tuple-element.189.table, bf16[2048,384]{1,0:T(8,128)(2,1)} %get-tuple-element.82.query, bf16[2048,384]{1,0:T(8,128)(2,1)} %get-tuple-element.83.refs_0_, ...), custom_call_target="tpu_custom_call" | custom-call | flops 8589934592 | bytes 16777216 | tf_op jit(solution)/shard_map/attend/pallas_call | solution.py:878
  140.6 5.1 %all-to-all-start.1 = ((bf16[4,64,512]{2,1,0:T(8,128)(2,1)}), bf16[4,64,512]{2,1,0:T(8,128)(2,1)S(1)}, u32[]{:S(2)}, u32[]{:S(2)}) async-start(bf16[4,64,512]{2,1,0:T(8,128)(2,1)} %get-tuple-element.87), calls=%async_computation.1 | async-start | bytes 524288 | tf_op jit(solution)/shard_map/all_to_all | solution.py:996
  145.7 16.0 %attend.5 = (bf16[16384,512]{1,0:T(8,128)(2,1)}, bf16[4,64,512]{2,1,0:T(8,128)(2,1)}, f32[4,80,512]{2,1,0:T(8,128)}) custom-call(s32[7]{0:T(128)} %concatenate.24.ints, f32[1,32]{1,0:T(1,128)} %get-tuple-element.188.table, bf16[2048,384]{1,0:T(8,128)(2,1)} %get-tuple-element.82.query, bf16[2048,384]{1,0:T(8,128)(2,1)} %get-tuple-element.83.refs_0_, ...), custom_call_target="tpu_custom_call" | custom-call | flops 8589934592 | bytes 16777216 | tf_op jit(solution)/shard_map/attend/pallas_call | solution.py:878
  162.1 15.4 %all_to_all.40.refs_2_ = bf16[4,64,512]{2,1,0:T(8,128)(2,1)} all-to-all(bf16[4,64,512]{2,1,0:T(8,128)(2,1)} %get-tuple-element.90), channel_id=1, replica_groups=mesh['batch'=4,'group'=4,'split'=2] {'group'}, dimensions={0} | all-to-all | bytes 524288 | tf_op jit(solution)/shard_map/all_to_all | solution.py:996
  177.4 0.7 all-gather.3.cloned.1.call-done.w_out.w_gate.w_up.w_packed
  178.1 29.1 %feed_forward.1 = (bf16[512,768]{1,0:T(8,128)(2,1)}, f32[512,768]{1,0:T(8,128)}, bf16[4,64,512]{2,1,0:T(8,128)(2,1)}, bf16[4,128,512]{2,1,0:T(8,128)(2,1)}, bf16[768,7168]{1,0:T(8,128)(2,1)}) custom-call(s32[7]{0:T(128)} %concatenate.24.ints, bf16[512,768]{1,0:T(8,128)(2,1)} %bitcast.45, ...), custom_call_target="tpu_custom_call" | custom-call | flops 16307453952 | bytes 18874368 | tf_op jit(solution)/shard_map/feed_forward/pallas_call | solution.py:635
  207.2 0.9 copy-done.17
  208.2 12.6 %all_to_all.41 = bf16[4,64,512]{2,1,0:T(8,128)(2,1)} all-to-all(bf16[4,64,512]{2,1,0:T(8,128)(2,1)S(1)} %copy-done.17), channel_id=1, replica_groups=mesh['batch'=4,'group'=4,'split'=2] {'group'}, dimensions={0} | all-to-all | bytes 524288 | tf_op jit(solution)/shard_map/all_to_all | solution.py:996
  220.8 3.7 all-to-all-start.4
  224.5 21.6 %attend_back.3 = (bf16[4,192,512]{2,1,0:T(8,128)(2,1)}, bf16[4,128,512]{2,1,0:T(8,128)(2,1)}, f32[32,128]{1,0:T(8,128)}) custom-call(s32[7]{0:T(128)} %concatenate.24.ints, bf16[2048,384]{1,0:T(8,128)(2,1)} %get-tuple-element.82.query, bf16[4,1,64,512]{3,2,1,0:T(8,128)(2,1)} %bitcast.56, f32[4,80,512]{2,1,0:T(8,128)} %get-tuple-element.94.stats, ...), custom_call_target="tpu_custom_call" | custom-call | flops 17179869184 | bytes 16777216 | tf_op jit(solution)/shard_map/attend_back/pallas_call | solution.py:915
  246.1 2.1 collective-permute-done.7
  248.3 2.2 add_convert_fusion.2.refs_0_
  250.4 5.0 %all-to-all-start.5 = ((bf16[4,192,512]{2,1,0:T(8,128)(2,1)}), bf16[4,192,512]{2,1,0:T(8,128)(2,1)S(1)}, u32[]{:S(2)}, u32[]{:S(2)}) async-start(bf16[4,192,512]{2,1,0:T(8,128)(2,1)} %add_convert_fusion.2.refs_0_), calls=%async_computation.5 | async-start | bytes 1572864 | tf_op jit(solution)/shard_map/all_to_all | solution.py:996
  255.4 21.5 %attend_back.4 = (bf16[4,192,512]{2,1,0:T(8,128)(2,1)}, bf16[4,128,512]{2,1,0:T(8,128)(2,1)}, f32[32,128]{1,0:T(8,128)}) custom-call(s32[7]{0:T(128)} %concatenate.24.ints, bf16[2048,384]{1,0:T(8,128)(2,1)} %get-tuple-element.82.query, bf16[4,2,64,512]{3,2,1,0:T(8,128)(2,1)} %bitcast.52, f32[4,80,512]{2,1,0:T(8,128)} %get-tuple-element.103.stats, ...), custom_call_target="tpu_custom_call" | custom-call | flops 17179869184 | bytes 16777216 | tf_op jit(solution)/shard_map/attend_back/pallas_call | solution.py:915
  277.0 2.1 collective-permute-done.8
  279.1 2.2 add_convert_fusion.1.refs_1_
  281.3 5.1 %all-to-all-start.6 = ((bf16[4,192,512]{2,1,0:T(8,128)(2,1)}), bf16[4,192,512]{2,1,0:T(8,128)(2,1)S(1)}, u32[]{:S(2)}, u32[]{:S(2)}) async-start(bf16[4,192,512]{2,1,0:T(8,128)(2,1)} %add_convert_fusion.1.refs_1_), calls=%async_computation.6 | async-start | bytes 1572864 | tf_op jit(solution)/shard_map/all_to_all | solution.py:996
  286.6 3.6 reduce-scatter.3.cloned.1.call-done
  290.2 21.5 %attend_back.5 = (bf16[4,192,512]{2,1,0:T(8,128)(2,1)}, bf16[4,128,512]{2,1,0:T(8,128)(2,1)}, f32[32,128]{1,0:T(8,128)}) custom-call(s32[7]{0:T(128)} %concatenate.24.ints, bf16[2048,384]{1,0:T(8,128)(2,1)} %get-tuple-element.82.query, bf16[4,2,64,512]{3,2,1,0:T(8,128)(2,1)} %bitcast.53, f32[4,80,512]{2,1,0:T(8,128)} %get-tuple-element.112.stats, ...), custom_call_target="tpu_custom_call" | custom-call | flops 17179869184 | bytes 16777216 | tf_op jit(solution)/shard_map/attend_back/pallas_call | solution.py:915
  311.8 2.1 collective-permute-done.9
  313.9 2.2 add_convert_fusion.refs_2_
  316.1 2.1 all-to-all-done.6.refs_1_
  318.2 5.9 %all-to-all-start.7 = ((bf16[4,192,512]{2,1,0:T(8,128)(2,1)}), bf16[4,192,512]{2,1,0:T(8,128)(2,1)S(1)}, u32[]{:S(2)}, u32[]{:S(2)}) async-start(bf16[4,192,512]{2,1,0:T(8,128)(2,1)} %add_convert_fusion.refs_2_), calls=%async_computation.8 | async-start | bytes 1572864 | tf_op jit(solution)/shard_map/all_to_all | solution.py:996
  324.1 6.8 %weight_grads.1 = (bf16[384,576]{1,0:T(8,128)(2,1)}, bf16[384,576]{1,0:T(8,128)(2,1)}) custom-call(bf16[768,2048]{1,0:T(8,128)(2,1)} %get-tuple-element.117.normed_t, bf16[4,192,512]{2,1,0:T(8,128)(2,1)} %add_convert_fusion.2.refs_0_, bf16[4,192,512]{2,1,0:T(8,128)(2,1)} %add_convert_fusion.1.refs_1_, bf16[4,192,512]{2,1,0:T(8,128)(2,1)} %add_convert_fusion.refs_2_), custom_call_target="tpu_custom_call" | custom-call | flops 1811939328 | bytes 3145728 | tf_op jit(solution)/shard_map/weight_grads/pallas_call | solution.py:712
  330.9 2.1 collective-permute-done.10.refs_1_
  333.0 0.8 copy-done.13
  333.8 2.0 added.1
  335.8 1.5 collective-permute-start.11
  337.2 1.5 collective-permute-start.12
  338.7 1.5 collective-permute-start.13
  340.2 5.6 %all-to-all-done.7.refs_2_ = bf16[4,192,512]{2,1,0:T(8,128)(2,1)S(1)} async-done(((bf16[4,192,512]{2,1,0:T(8,128)(2,1)}), bf16[4,192,512]{2,1,0:T(8,128)(2,1)S(1)}, u32[]{:S(2)}, u32[]{:S(2)}) %all-to-all-start.7) | async-done | bytes 786464 | tf_op jit(solution)/shard_map/all_to_all | solution.py:996
  345.8 0.6 copy-done.19
  346.5 2.2 counted.1
  348.7 2.4 collective-permute-start.14
  352.2 1.0 slice.253
  354.7 0.7 multiply_reduce_fusion.5
  355.7 0.7 copy.58
  356.4 8.5 %input_grads.1 = bf16[512,768]{1,0:T(8,128)(2,1)} custom-call(bf16[768,2560]{1,0:T(8,128)(2,1)} %all-gather.5.cloned.1.call-done.weights, bf16[512,768]{1,0:T(8,128)(2,1)} %bitcast.46, f32[8,768]{1,0:T(8,128)} %get-tuple-element.77.gains, f32[512,768]{1,0:T(8,128)} %get-tuple-element.92.d_mixed, bf16[4,192,512]{2,1,0:T(8,128)(2,1)} %copy-done.3, ...), custom_call_target="tpu_custom_call" | custom-call | tf_op jit(solution)/shard_map/input_grads/pallas_call | solution.py:848
  365.0 2.8 collective-permute-start.17
  367.9 1.2 collective-permute-start.19
  369.1 2.1 collective-permute-done.17
  371.2 5.6 %collective-permute-done.18 = f32[40,640]{1,0:T(8,128)S(1)} collective-permute-done((f32[40,640]{1,0:T(8,128)S(1)}, f32[40,640]{1,0:T(8,128)S(1)}, u32[]{:S(2)}, u32[]{:S(2)}) %collective-permute-start.18) | collective-permute-done | bytes 102432 | tf_op jit(solution)/shard_map/ppermute | solution.py:993
  (164 shorter events, 13.4 us)
Async XLA Ops:
  7.2 93.0 %copy-start = (f32[32,12]{0,1:T(8,128)S(1)}, f32[32,12]{0,1:T(8,128)}, u32[]{:S(2)}) copy-start(f32[32,12]{0,1:T(8,128)} %param.22) | copy-start | bytes 4612
  7.2 1.8 copy-start.40
  7.2 2.8 copy-start.2
  7.2 9.0 %copy-start.22 = (bf16[64,768]{1,0:T(8,128)(2,1)S(1)}, bf16[64,768]{1,0:T(8,128)(2,1)}, u32[]{:S(2)}) copy-start(bf16[64,768]{1,0:T(8,128)(2,1)} %param.26) | copy-start | bytes 294916
  7.2 9.1 %copy-start.27 = (bf16[24,768]{1,0:T(8,128)(2,1)S(1)}, bf16[24,768]{1,0:T(8,128)(2,1)}, u32[]{:S(2)}) copy-start(bf16[24,768]{1,0:T(8,128)(2,1)} %param.23) | copy-start | bytes 110596
  7.3 9.1 %copy-start.11 = (bf16[24,4096]{1,0:T(8,128)(2,1)S(1)}, bf16[24,4096]{1,0:T(8,128)(2,1)}, u32[]{:S(2)}) copy-start(bf16[24,4096]{1,0:T(8,128)(2,1)} %param.25) | copy-start | bytes 589828
  7.3 71.9 %all-gather.5.cloned.1.call-start = ((), (), s32[]{:S(2)}) async-start(), calls=%async_computation.11 | async-start | bytes 4055040 | tf_op jit(solution)/shard_map/all_gather | solution.py:1021
  8.5 66.7 %copy-start.38 = (s32[1,3]{1,0:T(1,128)S(1)}, s32[1,3]{1,0:T(1,128)}, u32[]{:S(2)}) copy-start(s32[1,3]{1,0:T(1,128)} %param.19) | copy-start | bytes 40
  9.9 168.2 %all-gather.3.cloned.1.call-start = ((), (), s32[]{:S(2)}) async-start(), calls=%async_computation.10 | async-start | bytes 10948608 | tf_op jit(solution)/shard_map/all_gather | solution.py:1025
  10.0 24.4 %collective-permute-start = (bf16[512,768]{1,0:T(8,128)(2,1)S(1)}, bf16[512,768]{1,0:T(8,128)(2,1)S(1)}, u32[]{:S(2)}, u32[]{:S(2)}) collective-permute-start(bf16[512,768]{1,0:T(8,128)(2,1)S(1)} %bitcast.47), channel_id=1, source_target_pairs={{0,2},{2,4},{4,6},{1,3},{3,5},{5,7},{8,10},{10,12},{12,14},{9,11},... | collective-permute-start | bytes 2359304 | tf_op jit(solution)/shard_map/ppermute | solution.py:1003
  15.0 23.5 %collective-permute-start.1 = (bf16[512,768]{1,0:T(8,128)(2,1)S(1)}, bf16[512,768]{1,0:T(8,128)(2,1)S(1)}, u32[]{:S(2)}, u32[]{:S(2)}) collective-permute-start(bf16[512,768]{1,0:T(8,128)(2,1)S(1)} %bitcast.48), channel_id=1, source_target_pairs={{2,0},{4,2},{6,4},{3,1},{5,3},{7,5},{10,8},{12,10},{14,12},{11,9},... | collective-permute-start | bytes 2359304 | tf_op jit(solution)/shard_map/ppermute | solution.py:1003
  34.3 44.8 %copy-start.36 = (bf16[512,768]{1,0:T(8,128)(2,1)}, bf16[512,768]{1,0:T(8,128)(2,1)S(1)}, u32[]{:S(2)}) copy-start(bf16[512,768]{1,0:T(8,128)(2,1)S(1)} %collective-permute-done.refs_0_) | copy-start | bytes 2359300
  38.5 40.6 %copy-start.37 = (bf16[512,768]{1,0:T(8,128)(2,1)}, bf16[512,768]{1,0:T(8,128)(2,1)S(1)}, u32[]{:S(2)}) copy-start(bf16[512,768]{1,0:T(8,128)(2,1)S(1)} %collective-permute-done.1.refs_2_) | copy-start | bytes 2359300
  38.5 27.9 %collective-permute-start.2 = (bf16[512,768]{1,0:T(8,128)(2,1)S(1)}, bf16[512,768]{1,0:T(8,128)(2,1)}, u32[]{:S(2)}, u32[]{:S(2)}) collective-permute-start(bf16[512,768]{1,0:T(8,128)(2,1)S(1)} %collective-permute-done.refs_0_), channel_id=1, source_target_pairs={{0,2},{2,4},{4,6},{1,3},{3,5},{5,7},{8,10},{10,12},{12,14},{9,11},... | collective-permute-start | bytes 2359304 | tf_op jit(solution)/shard_map/ppermute | solution.py:1003
  42.9 31.0 %collective-permute-start.3 = (bf16[512,768]{1,0:T(8,128)(2,1)S(1)}, bf16[512,768]{1,0:T(8,128)(2,1)}, u32[]{:S(2)}, u32[]{:S(2)}) collective-permute-start(bf16[512,768]{1,0:T(8,128)(2,1)S(1)} %collective-permute-done.1.refs_2_), channel_id=1, source_target_pairs={{2,0},{4,2},{6,4},{3,1},{5,3},{7,5},{10,8},{12,10},{14,12},{11,9},... | collective-permute-start | bytes 2359304 | tf_op jit(solution)/shard_map/ppermute | solution.py:1003
  66.5 24.8 %collective-permute-start.4 = (bf16[512,768]{1,0:T(8,128)(2,1)}, bf16[512,768]{1,0:T(8,128)(2,1)S(1)}, u32[]{:S(2)}, u32[]{:S(2)}) collective-permute-start(bf16[512,768]{1,0:T(8,128)(2,1)} %collective-permute-done.2.refs_1_), channel_id=1, source_target_pairs={{0,2},{2,4},{4,6},{1,3},{3,5},{5,7},{8,10},{10,12},{12,14},{9,11},... | collective-permute-start | bytes 2359304 | tf_op jit(solution)/shard_map/ppermute | solution.py:1003
  73.9 19.6 %collective-permute-start.5 = (bf16[512,768]{1,0:T(8,128)(2,1)}, bf16[512,768]{1,0:T(8,128)(2,1)S(1)}, u32[]{:S(2)}, u32[]{:S(2)}) collective-permute-start(bf16[512,768]{1,0:T(8,128)(2,1)} %collective-permute-done.3.refs_3_), channel_id=1, source_target_pairs={{2,0},{4,2},{6,4},{3,1},{5,3},{7,5},{10,8},{12,10},{14,12},{11,9},... | collective-permute-start | bytes 2359304 | tf_op jit(solution)/shard_map/ppermute | solution.py:1003
  91.3 2.2 copy-start.9
  100.2 3.6 collective-permute-start.6
  120.9 19.7 %all-to-all-start = ((bf16[4,64,512]{2,1,0:T(8,128)(2,1)}), bf16[4,64,512]{2,1,0:T(8,128)(2,1)S(1)}, u32[]{:S(2)}, u32[]{:S(2)}) async-start(bf16[4,64,512]{2,1,0:T(8,128)(2,1)} %get-tuple-element.84), calls=%async_computation | async-start | bytes 524288 | tf_op jit(solution)/shard_map/all_to_all | solution.py:996
  140.6 21.1 %copy-start.15 = (bf16[4,64,512]{2,1,0:T(8,128)(2,1)}, bf16[4,64,512]{2,1,0:T(8,128)(2,1)S(1)}, u32[]{:S(2)}) copy-start(bf16[4,64,512]{2,1,0:T(8,128)(2,1)S(1)} %all-to-all-done.refs_0_) | copy-start | bytes 786436
  140.6 21.5 %all-to-all-start.1 = ((bf16[4,64,512]{2,1,0:T(8,128)(2,1)}), bf16[4,64,512]{2,1,0:T(8,128)(2,1)S(1)}, u32[]{:S(2)}, u32[]{:S(2)}) async-start(bf16[4,64,512]{2,1,0:T(8,128)(2,1)} %get-tuple-element.87), calls=%async_computation.1 | async-start | bytes 524288 | tf_op jit(solution)/shard_map/all_to_all | solution.py:996
  145.7 144.5 %reduce-scatter.3.cloned.1.call-start = ((), (), s32[]{:S(2)}) async-start(), calls=%async_computation.12 | async-start | bytes 12386304 | tf_op jit(solution)/shard_map/reduce_scatter | solution.py:1075
  162.1 16.1 %copy-start.16 = (bf16[4,64,512]{2,1,0:T(8,128)(2,1)}, bf16[4,64,512]{2,1,0:T(8,128)(2,1)S(1)}, u32[]{:S(2)}) copy-start(bf16[4,64,512]{2,1,0:T(8,128)(2,1)S(1)} %all-to-all-done.1.refs_1_) | copy-start | bytes 786436
  220.8 25.3 %all-to-all-start.4 = ((bf16[4,128,512]{2,1,0:T(8,128)(2,1)}), bf16[4,128,512]{2,1,0:T(8,128)(2,1)S(1)}, u32[]{:S(2)}, u32[]{:S(2)}) async-start(bf16[4,128,512]{2,1,0:T(8,128)(2,1)} %get-tuple-element.99), calls=%async_computation.4 | async-start | bytes 1048576 | tf_op jit(solution)/shard_map/all_to_all | solution.py:996
  246.1 4.4 %copy-start.12 = (bf16[4,128,512]{2,1,0:T(8,128)(2,1)}, bf16[4,128,512]{2,1,0:T(8,128)(2,1)S(1)}, u32[]{:S(2)}) copy-start(bf16[4,128,512]{2,1,0:T(8,128)(2,1)S(1)} %all-to-all-done.4) | copy-start | bytes 1572868
  246.1 2.2 collective-permute-start.7
  250.4 26.5 %all-to-all-start.5 = ((bf16[4,192,512]{2,1,0:T(8,128)(2,1)}), bf16[4,192,512]{2,1,0:T(8,128)(2,1)S(1)}, u32[]{:S(2)}, u32[]{:S(2)}) async-start(bf16[4,192,512]{2,1,0:T(8,128)(2,1)} %add_convert_fusion.2.refs_0_), calls=%async_computation.5 | async-start | bytes 1572864 | tf_op jit(solution)/shard_map/all_to_all | solution.py:996
  276.9 4.4 %copy-start.3 = (bf16[4,192,512]{2,1,0:T(8,128)(2,1)}, bf16[4,192,512]{2,1,0:T(8,128)(2,1)S(1)}, u32[]{:S(2)}) copy-start(bf16[4,192,512]{2,1,0:T(8,128)(2,1)S(1)} %all-to-all-done.5.refs_0_) | copy-start | bytes 2359300
  276.9 2.2 collective-permute-start.8
  281.3 36.9 %all-to-all-start.6 = ((bf16[4,192,512]{2,1,0:T(8,128)(2,1)}), bf16[4,192,512]{2,1,0:T(8,128)(2,1)S(1)}, u32[]{:S(2)}, u32[]{:S(2)}) async-start(bf16[4,192,512]{2,1,0:T(8,128)(2,1)} %add_convert_fusion.1.refs_1_), calls=%async_computation.6 | async-start | bytes 1572864 | tf_op jit(solution)/shard_map/all_to_all | solution.py:996
  286.4 59.5 %reduce-scatter.5.cloned.1.call-start = ((), (), s32[]{:S(2)}) async-start(), calls=%async_computation.13 | async-start | bytes 1720320 | tf_op jit(solution)/shard_map/reduce_scatter | solution.py:1077
  311.8 2.1 collective-permute-start.9
  318.2 12.7 %copy-start.4 = (bf16[4,192,512]{2,1,0:T(8,128)(2,1)}, bf16[4,192,512]{2,1,0:T(8,128)(2,1)S(1)}, u32[]{:S(2)}) copy-start(bf16[4,192,512]{2,1,0:T(8,128)(2,1)S(1)} %all-to-all-done.6.refs_1_) | copy-start | bytes 2359300
  318.2 27.5 %all-to-all-start.7 = ((bf16[4,192,512]{2,1,0:T(8,128)(2,1)}), bf16[4,192,512]{2,1,0:T(8,128)(2,1)S(1)}, u32[]{:S(2)}, u32[]{:S(2)}) async-start(bf16[4,192,512]{2,1,0:T(8,128)(2,1)} %add_convert_fusion.refs_2_), calls=%async_computation.8 | async-start | bytes 1572864 | tf_op jit(solution)/shard_map/all_to_all | solution.py:996
  330.9 2.1 collective-permute-start.10
  335.8 10.0 %collective-permute-start.11 = (bf16[96,576]{1,0:T(8,128)(2,1)}, bf16[96,576]{1,0:T(8,128)(2,1)S(1)}, u32[]{:S(2)}, u32[]{:S(2)}) collective-permute-start(bf16[96,576]{1,0:T(8,128)(2,1)} %get-tuple-element.122), channel_id=1, source_target_pairs={{24,0},{0,8},{8,16},{16,24},{25,1},{1,9},{9,17},{17,25},{26,2},{2,... | collective-permute-start | bytes 331784 | tf_op jit(solution)/shard_map/ppermute | solution.py:993
  337.2 8.5 %collective-permute-start.12 = (bf16[96,576]{1,0:T(8,128)(2,1)}, bf16[96,576]{1,0:T(8,128)(2,1)S(1)}, u32[]{:S(2)}, u32[]{:S(2)}) collective-permute-start(bf16[96,576]{1,0:T(8,128)(2,1)} %get-tuple-element.123), channel_id=1, source_target_pairs={{16,0},{24,8},{0,16},{8,24},{17,1},{25,9},{1,17},{9,25},{18,2},{26... | collective-permute-start | bytes 331784 | tf_op jit(solution)/shard_map/ppermute | solution.py:993
  338.7 7.1 %collective-permute-start.13 = (bf16[96,576]{1,0:T(8,128)(2,1)}, bf16[96,576]{1,0:T(8,128)(2,1)S(1)}, u32[]{:S(2)}, u32[]{:S(2)}) collective-permute-start(bf16[96,576]{1,0:T(8,128)(2,1)} %get-tuple-element.124), channel_id=1, source_target_pairs={{8,0},{16,8},{24,16},{0,24},{9,1},{17,9},{25,17},{1,25},{10,2},{18... | collective-permute-start | bytes 331784 | tf_op jit(solution)/shard_map/ppermute | solution.py:993
  345.8 7.9 %copy-start.5 = (bf16[4,192,512]{2,1,0:T(8,128)(2,1)}, bf16[4,192,512]{2,1,0:T(8,128)(2,1)S(1)}, u32[]{:S(2)}) copy-start(bf16[4,192,512]{2,1,0:T(8,128)(2,1)S(1)} %all-to-all-done.7.refs_2_) | copy-start | bytes 2359300
  348.7 16.2 %collective-permute-start.14 = (f32[16,640]{1,0:T(8,128)}, f32[16,640]{1,0:T(8,128)S(1)}, u32[]{:S(2)}, u32[]{:S(2)}) collective-permute-start(f32[16,640]{1,0:T(8,128)} %get-tuple-element.128), channel_id=1, source_target_pairs={{8,0},{16,8},{24,16},{0,24},{9,1},{17,9},{25,17},{1,25},{10,2},{18... | collective-permute-start | bytes 122888 | tf_op jit(solution)/shard_map/ppermute | solution.py:993
  351.2 13.8 %collective-permute-start.15 = (f32[16,640]{1,0:T(8,128)}, f32[16,640]{1,0:T(8,128)S(1)}, u32[]{:S(2)}, u32[]{:S(2)}) collective-permute-start(f32[16,640]{1,0:T(8,128)} %get-tuple-element.128), channel_id=1, source_target_pairs={{16,0},{24,8},{0,16},{8,24},{17,1},{25,9},{1,17},{9,25},{18,2},{26... | collective-permute-start | bytes 122888 | tf_op jit(solution)/shard_map/ppermute | solution.py:993
  351.7 13.2 %collective-permute-start.16 = (f32[16,640]{1,0:T(8,128)}, f32[16,640]{1,0:T(8,128)S(1)}, u32[]{:S(2)}, u32[]{:S(2)}) collective-permute-start(f32[16,640]{1,0:T(8,128)} %get-tuple-element.128), channel_id=1, source_target_pairs={{24,0},{0,8},{8,16},{16,24},{25,1},{1,9},{9,17},{17,25},{26,2},{2,... | collective-permute-start | bytes 122888 | tf_op jit(solution)/shard_map/ppermute | solution.py:993
  353.9 11.0 %copy-start.7 = (f32[24,4096]{1,0:T(8,128)}, f32[24,4096]{1,0:T(8,128)S(1)}, u32[]{:S(2)}) copy-start(f32[24,4096]{1,0:T(8,128)S(1)} %reshape.122) | copy-start | bytes 1179652
  356.4 8.5 %copy-start.26 = (f32[16,640]{1,0:T(8,128)S(1)}, f32[16,640]{1,0:T(8,128)}, u32[]{:S(2)}) copy-start(f32[16,640]{1,0:T(8,128)} %get-tuple-element.128) | copy-start | bytes 122884
  356.4 8.6 %copy-start.23 = (f32[24,640]{1,0:T(8,128)S(1)}, f32[24,640]{1,0:T(8,128)}, u32[]{:S(2)}) copy-start(f32[24,640]{1,0:T(8,128)} %get-tuple-element.133) | copy-start | bytes 184324
  356.4 8.6 %copy-start.24 = (f32[24,640]{1,0:T(8,128)S(1)}, f32[24,640]{1,0:T(8,128)}, u32[]{:S(2)}) copy-start(f32[24,640]{1,0:T(8,128)} %get-tuple-element.132) | copy-start | bytes 184324
  356.4 8.6 %copy-start.25 = (f32[24,640]{1,0:T(8,128)S(1)}, f32[24,640]{1,0:T(8,128)}, u32[]{:S(2)}) copy-start(f32[24,640]{1,0:T(8,128)} %get-tuple-element.131) | copy-start | bytes 184324
  356.4 20.5 %copy-start.18 = (f32[24,640]{1,0:T(8,128)S(1)}, f32[24,640]{1,0:T(8,128)}, u32[]{:S(2)}) copy-start(f32[24,640]{1,0:T(8,128)} %get-tuple-element.134) | copy-start | bytes 184324
  365.0 12.5 %copy-start.14 = (bf16[24,2304]{1,0:T(8,128)(2,1)S(1)}, bf16[24,2304]{1,0:T(8,128)(2,1)}, u32[]{:S(2)}) copy-start(bf16[24,2304]{1,0:T(8,128)(2,1)} %param.21) | copy-start | bytes 331780
  365.0 6.2 %collective-permute-start.17 = (f32[40,640]{1,0:T(8,128)S(1)}, f32[40,640]{1,0:T(8,128)S(1)}, u32[]{:S(2)}, u32[]{:S(2)}) collective-permute-start(f32[40,640]{1,0:T(8,128)S(1)} %get-tuple-element.185), channel_id=1, source_target_pairs={{2,0},{4,2},{6,4},{0,6},{3,1},{5,3},{7,5},{1,7},{10,8},{12,10},{14... | collective-permute-start | bytes 307208 | tf_op jit(solution)/shard_map/ppermute | solution.py:993
  367.9 8.9 %collective-permute-start.18 = (f32[40,640]{1,0:T(8,128)S(1)}, f32[40,640]{1,0:T(8,128)S(1)}, u32[]{:S(2)}, u32[]{:S(2)}) collective-permute-start(f32[40,640]{1,0:T(8,128)S(1)} %get-tuple-element.186), channel_id=1, source_target_pairs={{4,0},{6,2},{0,4},{2,6},{5,1},{7,3},{1,5},{3,7},{12,8},{14,10},{8,... | collective-permute-start | bytes 307208 | tf_op jit(solution)/shard_map/ppermute | solution.py:993
  367.9 8.9 %collective-permute-start.19 = (f32[40,640]{1,0:T(8,128)S(1)}, f32[40,640]{1,0:T(8,128)S(1)}, u32[]{:S(2)}, u32[]{:S(2)}) collective-permute-start(f32[40,640]{1,0:T(8,128)S(1)} %get-tuple-element.187), channel_id=1, source_target_pairs={{6,0},{0,2},{2,4},{4,6},{7,1},{1,3},{3,5},{5,7},{14,8},{8,10},{10,... | collective-permute-start | bytes 307208 | tf_op jit(solution)/shard_map/ppermute | solution.py:993
  376.8 1.4 collective-permute-start.20
  376.9 6.6 %copy-start.41 = (f32[64]{0:T(128)S(1)}, f32[64]{0:T(128)}, u32[]{:S(2)}) copy-start(f32[64]{0:T(128)} %param.34) | copy-start | bytes 772
  376.9 7.1 %copy-start.28 = (f32[4096]{0:T(1024)S(1)}, f32[4096]{0:T(1024)}, u32[]{:S(2)}) copy-start(f32[4096]{0:T(1024)} %param.33) | copy-start | bytes 49156
  376.9 10.0 %copy-start.1 = (f32[32,12]{0,1:T(8,128)S(1)}, f32[32,12]{0,1:T(8,128)}, u32[]{:S(2)}) copy-start(f32[32,12]{0,1:T(8,128)} %param.22) | copy-start | bytes 4612
  377.0 7.6 %copy-start.29 = (f32[2304]{0:T(1024)S(1)}, f32[2304]{0:T(1024)}, u32[]{:S(2)}) copy-start(f32[2304]{0:T(1024)} %param.29) | copy-start | bytes 27652
  377.0 8.2 %copy-start.32 = (f32[24]{0:T(128)S(1)}, f32[24]{0:T(128)}, u32[]{:S(2)}) copy-start(f32[24]{0:T(128)} %param.28) | copy-start | bytes 292
  377.0 8.8 %copy-start.30 = (f32[768]{0:T(1024)S(1)}, f32[768]{0:T(1024)}, u32[]{:S(2)}) copy-start(f32[768]{0:T(1024)} %param.35) | copy-start | bytes 9220
  377.0 8.7 %copy-start.31 = (f32[768]{0:T(1024)S(1)}, f32[768]{0:T(1024)}, u32[]{:S(2)}) copy-start(f32[768]{0:T(1024)} %param.31) | copy-start | bytes 9220
  377.0 9.3 %copy-start.33 = (f32[24]{0:T(128)S(1)}, f32[24]{0:T(128)}, u32[]{:S(2)}) copy-start(f32[24]{0:T(128)} %param.32) | copy-start | bytes 292
  377.0 9.3 %copy-start.34 = (f32[24]{0:T(128)S(1)}, f32[24]{0:T(128)}, u32[]{:S(2)}) copy-start(f32[24]{0:T(128)} %param.30) | copy-start | bytes 292
  377.5 9.4 %copy-start.8 = (f32[24,2304]{1,0:T(8,128)}, f32[24,2304]{1,0:T(8,128)S(1)}, u32[]{:S(2)}) copy-start(f32[24,2304]{1,0:T(8,128)S(1)} %concatenate.31) | copy-start | bytes 663556
  (9 other events, 9.2 us)
Sparse Core Ops, SparseCore 0:
  11.7 67.3 all-gather.4
  82.7 95.3 all-gather.2
  207.4 82.8 reduce-scatter.2
  292.4 42.1 reduce-scatter.4

commit v2 on v1

--- a/solution.py
+++ b/solution.py
@@ -19,7 +19,7 @@
 LANES = 128
 TILE = 256
 GROUP = 4
-VMEM = 56 * 2**20
+VMEM = 60 * 2**20
 F32 = jnp.float32
 BF16 = jnp.bfloat16
 
@@ -478,14 +478,23 @@
 
 def scatter_order(groups, splits, unit):
     def source(index):
-        within = lax.rem(index, unit)
+        within = index % unit
         index = index // unit
-        g = lax.rem(index, groups)
+        g = index % groups
         index = index // groups
-        r = lax.rem(index, splits)
-        return ((index // splits * groups + g) * splits + r) * unit + within
+        return ((index // splits * groups + g) * splits + index % splits) * unit + within
 
     return source
+
+
+def reordered(values, source, unit):
+    return jnp.concatenate(
+        [
+            values[source(start) : source(start) + unit]
+            for start in range(0, values.shape[0], unit)
+        ],
+        axis=0,
+    )
 
 
 def packed_rows(values, tall, low):
@@ -534,18 +543,22 @@
     rows_apart, groups, splits = dims
     contexts, refs = refs[:heads], refs[heads:]
     result, d_mixed, d_first, d_rest, grads = refs[:5]
-    (context_t, mixed, normed, normed_t, d_normed, total, order, order_hidden) = refs[5:13]
-    wide, down, sems = refs[13:]
+    (context_t, mixed, normed, normed_t, d_normed, total, order) = refs[5:12]
+    wide, down, sems = refs[12:]
     step, chunks = pl.program_id(0), pl.num_programs(0) - 1
     width, chunk = w_gate.shape
     devices = rows_apart * groups * splits
     hidden_unit = chunk * chunks // devices
     gain = gains[1:2, :]
+    unit = width // devices
+    for_rows = scatter_order(groups, splits, unit)
+    for_hidden = scatter_order(groups, splits, hidden_unit)
+    whole_rows = unit % 8 == 0
 
     @pl.when(step == 0)
     def first():
-        order[...] = chosen((width, width), scatter_order(groups, splits, width // devices))
-        order_hidden[...] = chosen((chunk, chunk), scatter_order(groups, splits, hidden_unit))
+        if not whole_rows:
+            order[...] = chosen((width, width), for_rows)
         each = width // groups // heads
         for g in range(groups):
             for head in range(heads):
@@ -555,8 +568,13 @@
         values = tokens[...].astype(F32) + dot_nn(context, w_out[...])
         mixed[...] = values
         total[...] = values
-        normed[...] = rms_scale(values, gain).astype(BF16)
-        normed_t[...] = dot_nt(order[...], normed[...]).astype(BF16)
+        wide_values = rms_scale(values, gain)
+        normed[...] = wide_values.astype(BF16)
+        if whole_rows:
+            turned = reordered(jnp.transpose(wide_values), for_rows, unit)
+        else:
+            turned = dot_nt(order[...], normed[...])
+        normed_t[...] = turned.astype(BF16)
         d_normed[...] = jnp.zeros_like(d_normed)
 
     place = lax.rem(step, 2)
@@ -589,12 +607,13 @@
         half = 0.5 * (1.0 + turn)
         active = gate * half
         slope = half + 0.5 * gate * (1.0 - turn * turn) * (GELU_SCALE * (1.0 + 0.134145 * square))
-        hidden = (active * upward).astype(BF16)
+        wide_hidden = active * upward
+        hidden = wide_hidden.astype(BF16)
         d_gate = (d_hidden * upward * slope).astype(BF16)
         d_up = (d_hidden * active).astype(BF16)
         total[...] += dot_nn(hidden, w_down)
         d_normed[...] += dot_nt(d_gate, w_gate[...]) + dot_nt(d_up, w_up[...])
-        hidden_t = dot_nt(order_hidden[...], hidden).astype(BF16)
+        hidden_t = reordered(jnp.transpose(wide_hidden), for_hidden, hidden_unit).astype(BF16)
 
         d_down = dot_nn(hidden_t, upstream[...])
         down[place] = packed_rows(d_down, hidden_unit, width // devices).astype(BF16)
@@ -615,8 +634,11 @@
         for g in range(groups):
             d_first[g] = d_context[size * g : size * g + each]
             d_rest[g] = d_context[size * g + each : size * (g + 1)]
-        ordered = dot_nn(order[...], context_t[...]).astype(BF16)
-        wide[place, :, :width] = dot_nn(ordered, branch).astype(BF16)
+        if whole_rows:
+            d_out = reordered(dot_nn(context_t[...], branch), for_rows, unit)
+        else:
+            d_out = dot_nn(dot_nn(order[...], context_t[...]).astype(BF16), branch)
+        wide[place, :, :width] = d_out.astype(BF16)
         wide[place, :, width:] = jnp.zeros((width, 2 * chunk - width), BF16)
         wide_copy(place, step).start()
         wide_copy(1 - place, step - 1).wait()
@@ -670,7 +692,6 @@
             pltpu.VMEM((rows, width), F32),
             pltpu.VMEM((rows, width), F32),
             pltpu.VMEM((width, width), BF16),
-            pltpu.VMEM((chunk, chunk), BF16),
             pltpu.VMEM((2, width, 2 * chunk), BF16),
             pltpu.VMEM((2, width // steps, hidden), BF16),
             pltpu.SemaphoreType.DMA((2, 2)),
@@ -859,6 +880,11 @@
         out_shape=jax.ShapeDtypeStruct((tokens, width), BF16),
         scratch_shapes=[pltpu.VMEM((width, tokens), F32)],
         compiler_params=pltpu.CompilerParams(vmem_limit_bytes=VMEM),
+        cost_estimate=pl.CostEstimate(
+            flops=2 * tokens * width * weights.shape[1],
+            bytes_accessed=16 * tokens * width,
+            transcendentals=0,
+        ),
         name="input_grads",
     )(weights, own, gains, d_mixed, *d_heads)
 
@@ -1119,15 +1145,15 @@
     *columns, counts = counted(
         groups, group_heads, head_size, ints, held, d_tables, grads_own, down_shape
     )
+    counts = sum([ahead(counts, "batch", by) for by in range(1, rows_apart)], counts)
     d_received[-1] = after(d_received[-1], counts)
     d_inputs = input_grads(groups, early, own, gains, d_mixed, d_received)
-    counts = sum([ahead(counts, "batch", by) for by in range(1, rows_apart)], counts)
-    counts = after(counts, d_inputs)
     counts_rows = counts.shape[0]
     travelled = [jnp.concatenate([counts, columns[0]], axis=0)] + [
         ahead(jnp.concatenate([counts, columns[by]], axis=0), "group", groups - by)
         for by in range(1, groups)
     ]
+    *travelled, d_inputs = lax.optimization_barrier((*travelled, d_inputs))
     columns = [both[counts_rows:] for both in travelled]
     counts = sum([both[:counts_rows] for both in travelled[1:]], travelled[0][:counts_rows])
     counts = sum([ahead(counts, "split", by) for by in range(1, splits)], counts)

time: 399 us -> 389 us (0.975)
  waiting for transfers between devices: 83.1 us -> 76.1 us
  Pallas kernels: 179 us -> 175 us
    ppermute x15, waiting for transfers between devices: 19.1 us -> 11.7 us  [ahead(): lax.ppermute(array, axis, [((i + by) % size, i) for i in range(size)])]
    pallas_call x1, Pallas kernels: 29.1 us -> 25 us  [feed_forward(): pl.pallas_call(functools.partial(block_kernel, dims, len(contexts)), grid...]
  transfers between devices with their start and end apart: 31 -> 31, of which waited for: 18 -> 17; matrix products, arithmetic and copies ran while one was open for 4% -> 4% of each run, Pallas kernels for 38% -> 39%
where the time goes in v2:
time: 389 us; the launch traced here: 383 us
  Pallas kernels  175 us (45%)
  waiting for transfers between devices  76.1 us (20%)
  starting transfers between devices  60.3 us (16%)
  blocking collectives  26.7 us (7%)
  between operations  17.3 us (4%)
  other arithmetic  15.5 us (4%)
  local copies, waits for them, and re-layouts  11.8 us (3%)
    pallas_call x3, Pallas kernels, attend_back(): pl.pallas_call(functools.partial(backward_kernel, tokens, groups, splits)...  64.6 us
    ppermute x6, waiting for transfers between devices, line(): return lax.ppermute(array, 'group', pairs)  48.3 us
    pallas_call x3, Pallas kernels, attend(): pl.pallas_call(functools.partial(forward_kernel, tokens, groups, splits),...  48.1 us
    all_to_all x6, starting transfers between devices, swap_groups(): return lax.all_to_all(array, 'group', 0, 0)  28.4 us
    all_to_all x2, blocking collectives, swap_groups(): return lax.all_to_all(array, 'group', 0, 0)  26.7 us
    pallas_call x1, Pallas kernels, feed_forward(): pl.pallas_call(functools.partial(block_kernel, dims, len(contexts)), grid...  25 us
    ppermute x6, starting transfers between devices, line(): return lax.ppermute(array, 'group', pairs)  18.3 us
    ppermute x15, starting transfers between devices, ahead(): lax.ppermute(array, axis, [((i + by) % size, i) for i in range(size)])  13.6 us
  transfers between devices with their start and end apart: 31, of which 17 were waited for; matrix products, arithmetic and copies ran while one was open for 4% of the time, Pallas kernels for 39%

profile of v2, /device:TPU:0, one launch (start us, length us, event | category | flops | bytes accessed | tf_op | source)
XLA Modules:
  0.0 383.2 jit_solution(12913395795317396353)
XLA Ops:
  7.3 1.2 reshape.117
  9.2 0.7 copy.64
  10.0 5.0 %collective-permute-start = (bf16[512,768]{1,0:T(8,128)(2,1)S(1)}, bf16[512,768]{1,0:T(8,128)(2,1)S(1)}, u32[]{:S(2)}, u32[]{:S(2)}) collective-permute-start(bf16[512,768]{1,0:T(8,128)(2,1)S(1)} %bitcast.47), channel_id=1, source_target_pairs={{0,2},{2,4},{4,6},{1,3},{3,5},{5,7},{8,10},{10,12},{12,14},{9,11},... | collective-permute-start | bytes 2359304 | tf_op jit(solution)/shard_map/ppermute | solution.py:1029
  15.0 1.3 collective-permute-start.1
  16.3 0.7 pad_maximum_fusion
  17.1 17.3 %collective-permute-done.refs_0_ = bf16[512,768]{1,0:T(8,128)(2,1)S(1)} collective-permute-done((bf16[512,768]{1,0:T(8,128)(2,1)S(1)}, bf16[512,768]{1,0:T(8,128)(2,1)S(1)}, u32[]{:S(2)}, u32[]{:S(2)}) %collective-permute-start) | collective-permute-done | bytes 786464 | tf_op jit(solution)/shard_map/ppermute | solution.py:1029
  34.3 4.2 %collective-permute-done.1.refs_2_ = bf16[512,768]{1,0:T(8,128)(2,1)S(1)} collective-permute-done((bf16[512,768]{1,0:T(8,128)(2,1)S(1)}, bf16[512,768]{1,0:T(8,128)(2,1)S(1)}, u32[]{:S(2)}, u32[]{:S(2)}) %collective-permute-start.1) | collective-permute-done | bytes 786464 | tf_op jit(solution)/shard_map/ppermute | solution.py:1029
  38.5 4.3 %collective-permute-start.2 = (bf16[512,768]{1,0:T(8,128)(2,1)S(1)}, bf16[512,768]{1,0:T(8,128)(2,1)}, u32[]{:S(2)}, u32[]{:S(2)}) collective-permute-start(bf16[512,768]{1,0:T(8,128)(2,1)S(1)} %collective-permute-done.refs_0_), channel_id=1, source_target_pairs={{0,2},{2,4},{4,6},{1,3},{3,5},{5,7},{8,10},{10,12},{12,14},{9,11},... | collective-permute-start | bytes 2359304 | tf_op jit(solution)/shard_map/ppermute | solution.py:1029
  42.9 1.3 collective-permute-start.3
  44.2 22.3 %collective-permute-done.2.refs_1_ = bf16[512,768]{1,0:T(8,128)(2,1)} collective-permute-done((bf16[512,768]{1,0:T(8,128)(2,1)S(1)}, bf16[512,768]{1,0:T(8,128)(2,1)}, u32[]{:S(2)}, u32[]{:S(2)}) %collective-permute-start.2) | collective-permute-done | bytes 786464 | tf_op jit(solution)/shard_map/ppermute | solution.py:1029
  66.5 5.1 %collective-permute-start.4 = (bf16[512,768]{1,0:T(8,128)(2,1)}, bf16[512,768]{1,0:T(8,128)(2,1)S(1)}, u32[]{:S(2)}, u32[]{:S(2)}) collective-permute-start(bf16[512,768]{1,0:T(8,128)(2,1)} %collective-permute-done.2.refs_1_), channel_id=1, source_target_pairs={{0,2},{2,4},{4,6},{1,3},{3,5},{5,7},{8,10},{10,12},{12,14},{9,11},... | collective-permute-start | bytes 2359304 | tf_op jit(solution)/shard_map/ppermute | solution.py:1029
  71.6 2.3 collective-permute-done.3.refs_3_
  73.9 1.3 collective-permute-start.5
  76.0 3.2 all-gather.5.cloned.1.call-done.weights
  79.1 12.1 %project.1 = (bf16[768,2048]{1,0:T(8,128)(2,1)}, bf16[2048,384]{1,0:T(8,128)(2,1)}, bf16[2048,384]{1,0:T(8,128)(2,1)}, f32[8,768]{1,0:T(8,128)}, bf16[768,768]{1,0:T(8,128)(2,1)}) custom-call(s32[7]{0:T(128)} %concatenate.27.ints, bf16[768,2560]{1,0:T(8,128)(2,1)} %all-gather.5.cloned.1.call-done.weights, bf16[512,768]{1,0:T(8,128)(2,1)} %bitcast.43, ...), custom_call_target="tpu_custom_call" | custom-call | flops 4831838208 | bytes 12582912 | tf_op jit(solution)/shard_map/project/pallas_call | solution.py:398
  91.3 2.2 collective-permute-done.5.behind
  93.5 0.9 copy-done.10
  94.4 6.2 %project_last.1 = (bf16[768,2048]{1,0:T(8,128)(2,1)}, bf16[2048,384]{1,0:T(8,128)(2,1)}, bf16[2048,384]{1,0:T(8,128)(2,1)}) custom-call(s32[7]{0:T(128)} %concatenate.27.ints, bf16[768,2560]{1,0:T(8,128)(2,1)} %all-gather.5.cloned.1.call-done.weights, bf16[512,768]{1,0:T(8,128)(2,1)} %bitcast.44, ...), custom_call_target="tpu_custom_call", output_to_operand_aliasing={{0}: (7, {}), {1}: (8, {}), {2}: (9, {})} | custom-call | flops 1207959552 | bytes 3145728 | tf_op jit(solution)/shard_map/project_last/pallas_call | solution.py:452
  101.1 3.1 collective-permute-done.6.refs_1_
  104.1 1.2 copy-done.35
  105.3 16.0 %attend.3 = (bf16[16384,512]{1,0:T(8,128)(2,1)}, bf16[4,64,512]{2,1,0:T(8,128)(2,1)}, f32[4,80,512]{2,1,0:T(8,128)}) custom-call(s32[7]{0:T(128)} %concatenate.27.ints, f32[1,32]{1,0:T(1,128)} %get-tuple-element.200.table, bf16[2048,384]{1,0:T(8,128)(2,1)} %get-tuple-element.86.query, bf16[2048,384]{1,0:T(8,128)(2,1)} %get-tuple-element.87.refs_0_, ...), custom_call_target="tpu_custom_call" | custom-call | flops 8589934592 | bytes 16777216 | tf_op jit(solution)/shard_map/attend/pallas_call | solution.py:904
  121.3 3.6 all-to-all-start
  124.9 16.1 %attend.4 = (bf16[16384,512]{1,0:T(8,128)(2,1)}, bf16[4,64,512]{2,1,0:T(8,128)(2,1)}, f32[4,80,512]{2,1,0:T(8,128)}) custom-call(s32[7]{0:T(128)} %concatenate.27.ints, f32[1,32]{1,0:T(1,128)} %get-tuple-element.199.table, bf16[2048,384]{1,0:T(8,128)(2,1)} %get-tuple-element.86.query, bf16[2048,384]{1,0:T(8,128)(2,1)} %get-tuple-element.87.refs_0_, ...), custom_call_target="tpu_custom_call" | custom-call | flops 8589934592 | bytes 16777216 | tf_op jit(solution)/shard_map/attend/pallas_call | solution.py:904
  141.0 5.2 %all-to-all-start.1 = ((bf16[4,64,512]{2,1,0:T(8,128)(2,1)}), bf16[4,64,512]{2,1,0:T(8,128)(2,1)S(1)}, u32[]{:S(2)}, u32[]{:S(2)}) async-start(bf16[4,64,512]{2,1,0:T(8,128)(2,1)} %get-tuple-element.91), calls=%async_computation.1 | async-start | bytes 524288 | tf_op jit(solution)/shard_map/all_to_all | solution.py:1022
  146.2 16.0 %attend.5 = (bf16[16384,512]{1,0:T(8,128)(2,1)}, bf16[4,64,512]{2,1,0:T(8,128)(2,1)}, f32[4,80,512]{2,1,0:T(8,128)}) custom-call(s32[7]{0:T(128)} %concatenate.27.ints, f32[1,32]{1,0:T(1,128)} %get-tuple-element.198.table, bf16[2048,384]{1,0:T(8,128)(2,1)} %get-tuple-element.86.query, bf16[2048,384]{1,0:T(8,128)(2,1)} %get-tuple-element.87.refs_0_, ...), custom_call_target="tpu_custom_call" | custom-call | flops 8589934592 | bytes 16777216 | tf_op jit(solution)/shard_map/attend/pallas_call | solution.py:904
  162.2 0.9 all-to-all-done.1.refs_1_
  163.1 14.1 %all_to_all.40.refs_2_ = bf16[4,64,512]{2,1,0:T(8,128)(2,1)} all-to-all(bf16[4,64,512]{2,1,0:T(8,128)(2,1)} %get-tuple-element.94), channel_id=1, replica_groups=mesh['batch'=4,'group'=4,'split'=2] {'group'}, dimensions={0} | all-to-all | bytes 524288 | tf_op jit(solution)/shard_map/all_to_all | solution.py:1022
  177.8 25.0 %feed_forward.1 = (bf16[512,768]{1,0:T(8,128)(2,1)}, f32[512,768]{1,0:T(8,128)}, bf16[4,64,512]{2,1,0:T(8,128)(2,1)}, bf16[4,128,512]{2,1,0:T(8,128)(2,1)}, bf16[768,7168]{1,0:T(8,128)(2,1)}) custom-call(s32[7]{0:T(128)} %concatenate.27.ints, bf16[512,768]{1,0:T(8,128)(2,1)} %bitcast.45, ...), custom_call_target="tpu_custom_call" | custom-call | flops 16307453952 | bytes 18874368 | tf_op jit(solution)/shard_map/feed_forward/pallas_call | solution.py:657
  202.9 0.9 copy-done.17
  203.8 12.7 %all_to_all.41 = bf16[4,64,512]{2,1,0:T(8,128)(2,1)} all-to-all(bf16[4,64,512]{2,1,0:T(8,128)(2,1)S(1)} %copy-done.17), channel_id=1, replica_groups=mesh['batch'=4,'group'=4,'split'=2] {'group'}, dimensions={0} | all-to-all | bytes 524288 | tf_op jit(solution)/shard_map/all_to_all | solution.py:1022
  216.4 3.5 all-to-all-start.4
  219.9 21.6 %attend_back.3 = (bf16[4,192,512]{2,1,0:T(8,128)(2,1)}, bf16[4,128,512]{2,1,0:T(8,128)(2,1)}, f32[32,128]{1,0:T(8,128)}) custom-call(s32[7]{0:T(128)} %concatenate.27.ints, bf16[2048,384]{1,0:T(8,128)(2,1)} %get-tuple-element.86.query, bf16[4,1,64,512]{3,2,1,0:T(8,128)(2,1)} %bitcast.56, f32[4,80,512]{2,1,0:T(8,128)} %get-tuple-element.98.stats, ...), custom_call_target="tpu_custom_call" | custom-call | flops 17179869184 | bytes 16777216 | tf_op jit(solution)/shard_map/attend_back/pallas_call | solution.py:941
  241.6 2.1 collective-permute-done.7
  243.8 2.2 add_convert_fusion.2.refs_0_
  245.9 5.4 %all-to-all-start.5 = ((bf16[4,192,512]{2,1,0:T(8,128)(2,1)}), bf16[4,192,512]{2,1,0:T(8,128)(2,1)S(1)}, u32[]{:S(2)}, u32[]{:S(2)}) async-start(bf16[4,192,512]{2,1,0:T(8,128)(2,1)} %add_convert_fusion.2.refs_0_), calls=%async_computation.5 | async-start | bytes 1572864 | tf_op jit(solution)/shard_map/all_to_all | solution.py:1022
  251.3 21.5 %attend_back.4 = (bf16[4,192,512]{2,1,0:T(8,128)(2,1)}, bf16[4,128,512]{2,1,0:T(8,128)(2,1)}, f32[32,128]{1,0:T(8,128)}) custom-call(s32[7]{0:T(128)} %concatenate.27.ints, bf16[2048,384]{1,0:T(8,128)(2,1)} %get-tuple-element.86.query, bf16[4,2,64,512]{3,2,1,0:T(8,128)(2,1)} %bitcast.52, f32[4,80,512]{2,1,0:T(8,128)} %get-tuple-element.107.stats, ...), custom_call_target="tpu_custom_call" | custom-call | flops 17179869184 | bytes 16777216 | tf_op jit(solution)/shard_map/attend_back/pallas_call | solution.py:941
  272.9 2.1 collective-permute-done.8
  275.0 2.2 add_convert_fusion.1.refs_1_
  277.2 4.7 %all-to-all-start.6 = ((bf16[4,192,512]{2,1,0:T(8,128)(2,1)}), bf16[4,192,512]{2,1,0:T(8,128)(2,1)S(1)}, u32[]{:S(2)}, u32[]{:S(2)}) async-start(bf16[4,192,512]{2,1,0:T(8,128)(2,1)} %add_convert_fusion.1.refs_1_), calls=%async_computation.7 | async-start | bytes 1572864 | tf_op jit(solution)/shard_map/all_to_all | solution.py:1022
  281.9 4.0 %reduce-scatter.3.cloned.1.call-done = bf16[96,7168]{1,0:T(8,128)(2,1)} async-done(((bf16[768,7168]{1,0:T(8,128)(2,1)}), bf16[96,7168]{1,0:T(8,128)(2,1)}) %reduce-scatter.3.cloned.1.call-update) | async-done | bytes 1376272 | tf_op jit(solution)/shard_map/reduce_scatter | solution.py:1101
  285.9 21.5 %attend_back.5 = (bf16[4,192,512]{2,1,0:T(8,128)(2,1)}, bf16[4,128,512]{2,1,0:T(8,128)(2,1)}, f32[32,128]{1,0:T(8,128)}) custom-call(s32[7]{0:T(128)} %concatenate.27.ints, bf16[2048,384]{1,0:T(8,128)(2,1)} %get-tuple-element.86.query, bf16[4,2,64,512]{3,2,1,0:T(8,128)(2,1)} %bitcast.53, f32[4,80,512]{2,1,0:T(8,128)} %get-tuple-element.116.stats, ...), custom_call_target="tpu_custom_call" | custom-call | flops 17179869184 | bytes 16777216 | tf_op jit(solution)/shard_map/attend_back/pallas_call | solution.py:941
  307.4 2.1 collective-permute-done.9
  309.5 2.2 add_convert_fusion.refs_2_
  311.7 2.0 all-to-all-done.6.refs_1_
  313.7 6.1 %all-to-all-start.7 = ((bf16[4,192,512]{2,1,0:T(8,128)(2,1)}), bf16[4,192,512]{2,1,0:T(8,128)(2,1)S(1)}, u32[]{:S(2)}, u32[]{:S(2)}) async-start(bf16[4,192,512]{2,1,0:T(8,128)(2,1)} %add_convert_fusion.refs_2_), calls=%async_computation.8 | async-start | bytes 1572864 | tf_op jit(solution)/shard_map/all_to_all | solution.py:1022
  319.8 6.7 %weight_grads.1 = (bf16[384,576]{1,0:T(8,128)(2,1)}, bf16[384,576]{1,0:T(8,128)(2,1)}) custom-call(bf16[768,2048]{1,0:T(8,128)(2,1)} %get-tuple-element.96.normed_t, bf16[4,192,512]{2,1,0:T(8,128)(2,1)} %add_convert_fusion.2.refs_0_, bf16[4,192,512]{2,1,0:T(8,128)(2,1)} %add_convert_fusion.1.refs_1_, bf16[4,192,512]{2,1,0:T(8,128)(2,1)} %add_convert_fusion.refs_2_), custom_call_target="tpu_custom_call" | custom-call | flops 1811939328 | bytes 3145728 | tf_op jit(solution)/shard_map/weight_grads/pallas_call | solution.py:733
  326.6 2.1 collective-permute-done.10.refs_1_
  328.6 0.8 copy-done.13
  329.4 2.0 added.1
  331.4 1.5 collective-permute-start.11
  332.8 1.6 collective-permute-start.12
  334.5 1.3 collective-permute-start.13
  335.8 5.4 %all-to-all-done.7.refs_2_ = bf16[4,192,512]{2,1,0:T(8,128)(2,1)S(1)} async-done(((bf16[4,192,512]{2,1,0:T(8,128)(2,1)}), bf16[4,192,512]{2,1,0:T(8,128)(2,1)S(1)}, u32[]{:S(2)}, u32[]{:S(2)}) %all-to-all-start.7) | async-done | bytes 786464 | tf_op jit(solution)/shard_map/all_to_all | solution.py:1022
  341.3 0.6 copy-done.18
  342.0 2.2 counted.1
  344.2 2.5 collective-permute-start.14
  347.7 1.0 slice.255
  350.5 0.7 multiply_reduce_fusion.5
  351.3 0.7 copy.58
  352.4 1.6 collective-permute-start.17
  353.9 2.4 collective-permute-start.18
  356.3 1.5 collective-permute-start.19
  357.8 8.4 %input_grads.1 = bf16[512,768]{1,0:T(8,128)(2,1)} custom-call(bf16[768,2560]{1,0:T(8,128)(2,1)} %all-gather.5.cloned.1.call-done.weights, bf16[512,768]{1,0:T(8,128)(2,1)} %bitcast.46, f32[8,768]{1,0:T(8,128)} %get-tuple-element.81.gains, f32[512,768]{1,0:T(8,128)} %get-tuple-element.136.d_mixed, bf16[4,192,512]{2,1,0:T(8,128)(2,1)} %copy-done.3, ...), custom_call_target="tpu_custom_call" | custom-call | flops 2013265920 | bytes 6291456 | tf_op jit(solution)/shard_map/input_grads/pallas_call | solution.py:869
  373.6 0.6 multiply_add_fusion
  (163 shorter events, 13.1 us)
Async XLA Ops:
  7.2 93.3 %copy-start = (f32[32,12]{0,1:T(8,128)S(1)}, f32[32,12]{0,1:T(8,128)}, u32[]{:S(2)}) copy-start(f32[32,12]{0,1:T(8,128)} %param.22) | copy-start | bytes 4612
  7.2 1.8 copy-start.40
  7.2 1.8 copy-start.39
  7.2 2.8 copy-start.2
  7.2 9.0 %copy-start.21 = (bf16[64,768]{1,0:T(8,128)(2,1)S(1)}, bf16[64,768]{1,0:T(8,128)(2,1)}, u32[]{:S(2)}) copy-start(bf16[64,768]{1,0:T(8,128)(2,1)} %param.26) | copy-start | bytes 294916
  7.2 9.1 %copy-start.27 = (bf16[24,768]{1,0:T(8,128)(2,1)S(1)}, bf16[24,768]{1,0:T(8,128)(2,1)}, u32[]{:S(2)}) copy-start(bf16[24,768]{1,0:T(8,128)(2,1)} %param.23) | copy-start | bytes 110596
  7.3 9.1 %copy-start.11 = (bf16[24,4096]{1,0:T(8,128)(2,1)S(1)}, bf16[24,4096]{1,0:T(8,128)(2,1)}, u32[]{:S(2)}) copy-start(bf16[24,4096]{1,0:T(8,128)(2,1)} %param.25) | copy-start | bytes 589828
  7.3 71.9 %all-gather.5.cloned.1.call-start = ((), (), s32[]{:S(2)}) async-start(), calls=%async_computation.11 | async-start | bytes 4055040 | tf_op jit(solution)/shard_map/all_gather | solution.py:1047
  8.5 66.7 %copy-start.38 = (s32[1,3]{1,0:T(1,128)S(1)}, s32[1,3]{1,0:T(1,128)}, u32[]{:S(2)}) copy-start(s32[1,3]{1,0:T(1,128)} %param.19) | copy-start | bytes 40
  9.9 167.8 %all-gather.3.cloned.1.call-start = ((), (), s32[]{:S(2)}) async-start(), calls=%async_computation.10 | async-start | bytes 10948608 | tf_op jit(solution)/shard_map/all_gather | solution.py:1051
  10.0 24.4 %collective-permute-start = (bf16[512,768]{1,0:T(8,128)(2,1)S(1)}, bf16[512,768]{1,0:T(8,128)(2,1)S(1)}, u32[]{:S(2)}, u32[]{:S(2)}) collective-permute-start(bf16[512,768]{1,0:T(8,128)(2,1)S(1)} %bitcast.47), channel_id=1, source_target_pairs={{0,2},{2,4},{4,6},{1,3},{3,5},{5,7},{8,10},{10,12},{12,14},{9,11},... | collective-permute-start | bytes 2359304 | tf_op jit(solution)/shard_map/ppermute | solution.py:1029
  15.0 23.5 %collective-permute-start.1 = (bf16[512,768]{1,0:T(8,128)(2,1)S(1)}, bf16[512,768]{1,0:T(8,128)(2,1)S(1)}, u32[]{:S(2)}, u32[]{:S(2)}) collective-permute-start(bf16[512,768]{1,0:T(8,128)(2,1)S(1)} %bitcast.48), channel_id=1, source_target_pairs={{2,0},{4,2},{6,4},{3,1},{5,3},{7,5},{10,8},{12,10},{14,12},{11,9},... | collective-permute-start | bytes 2359304 | tf_op jit(solution)/shard_map/ppermute | solution.py:1029
  34.3 44.8 %copy-start.36 = (bf16[512,768]{1,0:T(8,128)(2,1)}, bf16[512,768]{1,0:T(8,128)(2,1)S(1)}, u32[]{:S(2)}) copy-start(bf16[512,768]{1,0:T(8,128)(2,1)S(1)} %collective-permute-done.refs_0_) | copy-start | bytes 2359300
  38.5 40.6 %copy-start.37 = (bf16[512,768]{1,0:T(8,128)(2,1)}, bf16[512,768]{1,0:T(8,128)(2,1)S(1)}, u32[]{:S(2)}) copy-start(bf16[512,768]{1,0:T(8,128)(2,1)S(1)} %collective-permute-done.1.refs_2_) | copy-start | bytes 2359300
  38.5 27.9 %collective-permute-start.2 = (bf16[512,768]{1,0:T(8,128)(2,1)S(1)}, bf16[512,768]{1,0:T(8,128)(2,1)}, u32[]{:S(2)}, u32[]{:S(2)}) collective-permute-start(bf16[512,768]{1,0:T(8,128)(2,1)S(1)} %collective-permute-done.refs_0_), channel_id=1, source_target_pairs={{0,2},{2,4},{4,6},{1,3},{3,5},{5,7},{8,10},{10,12},{12,14},{9,11},... | collective-permute-start | bytes 2359304 | tf_op jit(solution)/shard_map/ppermute | solution.py:1029
  42.9 31.0 %collective-permute-start.3 = (bf16[512,768]{1,0:T(8,128)(2,1)S(1)}, bf16[512,768]{1,0:T(8,128)(2,1)}, u32[]{:S(2)}, u32[]{:S(2)}) collective-permute-start(bf16[512,768]{1,0:T(8,128)(2,1)S(1)} %collective-permute-done.1.refs_2_), channel_id=1, source_target_pairs={{2,0},{4,2},{6,4},{3,1},{5,3},{7,5},{10,8},{12,10},{14,12},{11,9},... | collective-permute-start | bytes 2359304 | tf_op jit(solution)/shard_map/ppermute | solution.py:1029
  66.5 24.8 %collective-permute-start.4 = (bf16[512,768]{1,0:T(8,128)(2,1)}, bf16[512,768]{1,0:T(8,128)(2,1)S(1)}, u32[]{:S(2)}, u32[]{:S(2)}) collective-permute-start(bf16[512,768]{1,0:T(8,128)(2,1)} %collective-permute-done.2.refs_1_), channel_id=1, source_target_pairs={{0,2},{2,4},{4,6},{1,3},{3,5},{5,7},{8,10},{10,12},{12,14},{9,11},... | collective-permute-start | bytes 2359304 | tf_op jit(solution)/shard_map/ppermute | solution.py:1029
  73.9 19.6 %collective-permute-start.5 = (bf16[512,768]{1,0:T(8,128)(2,1)}, bf16[512,768]{1,0:T(8,128)(2,1)S(1)}, u32[]{:S(2)}, u32[]{:S(2)}) collective-permute-start(bf16[512,768]{1,0:T(8,128)(2,1)} %collective-permute-done.3.refs_3_), channel_id=1, source_target_pairs={{2,0},{4,2},{6,4},{3,1},{5,3},{7,5},{10,8},{12,10},{14,12},{11,9},... | collective-permute-start | bytes 2359304 | tf_op jit(solution)/shard_map/ppermute | solution.py:1029
  91.3 2.2 copy-start.9
  100.5 3.6 collective-permute-start.6
  121.3 19.7 %all-to-all-start = ((bf16[4,64,512]{2,1,0:T(8,128)(2,1)}), bf16[4,64,512]{2,1,0:T(8,128)(2,1)S(1)}, u32[]{:S(2)}, u32[]{:S(2)}) async-start(bf16[4,64,512]{2,1,0:T(8,128)(2,1)} %get-tuple-element.88), calls=%async_computation | async-start | bytes 524288 | tf_op jit(solution)/shard_map/all_to_all | solution.py:1022
  141.0 21.2 %copy-start.15 = (bf16[4,64,512]{2,1,0:T(8,128)(2,1)}, bf16[4,64,512]{2,1,0:T(8,128)(2,1)S(1)}, u32[]{:S(2)}) copy-start(bf16[4,64,512]{2,1,0:T(8,128)(2,1)S(1)} %all-to-all-done.refs_0_) | copy-start | bytes 786436
  141.0 22.1 %all-to-all-start.1 = ((bf16[4,64,512]{2,1,0:T(8,128)(2,1)}), bf16[4,64,512]{2,1,0:T(8,128)(2,1)S(1)}, u32[]{:S(2)}, u32[]{:S(2)}) async-start(bf16[4,64,512]{2,1,0:T(8,128)(2,1)} %get-tuple-element.91), calls=%async_computation.1 | async-start | bytes 524288 | tf_op jit(solution)/shard_map/all_to_all | solution.py:1022
  146.2 139.6 %reduce-scatter.3.cloned.1.call-start = ((), (), s32[]{:S(2)}) async-start(), calls=%async_computation.12 | async-start | bytes 12386304 | tf_op jit(solution)/shard_map/reduce_scatter | solution.py:1101
  163.1 14.6 %copy-start.16 = (bf16[4,64,512]{2,1,0:T(8,128)(2,1)}, bf16[4,64,512]{2,1,0:T(8,128)(2,1)S(1)}, u32[]{:S(2)}) copy-start(bf16[4,64,512]{2,1,0:T(8,128)(2,1)S(1)} %all-to-all-done.1.refs_1_) | copy-start | bytes 786436
  216.4 25.1 %all-to-all-start.4 = ((bf16[4,128,512]{2,1,0:T(8,128)(2,1)}), bf16[4,128,512]{2,1,0:T(8,128)(2,1)S(1)}, u32[]{:S(2)}, u32[]{:S(2)}) async-start(bf16[4,128,512]{2,1,0:T(8,128)(2,1)} %get-tuple-element.103), calls=%async_computation.4 | async-start | bytes 1048576 | tf_op jit(solution)/shard_map/all_to_all | solution.py:1022
  241.6 4.4 %copy-start.12 = (bf16[4,128,512]{2,1,0:T(8,128)(2,1)}, bf16[4,128,512]{2,1,0:T(8,128)(2,1)S(1)}, u32[]{:S(2)}) copy-start(bf16[4,128,512]{2,1,0:T(8,128)(2,1)S(1)} %all-to-all-done.4) | copy-start | bytes 1572868
  241.6 2.2 collective-permute-start.7
  245.9 26.9 %all-to-all-start.5 = ((bf16[4,192,512]{2,1,0:T(8,128)(2,1)}), bf16[4,192,512]{2,1,0:T(8,128)(2,1)S(1)}, u32[]{:S(2)}, u32[]{:S(2)}) async-start(bf16[4,192,512]{2,1,0:T(8,128)(2,1)} %add_convert_fusion.2.refs_0_), calls=%async_computation.5 | async-start | bytes 1572864 | tf_op jit(solution)/shard_map/all_to_all | solution.py:1022
  272.8 4.4 %copy-start.3 = (bf16[4,192,512]{2,1,0:T(8,128)(2,1)}, bf16[4,192,512]{2,1,0:T(8,128)(2,1)S(1)}, u32[]{:S(2)}) copy-start(bf16[4,192,512]{2,1,0:T(8,128)(2,1)S(1)} %all-to-all-done.5.refs_0_) | copy-start | bytes 2359300
  272.8 2.2 collective-permute-start.8
  277.2 36.5 %all-to-all-start.6 = ((bf16[4,192,512]{2,1,0:T(8,128)(2,1)}), bf16[4,192,512]{2,1,0:T(8,128)(2,1)S(1)}, u32[]{:S(2)}, u32[]{:S(2)}) async-start(bf16[4,192,512]{2,1,0:T(8,128)(2,1)} %add_convert_fusion.1.refs_1_), calls=%async_computation.7 | async-start | bytes 1572864 | tf_op jit(solution)/shard_map/all_to_all | solution.py:1022
  281.9 59.5 %reduce-scatter.5.cloned.1.call-start = ((), (), s32[]{:S(2)}) async-start(), calls=%async_computation.13 | async-start | bytes 1720320 | tf_op jit(solution)/shard_map/reduce_scatter | solution.py:1103
  307.4 2.1 collective-permute-start.9
  313.7 12.9 %copy-start.4 = (bf16[4,192,512]{2,1,0:T(8,128)(2,1)}, bf16[4,192,512]{2,1,0:T(8,128)(2,1)S(1)}, u32[]{:S(2)}) copy-start(bf16[4,192,512]{2,1,0:T(8,128)(2,1)S(1)} %all-to-all-done.6.refs_1_) | copy-start | bytes 2359300
  313.7 27.5 %all-to-all-start.7 = ((bf16[4,192,512]{2,1,0:T(8,128)(2,1)}), bf16[4,192,512]{2,1,0:T(8,128)(2,1)S(1)}, u32[]{:S(2)}, u32[]{:S(2)}) async-start(bf16[4,192,512]{2,1,0:T(8,128)(2,1)} %add_convert_fusion.refs_2_), calls=%async_computation.8 | async-start | bytes 1572864 | tf_op jit(solution)/shard_map/all_to_all | solution.py:1022
  326.5 2.1 collective-permute-start.10
  331.4 9.9 %collective-permute-start.11 = (bf16[96,576]{1,0:T(8,128)(2,1)}, bf16[96,576]{1,0:T(8,128)(2,1)S(1)}, u32[]{:S(2)}, u32[]{:S(2)}) collective-permute-start(bf16[96,576]{1,0:T(8,128)(2,1)} %get-tuple-element.125), channel_id=1, source_target_pairs={{24,0},{0,8},{8,16},{16,24},{25,1},{1,9},{9,17},{17,25},{26,2},{2,... | collective-permute-start | bytes 331784 | tf_op jit(solution)/shard_map/ppermute | solution.py:1019
  332.8 8.4 %collective-permute-start.12 = (bf16[96,576]{1,0:T(8,128)(2,1)}, bf16[96,576]{1,0:T(8,128)(2,1)S(1)}, u32[]{:S(2)}, u32[]{:S(2)}) collective-permute-start(bf16[96,576]{1,0:T(8,128)(2,1)} %get-tuple-element.126), channel_id=1, source_target_pairs={{16,0},{24,8},{0,16},{8,24},{17,1},{25,9},{1,17},{9,25},{18,2},{26... | collective-permute-start | bytes 331784 | tf_op jit(solution)/shard_map/ppermute | solution.py:1019
  334.5 6.8 %collective-permute-start.13 = (bf16[96,576]{1,0:T(8,128)(2,1)}, bf16[96,576]{1,0:T(8,128)(2,1)S(1)}, u32[]{:S(2)}, u32[]{:S(2)}) collective-permute-start(bf16[96,576]{1,0:T(8,128)(2,1)} %get-tuple-element.127), channel_id=1, source_target_pairs={{8,0},{16,8},{24,16},{0,24},{9,1},{17,9},{25,17},{1,25},{10,2},{18... | collective-permute-start | bytes 331784 | tf_op jit(solution)/shard_map/ppermute | solution.py:1019
  341.2 8.2 %copy-start.5 = (bf16[4,192,512]{2,1,0:T(8,128)(2,1)}, bf16[4,192,512]{2,1,0:T(8,128)(2,1)S(1)}, u32[]{:S(2)}) copy-start(bf16[4,192,512]{2,1,0:T(8,128)(2,1)S(1)} %all-to-all-done.7.refs_2_) | copy-start | bytes 2359300
  344.2 7.8 %collective-permute-start.14 = (f32[16,640]{1,0:T(8,128)}, f32[16,640]{1,0:T(8,128)S(1)}, u32[]{:S(2)}, u32[]{:S(2)}) collective-permute-start(f32[16,640]{1,0:T(8,128)} %get-tuple-element.131), channel_id=1, source_target_pairs={{8,0},{16,8},{24,16},{0,24},{9,1},{17,9},{25,17},{1,25},{10,2},{18... | collective-permute-start | bytes 122888 | tf_op jit(solution)/shard_map/ppermute | solution.py:1019
  346.7 5.3 %collective-permute-start.15 = (f32[16,640]{1,0:T(8,128)}, f32[16,640]{1,0:T(8,128)S(1)}, u32[]{:S(2)}, u32[]{:S(2)}) collective-permute-start(f32[16,640]{1,0:T(8,128)} %get-tuple-element.131), channel_id=1, source_target_pairs={{16,0},{24,8},{0,16},{8,24},{17,1},{25,9},{1,17},{9,25},{18,2},{26... | collective-permute-start | bytes 122888 | tf_op jit(solution)/shard_map/ppermute | solution.py:1019
  347.1 5.1 %collective-permute-start.16 = (f32[16,640]{1,0:T(8,128)}, f32[16,640]{1,0:T(8,128)S(1)}, u32[]{:S(2)}, u32[]{:S(2)}) collective-permute-start(f32[16,640]{1,0:T(8,128)} %get-tuple-element.131), channel_id=1, source_target_pairs={{24,0},{0,8},{8,16},{16,24},{25,1},{1,9},{9,17},{17,25},{26,2},{2,... | collective-permute-start | bytes 122888 | tf_op jit(solution)/shard_map/ppermute | solution.py:1019
  349.3 2.9 copy-start.26
  349.3 2.9 copy-start.22
  349.3 2.9 copy-start.23
  349.4 2.9 copy-start.24
  349.4 2.9 copy-start.25
  349.8 16.4 %copy-start.7 = (f32[24,4096]{1,0:T(8,128)}, f32[24,4096]{1,0:T(8,128)S(1)}, u32[]{:S(2)}) copy-start(f32[24,4096]{1,0:T(8,128)S(1)} %reshape.122) | copy-start | bytes 1179652
  352.4 13.8 %collective-permute-start.17 = (f32[40,640]{1,0:T(8,128)S(1)}, f32[40,640]{1,0:T(8,128)S(1)}, u32[]{:S(2)}, u32[]{:S(2)}) collective-permute-start(f32[40,640]{1,0:T(8,128)S(1)} %get-tuple-element.195), channel_id=1, source_target_pairs={{6,0},{0,2},{2,4},{4,6},{7,1},{1,3},{3,5},{5,7},{14,8},{8,10},{10,... | collective-permute-start | bytes 307208 | tf_op jit(solution)/shard_map/ppermute | solution.py:1019
  353.9 12.3 %collective-permute-start.18 = (f32[40,640]{1,0:T(8,128)S(1)}, f32[40,640]{1,0:T(8,128)S(1)}, u32[]{:S(2)}, u32[]{:S(2)}) collective-permute-start(f32[40,640]{1,0:T(8,128)S(1)} %get-tuple-element.196), channel_id=1, source_target_pairs={{4,0},{6,2},{0,4},{2,6},{5,1},{7,3},{1,5},{3,7},{12,8},{14,10},{8,... | collective-permute-start | bytes 307208 | tf_op jit(solution)/shard_map/ppermute | solution.py:1019
  356.3 9.9 %collective-permute-start.19 = (f32[40,640]{1,0:T(8,128)S(1)}, f32[40,640]{1,0:T(8,128)S(1)}, u32[]{:S(2)}, u32[]{:S(2)}) collective-permute-start(f32[40,640]{1,0:T(8,128)S(1)} %get-tuple-element.194), channel_id=1, source_target_pairs={{2,0},{4,2},{6,4},{0,6},{3,1},{5,3},{7,5},{1,7},{10,8},{12,10},{14... | collective-permute-start | bytes 307208 | tf_op jit(solution)/shard_map/ppermute | solution.py:1019
  366.2 1.5 collective-permute-start.20
  366.3 10.2 %copy-start.1 = (f32[32,12]{0,1:T(8,128)S(1)}, f32[32,12]{0,1:T(8,128)}, u32[]{:S(2)}) copy-start(f32[32,12]{0,1:T(8,128)} %param.22) | copy-start | bytes 4612
  366.3 6.7 %copy-start.41 = (f32[64]{0:T(128)S(1)}, f32[64]{0:T(128)}, u32[]{:S(2)}) copy-start(f32[64]{0:T(128)} %param.34) | copy-start | bytes 772
  366.4 7.2 %copy-start.28 = (f32[4096]{0:T(1024)S(1)}, f32[4096]{0:T(1024)}, u32[]{:S(2)}) copy-start(f32[4096]{0:T(1024)} %param.33) | copy-start | bytes 49156
  366.4 7.8 %copy-start.29 = (f32[2304]{0:T(1024)S(1)}, f32[2304]{0:T(1024)}, u32[]{:S(2)}) copy-start(f32[2304]{0:T(1024)} %param.29) | copy-start | bytes 27652
  366.4 8.4 %copy-start.32 = (f32[24]{0:T(128)S(1)}, f32[24]{0:T(128)}, u32[]{:S(2)}) copy-start(f32[24]{0:T(128)} %param.28) | copy-start | bytes 292
  366.4 8.9 %copy-start.30 = (f32[768]{0:T(1024)S(1)}, f32[768]{0:T(1024)}, u32[]{:S(2)}) copy-start(f32[768]{0:T(1024)} %param.35) | copy-start | bytes 9220
  366.4 8.9 %copy-start.31 = (f32[768]{0:T(1024)S(1)}, f32[768]{0:T(1024)}, u32[]{:S(2)}) copy-start(f32[768]{0:T(1024)} %param.31) | copy-start | bytes 9220
  366.4 9.5 %copy-start.33 = (f32[24]{0:T(128)S(1)}, f32[24]{0:T(128)}, u32[]{:S(2)}) copy-start(f32[24]{0:T(128)} %param.32) | copy-start | bytes 292
  366.4 9.5 %copy-start.34 = (f32[24]{0:T(128)S(1)}, f32[24]{0:T(128)}, u32[]{:S(2)}) copy-start(f32[24]{0:T(128)} %param.30) | copy-start | bytes 292
  367.1 9.4 %copy-start.8 = (f32[24,2304]{1,0:T(8,128)}, f32[24,2304]{1,0:T(8,128)S(1)}, u32[]{:S(2)}) copy-start(f32[24,2304]{1,0:T(8,128)S(1)} %concatenate.35) | copy-start | bytes 663556
  (9 other events, 8.6 us)
Sparse Core Ops, SparseCore 0:
  11.7 67.3 all-gather.4
  82.7 95.0 all-gather.2
  203.0 82.7 reduce-scatter.2
  288.0 41.4 reduce-scatter.4

commit v3 on v2

--- a/solution.py
+++ b/solution.py
@@ -1095,7 +1095,17 @@
     )
     result, d_mixed, d_first, d_rest, held = outs
 
-    d_first = swap_groups(d_first)
+    parts = [lax.dynamic_index_in_dim(d_first, group, 0, keepdims=False)]
+    for by in range(1, groups):
+        piece = lax.dynamic_index_in_dim(d_first, (group + by) % groups, 0, keepdims=False)
+        parts.append(ahead(piece, "group", groups - by))
+    d_first = []
+    for index in range(groups):
+        piece = parts[0]
+        for by in range(1, groups):
+            piece = jnp.where((group + groups - by) % groups == index, parts[by], piece)
+        d_first.append(piece)
+    d_first = jnp.stack(d_first)
     d_rest = swap_groups(d_rest)
     d_contexts = [d_first[:, None], d_rest.reshape(groups, group_heads - 1, head_size, tok_rows)]
     row_sum = lax.psum_scatter(held, ("batch", "split"), scatter_dimension=0, tiled=True)

time: 389 us -> 386 us (level)
  blocking collectives: 26.7 us -> 14.1 us
  waiting for transfers between devices: 76.1 us -> 82.6 us
    all_to_all x2 -> x1, blocking collectives: 26.7 us -> 14.1 us  [swap_groups(): return lax.all_to_all(array, 'group', 0, 0)]
    reduce_scatter x1, waiting for transfers between devices: 3.96 us -> 10.1 us  [shards(): lax.psum_scatter(held, ('batch', 'split'), scatter_dimension=0, tiled=True)]
    ppermute x15 -> x18, waiting for transfers between devices: 11.7 us -> 14.7 us  [ahead(): lax.ppermute(array, axis, [((i + by) % size, i) for i in range(size)])]
    ppermute x15 -> x18, starting transfers between devices: 13.6 us -> 16.5 us  [ahead(): lax.ppermute(array, axis, [((i + by) % size, i) for i in range(size)])]
  transfers between devices with their start and end apart: 31 -> 34, of which waited for: 17 -> 18; matrix products, arithmetic and copies ran while one was open for 4% -> 4% of each run, Pallas kernels for 39% -> 39%
where the time goes in v3:
time: 386 us; the launch traced here: 380 us
  Pallas kernels  176 us (46%)
  waiting for transfers between devices  82.6 us (21%)
  starting transfers between devices  61.6 us (16%)
  between operations  17.6 us (5%)
  other arithmetic  16.3 us (4%)
  blocking collectives  14.1 us (4%)
  local copies, waits for them, and re-layouts  11.7 us (3%)
    pallas_call x3, Pallas kernels, attend_back(): pl.pallas_call(functools.partial(backward_kernel, tokens, groups, splits)...  65.8 us
    ppermute x6, waiting for transfers between devices, line(): return lax.ppermute(array, 'group', pairs)  48.3 us
    pallas_call x3, Pallas kernels, attend(): pl.pallas_call(functools.partial(forward_kernel, tokens, groups, splits),...  48.1 us
    all_to_all x6, starting transfers between devices, swap_groups(): return lax.all_to_all(array, 'group', 0, 0)  26.5 us
    pallas_call x1, Pallas kernels, feed_forward(): pl.pallas_call(functools.partial(block_kernel, dims, len(contexts)), grid...  25.1 us
    ppermute x6, starting transfers between devices, line(): return lax.ppermute(array, 'group', pairs)  18.3 us
    ppermute x18, starting transfers between devices, ahead(): lax.ppermute(array, axis, [((i + by) % size, i) for i in range(size)])  16.5 us
    ppermute x18, waiting for transfers between devices, ahead(): lax.ppermute(array, axis, [((i + by) % size, i) for i in range(size)])  14.7 us
  transfers between devices with their start and end apart: 34, of which 18 were waited for; matrix products, arithmetic and copies ran while one was open for 4% of the time, Pallas kernels for 39%

profile of v3, /device:TPU:0, one launch (start us, length us, event | category | flops | bytes accessed | tf_op | source)
XLA Modules:
  0.0 380.1 jit_solution(14713964038617532297)
XLA Ops:
  7.3 1.2 reshape.117
  9.2 0.7 copy.64
  10.0 5.0 %collective-permute-start = (bf16[512,768]{1,0:T(8,128)(2,1)S(1)}, bf16[512,768]{1,0:T(8,128)(2,1)S(1)}, u32[]{:S(2)}, u32[]{:S(2)}) collective-permute-start(bf16[512,768]{1,0:T(8,128)(2,1)S(1)} %bitcast.91), channel_id=1, source_target_pairs={{0,2},{2,4},{4,6},{1,3},{3,5},{5,7},{8,10},{10,12},{12,14},{9,11},... | collective-permute-start | bytes 2359304 | tf_op jit(solution)/shard_map/ppermute | solution.py:1029
  15.0 1.3 collective-permute-start.1
  16.3 0.7 pad_maximum_fusion
  17.1 17.3 %collective-permute-done.refs_0_ = bf16[512,768]{1,0:T(8,128)(2,1)S(1)} collective-permute-done((bf16[512,768]{1,0:T(8,128)(2,1)S(1)}, bf16[512,768]{1,0:T(8,128)(2,1)S(1)}, u32[]{:S(2)}, u32[]{:S(2)}) %collective-permute-start) | collective-permute-done | bytes 786464 | tf_op jit(solution)/shard_map/ppermute | solution.py:1029
  34.3 4.2 %collective-permute-done.1.refs_2_ = bf16[512,768]{1,0:T(8,128)(2,1)S(1)} collective-permute-done((bf16[512,768]{1,0:T(8,128)(2,1)S(1)}, bf16[512,768]{1,0:T(8,128)(2,1)S(1)}, u32[]{:S(2)}, u32[]{:S(2)}) %collective-permute-start.1) | collective-permute-done | bytes 786464 | tf_op jit(solution)/shard_map/ppermute | solution.py:1029
  38.5 4.4 %collective-permute-start.2 = (bf16[512,768]{1,0:T(8,128)(2,1)S(1)}, bf16[512,768]{1,0:T(8,128)(2,1)}, u32[]{:S(2)}, u32[]{:S(2)}) collective-permute-start(bf16[512,768]{1,0:T(8,128)(2,1)S(1)} %collective-permute-done.refs_0_), channel_id=1, source_target_pairs={{0,2},{2,4},{4,6},{1,3},{3,5},{5,7},{8,10},{10,12},{12,14},{9,11},... | collective-permute-start | bytes 2359304 | tf_op jit(solution)/shard_map/ppermute | solution.py:1029
  42.9 1.3 collective-permute-start.3
  44.2 22.3 %collective-permute-done.2.refs_1_ = bf16[512,768]{1,0:T(8,128)(2,1)} collective-permute-done((bf16[512,768]{1,0:T(8,128)(2,1)S(1)}, bf16[512,768]{1,0:T(8,128)(2,1)}, u32[]{:S(2)}, u32[]{:S(2)}) %collective-permute-start.2) | collective-permute-done | bytes 786464 | tf_op jit(solution)/shard_map/ppermute | solution.py:1029
  66.5 5.1 %collective-permute-start.4 = (bf16[512,768]{1,0:T(8,128)(2,1)}, bf16[512,768]{1,0:T(8,128)(2,1)S(1)}, u32[]{:S(2)}, u32[]{:S(2)}) collective-permute-start(bf16[512,768]{1,0:T(8,128)(2,1)} %collective-permute-done.2.refs_1_), channel_id=1, source_target_pairs={{0,2},{2,4},{4,6},{1,3},{3,5},{5,7},{8,10},{10,12},{12,14},{9,11},... | collective-permute-start | bytes 2359304 | tf_op jit(solution)/shard_map/ppermute | solution.py:1029
  71.6 2.4 collective-permute-done.3.refs_3_
  73.9 1.3 collective-permute-start.5
  76.0 3.1 all-gather.5.cloned.1.call-done.weights
  79.1 12.0 %project.1 = (bf16[768,2048]{1,0:T(8,128)(2,1)}, bf16[2048,384]{1,0:T(8,128)(2,1)}, bf16[2048,384]{1,0:T(8,128)(2,1)}, f32[8,768]{1,0:T(8,128)}, bf16[768,768]{1,0:T(8,128)(2,1)}) custom-call(s32[7]{0:T(128)} %concatenate.27.ints, bf16[768,2560]{1,0:T(8,128)(2,1)} %all-gather.5.cloned.1.call-done.weights, bf16[512,768]{1,0:T(8,128)(2,1)} %bitcast.87, ...), custom_call_target="tpu_custom_call" | custom-call | flops 4831838208 | bytes 12582912 | tf_op jit(solution)/shard_map/project/pallas_call | solution.py:398
  91.2 2.3 collective-permute-done.5.behind
  93.5 0.9 copy-done.10
  94.4 5.9 %project_last.1 = (bf16[768,2048]{1,0:T(8,128)(2,1)}, bf16[2048,384]{1,0:T(8,128)(2,1)}, bf16[2048,384]{1,0:T(8,128)(2,1)}) custom-call(s32[7]{0:T(128)} %concatenate.27.ints, bf16[768,2560]{1,0:T(8,128)(2,1)} %all-gather.5.cloned.1.call-done.weights, bf16[512,768]{1,0:T(8,128)(2,1)} %bitcast.88, ...), custom_call_target="tpu_custom_call", output_to_operand_aliasing={{0}: (7, {}), {1}: (8, {}), {2}: (9, {})} | custom-call | flops 1207959552 | bytes 3145728 | tf_op jit(solution)/shard_map/project_last/pallas_call | solution.py:452
  100.8 3.1 collective-permute-done.6.refs_1_
  103.9 1.1 copy-done.35
  105.0 16.0 %attend.3 = (bf16[16384,512]{1,0:T(8,128)(2,1)}, bf16[4,64,512]{2,1,0:T(8,128)(2,1)}, f32[4,80,512]{2,1,0:T(8,128)}) custom-call(s32[7]{0:T(128)} %concatenate.27.ints, f32[1,32]{1,0:T(1,128)} %get-tuple-element.207.table, bf16[2048,384]{1,0:T(8,128)(2,1)} %get-tuple-element.86.query, bf16[2048,384]{1,0:T(8,128)(2,1)} %get-tuple-element.87.refs_0_, ...), custom_call_target="tpu_custom_call" | custom-call | flops 8589934592 | bytes 16777216 | tf_op jit(solution)/shard_map/attend/pallas_call | solution.py:904
  121.0 3.9 %all-to-all-start = ((bf16[4,64,512]{2,1,0:T(8,128)(2,1)}), bf16[4,64,512]{2,1,0:T(8,128)(2,1)S(1)}, u32[]{:S(2)}, u32[]{:S(2)}) async-start(bf16[4,64,512]{2,1,0:T(8,128)(2,1)} %get-tuple-element.88), calls=%async_computation | async-start | bytes 524288 | tf_op jit(solution)/shard_map/all_to_all | solution.py:1022
  124.8 16.1 %attend.4 = (bf16[16384,512]{1,0:T(8,128)(2,1)}, bf16[4,64,512]{2,1,0:T(8,128)(2,1)}, f32[4,80,512]{2,1,0:T(8,128)}) custom-call(s32[7]{0:T(128)} %concatenate.27.ints, f32[1,32]{1,0:T(1,128)} %get-tuple-element.206.table, bf16[2048,384]{1,0:T(8,128)(2,1)} %get-tuple-element.86.query, bf16[2048,384]{1,0:T(8,128)(2,1)} %get-tuple-element.87.refs_0_, ...), custom_call_target="tpu_custom_call" | custom-call | flops 8589934592 | bytes 16777216 | tf_op jit(solution)/shard_map/attend/pallas_call | solution.py:904
  141.0 5.1 %all-to-all-start.1 = ((bf16[4,64,512]{2,1,0:T(8,128)(2,1)}), bf16[4,64,512]{2,1,0:T(8,128)(2,1)S(1)}, u32[]{:S(2)}, u32[]{:S(2)}) async-start(bf16[4,64,512]{2,1,0:T(8,128)(2,1)} %get-tuple-element.91), calls=%async_computation.1 | async-start | bytes 524288 | tf_op jit(solution)/shard_map/all_to_all | solution.py:1022
  146.1 16.0 %attend.5 = (bf16[16384,512]{1,0:T(8,128)(2,1)}, bf16[4,64,512]{2,1,0:T(8,128)(2,1)}, f32[4,80,512]{2,1,0:T(8,128)}) custom-call(s32[7]{0:T(128)} %concatenate.27.ints, f32[1,32]{1,0:T(1,128)} %get-tuple-element.205.table, bf16[2048,384]{1,0:T(8,128)(2,1)} %get-tuple-element.86.query, bf16[2048,384]{1,0:T(8,128)(2,1)} %get-tuple-element.87.refs_0_, ...), custom_call_target="tpu_custom_call" | custom-call | flops 8589934592 | bytes 16777216 | tf_op jit(solution)/shard_map/attend/pallas_call | solution.py:904
  162.1 1.1 all-to-all-done.1.refs_1_
  163.1 14.1 %all_to_all.35.refs_2_ = bf16[4,64,512]{2,1,0:T(8,128)(2,1)} all-to-all(bf16[4,64,512]{2,1,0:T(8,128)(2,1)} %get-tuple-element.94), channel_id=1, replica_groups=mesh['batch'=4,'group'=4,'split'=2] {'group'}, dimensions={0} | all-to-all | bytes 524288 | tf_op jit(solution)/shard_map/all_to_all | solution.py:1022
  177.9 25.1 %feed_forward.1 = (bf16[512,768]{1,0:T(8,128)(2,1)}, f32[512,768]{1,0:T(8,128)}, bf16[4,64,512]{2,1,0:T(8,128)(2,1)}, bf16[4,128,512]{2,1,0:T(8,128)(2,1)}, bf16[768,7168]{1,0:T(8,128)(2,1)}) custom-call(s32[7]{0:T(128)} %concatenate.27.ints, bf16[512,768]{1,0:T(8,128)(2,1)} %bitcast.89, ...), custom_call_target="tpu_custom_call" | custom-call | flops 16307453952 | bytes 18874368 | tf_op jit(solution)/shard_map/feed_forward/pallas_call | solution.py:657
  203.1 0.9 copy-done.15
  204.0 1.6 collective-permute-start.7
  206.2 4.5 %all-to-all-start.3 = ((bf16[4,128,512]{2,1,0:T(8,128)(2,1)}), bf16[4,128,512]{2,1,0:T(8,128)(2,1)S(1)}, u32[]{:S(2)}, u32[]{:S(2)}) async-start(bf16[4,128,512]{2,1,0:T(8,128)(2,1)} %get-tuple-element.103), calls=%async_computation.3 | async-start | bytes 1048576 | tf_op jit(solution)/shard_map/all_to_all | solution.py:1022
  210.7 2.5 collective-permute-done.8
  213.2 0.7 maximum_bitcast_fusion.d_context
  214.0 22.8 %attend_back.3 = (bf16[4,192,512]{2,1,0:T(8,128)(2,1)}, bf16[4,128,512]{2,1,0:T(8,128)(2,1)}, f32[32,128]{1,0:T(8,128)}) custom-call(s32[7]{0:T(128)} %concatenate.27.ints, bf16[2048,384]{1,0:T(8,128)(2,1)} %get-tuple-element.86.query, bf16[4,1,64,512]{3,2,1,0:T(8,128)(2,1)} %maximum_bitcast_fusion.d_context, f32[4,80,512]{2,1,0:T(8,128)} %get-tuple-element.98.stats, ...), custom_call_target="tpu_custom_call" | custom-call | flops 17179869184 | bytes 16777216 | tf_op jit(solution)/shard_map/attend_back/pallas_call | solution.py:941
  236.9 2.1 collective-permute-done.10
  239.0 2.2 add_convert_fusion.2.refs_0_
  241.2 3.5 all-to-all-start.4
  244.7 21.5 %attend_back.4 = (bf16[4,192,512]{2,1,0:T(8,128)(2,1)}, bf16[4,128,512]{2,1,0:T(8,128)(2,1)}, f32[32,128]{1,0:T(8,128)}) custom-call(s32[7]{0:T(128)} %concatenate.27.ints, bf16[2048,384]{1,0:T(8,128)(2,1)} %get-tuple-element.86.query, bf16[4,2,64,512]{3,2,1,0:T(8,128)(2,1)} %bitcast.96, f32[4,80,512]{2,1,0:T(8,128)} %get-tuple-element.107.stats, ...), custom_call_target="tpu_custom_call" | custom-call | flops 17179869184 | bytes 16777216 | tf_op jit(solution)/shard_map/attend_back/pallas_call | solution.py:941
  266.9 1.7 collective-permute-done.11
  268.6 2.2 add_convert_fusion.1.refs_1_
  270.8 4.9 %all-to-all-start.5 = ((bf16[4,192,512]{2,1,0:T(8,128)(2,1)}), bf16[4,192,512]{2,1,0:T(8,128)(2,1)S(1)}, u32[]{:S(2)}, u32[]{:S(2)}) async-start(bf16[4,192,512]{2,1,0:T(8,128)(2,1)} %add_convert_fusion.1.refs_1_), calls=%async_computation.6 | async-start | bytes 1572864 | tf_op jit(solution)/shard_map/all_to_all | solution.py:1022
  275.9 10.1 %reduce-scatter.3.cloned.1.call-done = bf16[96,7168]{1,0:T(8,128)(2,1)} async-done(((bf16[768,7168]{1,0:T(8,128)(2,1)}), bf16[96,7168]{1,0:T(8,128)(2,1)}) %reduce-scatter.3.cloned.1.call-update) | async-done | bytes 1376272 | tf_op jit(solution)/shard_map/reduce_scatter | solution.py:1111
  286.1 21.5 %attend_back.5 = (bf16[4,192,512]{2,1,0:T(8,128)(2,1)}, bf16[4,128,512]{2,1,0:T(8,128)(2,1)}, f32[32,128]{1,0:T(8,128)}) custom-call(s32[7]{0:T(128)} %concatenate.27.ints, bf16[2048,384]{1,0:T(8,128)(2,1)} %get-tuple-element.86.query, bf16[4,2,64,512]{3,2,1,0:T(8,128)(2,1)} %bitcast.97, f32[4,80,512]{2,1,0:T(8,128)} %get-tuple-element.116.stats, ...), custom_call_target="tpu_custom_call" | custom-call | flops 17179869184 | bytes 16777216 | tf_op jit(solution)/shard_map/attend_back/pallas_call | solution.py:941
  307.6 2.1 collective-permute-done.12
  309.7 2.2 add_convert_fusion.refs_2_
  311.9 4.6 %all-to-all-start.6 = ((bf16[4,192,512]{2,1,0:T(8,128)(2,1)}), bf16[4,192,512]{2,1,0:T(8,128)(2,1)S(1)}, u32[]{:S(2)}, u32[]{:S(2)}) async-start(bf16[4,192,512]{2,1,0:T(8,128)(2,1)} %add_convert_fusion.refs_2_), calls=%async_computation.7 | async-start | bytes 1572864 | tf_op jit(solution)/shard_map/all_to_all | solution.py:1022
  316.5 6.7 %weight_grads.1 = (bf16[384,576]{1,0:T(8,128)(2,1)}, bf16[384,576]{1,0:T(8,128)(2,1)}) custom-call(bf16[768,2048]{1,0:T(8,128)(2,1)} %get-tuple-element.96.normed_t, bf16[4,192,512]{2,1,0:T(8,128)(2,1)} %add_convert_fusion.2.refs_0_, bf16[4,192,512]{2,1,0:T(8,128)(2,1)} %add_convert_fusion.1.refs_1_, bf16[4,192,512]{2,1,0:T(8,128)(2,1)} %add_convert_fusion.refs_2_), custom_call_target="tpu_custom_call" | custom-call | flops 1811939328 | bytes 3145728 | tf_op jit(solution)/shard_map/weight_grads/pallas_call | solution.py:733
  323.2 2.1 collective-permute-done.13.refs_1_
  325.3 0.8 copy-done.13
  326.1 2.0 added.1
  328.1 1.4 collective-permute-start.14
  330.1 2.3 collective-permute-start.16
  332.3 4.5 %all-to-all-done.6.refs_2_ = bf16[4,192,512]{2,1,0:T(8,128)(2,1)S(1)} async-done(((bf16[4,192,512]{2,1,0:T(8,128)(2,1)}), bf16[4,192,512]{2,1,0:T(8,128)(2,1)S(1)}, u32[]{:S(2)}, u32[]{:S(2)}) %all-to-all-start.6) | async-done | bytes 786464 | tf_op jit(solution)/shard_map/all_to_all | solution.py:1022
  337.9 2.2 counted.1
  340.1 1.7 collective-permute-start.17
  341.8 1.3 collective-permute-start.18
  343.2 1.0 slice.255
  346.0 0.7 multiply_reduce_fusion.5
  346.8 0.7 copy.58
  347.5 0.8 collective-permute-done.19
  348.4 2.1 collective-permute-start.20
  350.4 2.3 collective-permute-start.21
  352.8 1.7 collective-permute-start.22
  354.5 8.4 %input_grads.1 = bf16[512,768]{1,0:T(8,128)(2,1)} custom-call(bf16[768,2560]{1,0:T(8,128)(2,1)} %all-gather.5.cloned.1.call-done.weights, bf16[512,768]{1,0:T(8,128)(2,1)} %bitcast.90, f32[8,768]{1,0:T(8,128)} %get-tuple-element.81.gains, f32[512,768]{1,0:T(8,128)} %get-tuple-element.136.d_mixed, bf16[4,192,512]{2,1,0:T(8,128)(2,1)} %copy-done.3, ...), custom_call_target="tpu_custom_call" | custom-call | flops 2013265920 | bytes 6291456 | tf_op jit(solution)/shard_map/input_grads/pallas_call | solution.py:869
  (171 shorter events, 15.6 us)
Async XLA Ops:
  7.2 93.0 %copy-start = (f32[32,12]{0,1:T(8,128)S(1)}, f32[32,12]{0,1:T(8,128)}, u32[]{:S(2)}) copy-start(f32[32,12]{0,1:T(8,128)} %param.22) | copy-start | bytes 4612
  7.2 2.8 copy-start.2
  7.2 9.0 %copy-start.21 = (bf16[64,768]{1,0:T(8,128)(2,1)S(1)}, bf16[64,768]{1,0:T(8,128)(2,1)}, u32[]{:S(2)}) copy-start(bf16[64,768]{1,0:T(8,128)(2,1)} %param.26) | copy-start | bytes 294916
  7.2 9.1 %copy-start.27 = (bf16[24,768]{1,0:T(8,128)(2,1)S(1)}, bf16[24,768]{1,0:T(8,128)(2,1)}, u32[]{:S(2)}) copy-start(bf16[24,768]{1,0:T(8,128)(2,1)} %param.23) | copy-start | bytes 110596
  7.3 9.1 %copy-start.11 = (bf16[24,4096]{1,0:T(8,128)(2,1)S(1)}, bf16[24,4096]{1,0:T(8,128)(2,1)}, u32[]{:S(2)}) copy-start(bf16[24,4096]{1,0:T(8,128)(2,1)} %param.25) | copy-start | bytes 589828
  7.3 71.9 %all-gather.5.cloned.1.call-start = ((), (), s32[]{:S(2)}) async-start(), calls=%async_computation.10 | async-start | bytes 4055040 | tf_op jit(solution)/shard_map/all_gather | solution.py:1047
  8.5 66.7 %copy-start.38 = (s32[1,3]{1,0:T(1,128)S(1)}, s32[1,3]{1,0:T(1,128)}, u32[]{:S(2)}) copy-start(s32[1,3]{1,0:T(1,128)} %param.19) | copy-start | bytes 40
  9.9 168.0 %all-gather.3.cloned.1.call-start = ((), (), s32[]{:S(2)}) async-start(), calls=%async_computation.9 | async-start | bytes 10948608 | tf_op jit(solution)/shard_map/all_gather | solution.py:1051
  10.0 24.4 %collective-permute-start = (bf16[512,768]{1,0:T(8,128)(2,1)S(1)}, bf16[512,768]{1,0:T(8,128)(2,1)S(1)}, u32[]{:S(2)}, u32[]{:S(2)}) collective-permute-start(bf16[512,768]{1,0:T(8,128)(2,1)S(1)} %bitcast.91), channel_id=1, source_target_pairs={{0,2},{2,4},{4,6},{1,3},{3,5},{5,7},{8,10},{10,12},{12,14},{9,11},... | collective-permute-start | bytes 2359304 | tf_op jit(solution)/shard_map/ppermute | solution.py:1029
  15.0 23.5 %collective-permute-start.1 = (bf16[512,768]{1,0:T(8,128)(2,1)S(1)}, bf16[512,768]{1,0:T(8,128)(2,1)S(1)}, u32[]{:S(2)}, u32[]{:S(2)}) collective-permute-start(bf16[512,768]{1,0:T(8,128)(2,1)S(1)} %bitcast.92), channel_id=1, source_target_pairs={{2,0},{4,2},{6,4},{3,1},{5,3},{7,5},{10,8},{12,10},{14,12},{11,9},... | collective-permute-start | bytes 2359304 | tf_op jit(solution)/shard_map/ppermute | solution.py:1029
  34.3 44.8 %copy-start.36 = (bf16[512,768]{1,0:T(8,128)(2,1)}, bf16[512,768]{1,0:T(8,128)(2,1)S(1)}, u32[]{:S(2)}) copy-start(bf16[512,768]{1,0:T(8,128)(2,1)S(1)} %collective-permute-done.refs_0_) | copy-start | bytes 2359300
  38.5 40.6 %copy-start.37 = (bf16[512,768]{1,0:T(8,128)(2,1)}, bf16[512,768]{1,0:T(8,128)(2,1)S(1)}, u32[]{:S(2)}) copy-start(bf16[512,768]{1,0:T(8,128)(2,1)S(1)} %collective-permute-done.1.refs_2_) | copy-start | bytes 2359300
  38.5 27.9 %collective-permute-start.2 = (bf16[512,768]{1,0:T(8,128)(2,1)S(1)}, bf16[512,768]{1,0:T(8,128)(2,1)}, u32[]{:S(2)}, u32[]{:S(2)}) collective-permute-start(bf16[512,768]{1,0:T(8,128)(2,1)S(1)} %collective-permute-done.refs_0_), channel_id=1, source_target_pairs={{0,2},{2,4},{4,6},{1,3},{3,5},{5,7},{8,10},{10,12},{12,14},{9,11},... | collective-permute-start | bytes 2359304 | tf_op jit(solution)/shard_map/ppermute | solution.py:1029
  42.9 31.0 %collective-permute-start.3 = (bf16[512,768]{1,0:T(8,128)(2,1)S(1)}, bf16[512,768]{1,0:T(8,128)(2,1)}, u32[]{:S(2)}, u32[]{:S(2)}) collective-permute-start(bf16[512,768]{1,0:T(8,128)(2,1)S(1)} %collective-permute-done.1.refs_2_), channel_id=1, source_target_pairs={{2,0},{4,2},{6,4},{3,1},{5,3},{7,5},{10,8},{12,10},{14,12},{11,9},... | collective-permute-start | bytes 2359304 | tf_op jit(solution)/shard_map/ppermute | solution.py:1029
  66.5 24.7 %collective-permute-start.4 = (bf16[512,768]{1,0:T(8,128)(2,1)}, bf16[512,768]{1,0:T(8,128)(2,1)S(1)}, u32[]{:S(2)}, u32[]{:S(2)}) collective-permute-start(bf16[512,768]{1,0:T(8,128)(2,1)} %collective-permute-done.2.refs_1_), channel_id=1, source_target_pairs={{0,2},{2,4},{4,6},{1,3},{3,5},{5,7},{8,10},{10,12},{12,14},{9,11},... | collective-permute-start | bytes 2359304 | tf_op jit(solution)/shard_map/ppermute | solution.py:1029
  73.9 19.6 %collective-permute-start.5 = (bf16[512,768]{1,0:T(8,128)(2,1)}, bf16[512,768]{1,0:T(8,128)(2,1)S(1)}, u32[]{:S(2)}, u32[]{:S(2)}) collective-permute-start(bf16[512,768]{1,0:T(8,128)(2,1)} %collective-permute-done.3.refs_3_), channel_id=1, source_target_pairs={{2,0},{4,2},{6,4},{3,1},{5,3},{7,5},{10,8},{12,10},{14,12},{11,9},... | collective-permute-start | bytes 2359304 | tf_op jit(solution)/shard_map/ppermute | solution.py:1029
  100.2 3.6 collective-permute-start.6
  121.0 20.0 %all-to-all-start = ((bf16[4,64,512]{2,1,0:T(8,128)(2,1)}), bf16[4,64,512]{2,1,0:T(8,128)(2,1)S(1)}, u32[]{:S(2)}, u32[]{:S(2)}) async-start(bf16[4,64,512]{2,1,0:T(8,128)(2,1)} %get-tuple-element.88), calls=%async_computation | async-start | bytes 524288 | tf_op jit(solution)/shard_map/all_to_all | solution.py:1022
  141.0 21.1 %copy-start.16 = (bf16[4,64,512]{2,1,0:T(8,128)(2,1)}, bf16[4,64,512]{2,1,0:T(8,128)(2,1)S(1)}, u32[]{:S(2)}) copy-start(bf16[4,64,512]{2,1,0:T(8,128)(2,1)S(1)} %all-to-all-done.refs_0_) | copy-start | bytes 786436
  141.0 22.1 %all-to-all-start.1 = ((bf16[4,64,512]{2,1,0:T(8,128)(2,1)}), bf16[4,64,512]{2,1,0:T(8,128)(2,1)S(1)}, u32[]{:S(2)}, u32[]{:S(2)}) async-start(bf16[4,64,512]{2,1,0:T(8,128)(2,1)} %get-tuple-element.91), calls=%async_computation.1 | async-start | bytes 524288 | tf_op jit(solution)/shard_map/all_to_all | solution.py:1022
  146.1 140.0 %reduce-scatter.3.cloned.1.call-start = ((), (), s32[]{:S(2)}) async-start(), calls=%async_computation.11 | async-start | bytes 12386304 | tf_op jit(solution)/shard_map/reduce_scatter | solution.py:1111
  163.1 14.8 %copy-start.17 = (bf16[4,64,512]{2,1,0:T(8,128)(2,1)}, bf16[4,64,512]{2,1,0:T(8,128)(2,1)S(1)}, u32[]{:S(2)}) copy-start(bf16[4,64,512]{2,1,0:T(8,128)(2,1)S(1)} %all-to-all-done.1.refs_1_) | copy-start | bytes 786436
  204.0 6.7 %collective-permute-start.7 = (bf16[64,512]{1,0:T(8,128)(2,1)S(1)}, bf16[64,512]{1,0:T(8,128)(2,1)S(1)}, u32[]{:S(2)}, u32[]{:S(2)}) collective-permute-start(bf16[64,512]{1,0:T(8,128)(2,1)S(1)} %get-tuple-element.162), channel_id=1, source_target_pairs={{2,0},{4,2},{6,4},{0,6},{3,1},{5,3},{7,5},{1,7},{10,8},{12,10},{14... | collective-permute-start | bytes 196616 | tf_op jit(solution)/shard_map/ppermute | solution.py:1019
  205.6 7.6 %collective-permute-start.8 = (bf16[64,512]{1,0:T(8,128)(2,1)S(1)}, bf16[64,512]{1,0:T(8,128)(2,1)S(1)}, u32[]{:S(2)}, u32[]{:S(2)}) collective-permute-start(bf16[64,512]{1,0:T(8,128)(2,1)S(1)} %get-tuple-element.161), channel_id=1, source_target_pairs={{4,0},{6,2},{0,4},{2,6},{5,1},{7,3},{1,5},{3,7},{12,8},{14,10},{8,... | collective-permute-start | bytes 196616 | tf_op jit(solution)/shard_map/ppermute | solution.py:1019
  205.6 7.6 %collective-permute-start.9 = (bf16[64,512]{1,0:T(8,128)(2,1)S(1)}, bf16[64,512]{1,0:T(8,128)(2,1)S(1)}, u32[]{:S(2)}, u32[]{:S(2)}) collective-permute-start(bf16[64,512]{1,0:T(8,128)(2,1)S(1)} %get-tuple-element.160), channel_id=1, source_target_pairs={{6,0},{0,2},{2,4},{4,6},{7,1},{1,3},{3,5},{5,7},{14,8},{8,10},{10,... | collective-permute-start | bytes 196616 | tf_op jit(solution)/shard_map/ppermute | solution.py:1019
  206.2 30.6 %all-to-all-start.3 = ((bf16[4,128,512]{2,1,0:T(8,128)(2,1)}), bf16[4,128,512]{2,1,0:T(8,128)(2,1)S(1)}, u32[]{:S(2)}, u32[]{:S(2)}) async-start(bf16[4,128,512]{2,1,0:T(8,128)(2,1)} %get-tuple-element.103), calls=%async_computation.3 | async-start | bytes 1048576 | tf_op jit(solution)/shard_map/all_to_all | solution.py:1022
  236.8 4.4 %copy-start.12 = (bf16[4,128,512]{2,1,0:T(8,128)(2,1)}, bf16[4,128,512]{2,1,0:T(8,128)(2,1)S(1)}, u32[]{:S(2)}) copy-start(bf16[4,128,512]{2,1,0:T(8,128)(2,1)S(1)} %all-to-all-done.3) | copy-start | bytes 1572868
  236.8 2.2 collective-permute-start.10
  241.2 25.0 %all-to-all-start.4 = ((bf16[4,192,512]{2,1,0:T(8,128)(2,1)}), bf16[4,192,512]{2,1,0:T(8,128)(2,1)S(1)}, u32[]{:S(2)}, u32[]{:S(2)}) async-start(bf16[4,192,512]{2,1,0:T(8,128)(2,1)} %add_convert_fusion.2.refs_0_), calls=%async_computation.4 | async-start | bytes 1572864 | tf_op jit(solution)/shard_map/all_to_all | solution.py:1022
  266.2 4.6 %copy-start.3 = (bf16[4,192,512]{2,1,0:T(8,128)(2,1)}, bf16[4,192,512]{2,1,0:T(8,128)(2,1)S(1)}, u32[]{:S(2)}) copy-start(bf16[4,192,512]{2,1,0:T(8,128)(2,1)S(1)} %all-to-all-done.4.refs_0_) | copy-start | bytes 2359300
  266.2 2.4 collective-permute-start.11
  270.8 41.1 %all-to-all-start.5 = ((bf16[4,192,512]{2,1,0:T(8,128)(2,1)}), bf16[4,192,512]{2,1,0:T(8,128)(2,1)S(1)}, u32[]{:S(2)}, u32[]{:S(2)}) async-start(bf16[4,192,512]{2,1,0:T(8,128)(2,1)} %add_convert_fusion.1.refs_1_), calls=%async_computation.6 | async-start | bytes 1572864 | tf_op jit(solution)/shard_map/all_to_all | solution.py:1022
  275.7 61.5 %reduce-scatter.5.cloned.1.call-start = ((), (), s32[]{:S(2)}) async-start(), calls=%async_computation.12 | async-start | bytes 1720320 | tf_op jit(solution)/shard_map/reduce_scatter | solution.py:1113
  307.6 2.1 collective-permute-start.12
  311.9 11.4 %copy-start.4 = (bf16[4,192,512]{2,1,0:T(8,128)(2,1)}, bf16[4,192,512]{2,1,0:T(8,128)(2,1)S(1)}, u32[]{:S(2)}) copy-start(bf16[4,192,512]{2,1,0:T(8,128)(2,1)S(1)} %all-to-all-done.5.refs_1_) | copy-start | bytes 2359300
  311.9 25.0 %all-to-all-start.6 = ((bf16[4,192,512]{2,1,0:T(8,128)(2,1)}), bf16[4,192,512]{2,1,0:T(8,128)(2,1)S(1)}, u32[]{:S(2)}, u32[]{:S(2)}) async-start(bf16[4,192,512]{2,1,0:T(8,128)(2,1)} %add_convert_fusion.refs_2_), calls=%async_computation.7 | async-start | bytes 1572864 | tf_op jit(solution)/shard_map/all_to_all | solution.py:1022
  323.2 2.1 collective-permute-start.13
  328.1 8.8 %collective-permute-start.14 = (bf16[96,576]{1,0:T(8,128)(2,1)}, bf16[96,576]{1,0:T(8,128)(2,1)S(1)}, u32[]{:S(2)}, u32[]{:S(2)}) collective-permute-start(bf16[96,576]{1,0:T(8,128)(2,1)} %get-tuple-element.125), channel_id=1, source_target_pairs={{24,0},{0,8},{8,16},{16,24},{25,1},{1,9},{9,17},{17,25},{26,2},{2,... | collective-permute-start | bytes 331784 | tf_op jit(solution)/shard_map/ppermute | solution.py:1019
  329.4 7.7 %collective-permute-start.15 = (bf16[96,576]{1,0:T(8,128)(2,1)}, bf16[96,576]{1,0:T(8,128)(2,1)S(1)}, u32[]{:S(2)}, u32[]{:S(2)}) collective-permute-start(bf16[96,576]{1,0:T(8,128)(2,1)} %get-tuple-element.126), channel_id=1, source_target_pairs={{16,0},{24,8},{0,16},{8,24},{17,1},{25,9},{1,17},{9,25},{18,2},{26... | collective-permute-start | bytes 331784 | tf_op jit(solution)/shard_map/ppermute | solution.py:1019
  330.1 7.1 %collective-permute-start.16 = (bf16[96,576]{1,0:T(8,128)(2,1)}, bf16[96,576]{1,0:T(8,128)(2,1)S(1)}, u32[]{:S(2)}, u32[]{:S(2)}) collective-permute-start(bf16[96,576]{1,0:T(8,128)(2,1)} %get-tuple-element.127), channel_id=1, source_target_pairs={{8,0},{16,8},{24,16},{0,24},{9,1},{17,9},{25,17},{1,25},{10,2},{18... | collective-permute-start | bytes 331784 | tf_op jit(solution)/shard_map/ppermute | solution.py:1019
  336.9 8.1 %copy-start.5 = (bf16[4,192,512]{2,1,0:T(8,128)(2,1)}, bf16[4,192,512]{2,1,0:T(8,128)(2,1)S(1)}, u32[]{:S(2)}) copy-start(bf16[4,192,512]{2,1,0:T(8,128)(2,1)S(1)} %all-to-all-done.6.refs_2_) | copy-start | bytes 2359300
  340.1 7.4 %collective-permute-start.17 = (f32[16,640]{1,0:T(8,128)}, f32[16,640]{1,0:T(8,128)S(1)}, u32[]{:S(2)}, u32[]{:S(2)}) collective-permute-start(f32[16,640]{1,0:T(8,128)} %get-tuple-element.131), channel_id=1, source_target_pairs={{8,0},{16,8},{24,16},{0,24},{9,1},{17,9},{25,17},{1,25},{10,2},{18... | collective-permute-start | bytes 122888 | tf_op jit(solution)/shard_map/ppermute | solution.py:1019
  341.8 5.7 %collective-permute-start.18 = (f32[16,640]{1,0:T(8,128)}, f32[16,640]{1,0:T(8,128)S(1)}, u32[]{:S(2)}, u32[]{:S(2)}) collective-permute-start(f32[16,640]{1,0:T(8,128)} %get-tuple-element.131), channel_id=1, source_target_pairs={{16,0},{24,8},{0,16},{8,24},{17,1},{25,9},{1,17},{9,25},{18,2},{26... | collective-permute-start | bytes 122888 | tf_op jit(solution)/shard_map/ppermute | solution.py:1019
  343.2 5.1 %collective-permute-start.19 = (f32[16,640]{1,0:T(8,128)}, f32[16,640]{1,0:T(8,128)S(1)}, u32[]{:S(2)}, u32[]{:S(2)}) collective-permute-start(f32[16,640]{1,0:T(8,128)} %get-tuple-element.131), channel_id=1, source_target_pairs={{24,0},{0,8},{8,16},{16,24},{25,1},{1,9},{9,17},{17,25},{26,2},{2,... | collective-permute-start | bytes 122888 | tf_op jit(solution)/shard_map/ppermute | solution.py:1019
  344.8 3.5 copy-start.26
  344.8 3.5 copy-start.22
  344.8 3.5 copy-start.23
  344.8 3.5 copy-start.24
  344.8 3.5 copy-start.25
  345.2 17.6 %copy-start.7 = (f32[24,4096]{1,0:T(8,128)}, f32[24,4096]{1,0:T(8,128)S(1)}, u32[]{:S(2)}) copy-start(f32[24,4096]{1,0:T(8,128)S(1)} %reshape.122) | copy-start | bytes 1179652
  348.4 14.5 %collective-permute-start.20 = (f32[40,640]{1,0:T(8,128)S(1)}, f32[40,640]{1,0:T(8,128)S(1)}, u32[]{:S(2)}, u32[]{:S(2)}) collective-permute-start(f32[40,640]{1,0:T(8,128)S(1)} %get-tuple-element.202), channel_id=1, source_target_pairs={{6,0},{0,2},{2,4},{4,6},{7,1},{1,3},{3,5},{5,7},{14,8},{8,10},{10,... | collective-permute-start | bytes 307208 | tf_op jit(solution)/shard_map/ppermute | solution.py:1019
  350.4 12.5 %collective-permute-start.21 = (f32[40,640]{1,0:T(8,128)S(1)}, f32[40,640]{1,0:T(8,128)S(1)}, u32[]{:S(2)}, u32[]{:S(2)}) collective-permute-start(f32[40,640]{1,0:T(8,128)S(1)} %get-tuple-element.203), channel_id=1, source_target_pairs={{4,0},{6,2},{0,4},{2,6},{5,1},{7,3},{1,5},{3,7},{12,8},{14,10},{8,... | collective-permute-start | bytes 307208 | tf_op jit(solution)/shard_map/ppermute | solution.py:1019
  352.8 10.1 %collective-permute-start.22 = (f32[40,640]{1,0:T(8,128)S(1)}, f32[40,640]{1,0:T(8,128)S(1)}, u32[]{:S(2)}, u32[]{:S(2)}) collective-permute-start(f32[40,640]{1,0:T(8,128)S(1)} %get-tuple-element.201), channel_id=1, source_target_pairs={{2,0},{4,2},{6,4},{0,6},{3,1},{5,3},{7,5},{1,7},{10,8},{12,10},{14... | collective-permute-start | bytes 307208 | tf_op jit(solution)/shard_map/ppermute | solution.py:1019
  362.9 10.2 %copy-start.1 = (f32[32,12]{0,1:T(8,128)S(1)}, f32[32,12]{0,1:T(8,128)}, u32[]{:S(2)}) copy-start(f32[32,12]{0,1:T(8,128)} %param.22) | copy-start | bytes 4612
  363.0 6.8 %copy-start.41 = (f32[64]{0:T(128)S(1)}, f32[64]{0:T(128)}, u32[]{:S(2)}) copy-start(f32[64]{0:T(128)} %param.34) | copy-start | bytes 772
  363.0 7.3 %copy-start.28 = (f32[4096]{0:T(1024)S(1)}, f32[4096]{0:T(1024)}, u32[]{:S(2)}) copy-start(f32[4096]{0:T(1024)} %param.33) | copy-start | bytes 49156
  363.0 7.9 %copy-start.29 = (f32[2304]{0:T(1024)S(1)}, f32[2304]{0:T(1024)}, u32[]{:S(2)}) copy-start(f32[2304]{0:T(1024)} %param.29) | copy-start | bytes 27652
  363.0 8.5 %copy-start.32 = (f32[24]{0:T(128)S(1)}, f32[24]{0:T(128)}, u32[]{:S(2)}) copy-start(f32[24]{0:T(128)} %param.28) | copy-start | bytes 292
  363.0 9.0 %copy-start.30 = (f32[768]{0:T(1024)S(1)}, f32[768]{0:T(1024)}, u32[]{:S(2)}) copy-start(f32[768]{0:T(1024)} %param.35) | copy-start | bytes 9220
  363.0 9.0 %copy-start.31 = (f32[768]{0:T(1024)S(1)}, f32[768]{0:T(1024)}, u32[]{:S(2)}) copy-start(f32[768]{0:T(1024)} %param.31) | copy-start | bytes 9220
  363.0 9.6 %copy-start.33 = (f32[24]{0:T(128)S(1)}, f32[24]{0:T(128)}, u32[]{:S(2)}) copy-start(f32[24]{0:T(128)} %param.32) | copy-start | bytes 292
  363.0 9.6 %copy-start.34 = (f32[24]{0:T(128)S(1)}, f32[24]{0:T(128)}, u32[]{:S(2)}) copy-start(f32[24]{0:T(128)} %param.30) | copy-start | bytes 292
  363.1 1.4 collective-permute-start.23
  363.8 9.4 %copy-start.8 = (f32[24,2304]{1,0:T(8,128)}, f32[24,2304]{1,0:T(8,128)S(1)}, u32[]{:S(2)}) copy-start(f32[24,2304]{1,0:T(8,128)S(1)} %concatenate.35) | copy-start | bytes 663556
  (12 other events, 14.4 us)
Sparse Core Ops, SparseCore 0:
  11.7 67.3 all-gather.4
  82.7 95.1 all-gather.2
  203.2 82.7 reduce-scatter.2
  288.2 32.2 reduce-scatter.4
